TPU v7x, 1024 devices: a whole 4x4x32 slice. The times are simulated.
1024 devices in a mesh: blk: 64 (over y_lo, z), depth: 16 (over x, y_hi, core).
Axes of the slice: x: 4, y: 4 (y_hi: 2, y_lo: 2; y = y_hi * 2 + y_lo), z: 32, core: 2. Of those that a mesh axis runs over, the one named last changes fastest.
Arguments:
- video: bfloat16 [32768, 1152], P('blk'), may hold values from -0.1875 to 0.1875
- text: bfloat16 [32768, 1152], P(('blk', 'depth')), may hold values from -0.1875 to 0.1875
- video_ids: int32 [32768], P('blk'), may hold values from 0 to 511
- text_ids: int32 [32768], P(('blk', 'depth')), may hold values from 0 to 511
- log_scale: float32 [1], replicated, may hold values from 1.5 to 2.5
- bias: float32 [1], replicated, may hold values from -8 to -4
Outputs:
- loss: float32 [], replicated
- grad_video: float32 [32768, 1152], P(('blk', 'depth'))
- grad_text: float32 [32768, 1152], P(('blk', 'depth'))
All inputs are finite; a program needn't handle non-finite values.
Results may differ from a plain program's by a relative error of at most 0.00095.
The roundings to bfloat16 on the way count: a program that leaves them out, or rounds other values in their place, can miss the bound.
Values may be sent and summed in bfloat16 or wider, within the bound.
No kernel may reach another device: no remote copies, remote signals or barrier semaphores. Data moves between devices by JAX's collectives and lax.ppermute only.
A program may use at most 32 MiB of HBM per device.

v0:
```python
import jax
import jax.numpy as jnp
from jax import lax
from jax.sharding import PartitionSpec as P

EPS = 1e-06


def passed_along(value, axis, steps):
    count = lax.axis_size(axis)
    pairs = [(source, (source + steps) % count) for source in range(count)]
    return lax.ppermute(value, axis, pairs)


def unit_rows(x):
    x32 = x.astype(jnp.float32)
    norms = jnp.sqrt(jnp.sum(x32 * x32, axis=-1, keepdims=True) + EPS)
    return (x32 / norms, norms)


def shards(video, text, video_ids, text_ids, log_scale, bias):
    rows = video.shape[0]
    width = video.shape[1]
    slice_rows = text.shape[0]
    nblk = lax.axis_size("blk")
    half = nblk // 8
    scale = jnp.exp(log_scale[0])
    vunit, vnorm = unit_rows(video)
    tunit, tnorm = unit_rows(text)
    vhat = vunit.astype(jnp.bfloat16)
    that = tunit.astype(jnp.bfloat16)

    def pair_terms(tblock, tids):
        dots = jnp.einsum("rd,cd->rc", vhat, tblock, preferred_element_type=jnp.float32)
        logits = scale * dots + bias[0]
        sign = jnp.where(video_ids[:, None] == tids[None, :], 1.0, -1.0).astype(jnp.float32)
        part_loss = jnp.sum(jax.nn.softplus(-sign * logits))
        coef = (-sign * jax.nn.sigmoid(-sign * logits) * scale).astype(jnp.bfloat16)
        tgrad = jnp.einsum("rc,rd->cd", coef, vhat, preferred_element_type=jnp.float32)
        return (part_loss, coef, tgrad)

    coefs = jnp.zeros((2 * half, rows, slice_rows), jnp.bfloat16)
    blocks = jnp.zeros((2 * half, slice_rows, width), jnp.bfloat16)

    def store(coefs, blocks, coef, tblock, slot):
        coefs = lax.dynamic_update_index_in_dim(coefs, coef, slot, 0)
        blocks = lax.dynamic_update_index_in_dim(blocks, tblock, slot, 0)
        return (coefs, blocks)

    first_text, first_ids = passed_along((that, text_ids), "blk", -half)
    total, coef, accum = pair_terms(first_text, first_ids)
    coefs, blocks = store(coefs, blocks, coef, first_text, 0)

    def step_one(slot, carry):
        tblock, tids, accum, total, coefs, blocks = carry
        tblock, tids = passed_along((tblock, tids), "blk", 1)
        accum = passed_along(accum, "blk", 1)
        part_loss, coef, tgrad = pair_terms(tblock, tids)
        coefs, blocks = store(coefs, blocks, coef, tblock, slot)
        return (tblock, tids, accum + tgrad, total + part_loss, coefs, blocks)

    carry = (first_text, first_ids, accum, total, coefs, blocks)
    carry = lax.fori_loop(1, 2 * half, step_one, carry)
    accum, total, coefs, blocks = (carry[2], carry[3], carry[4], carry[5])
    accum = passed_along(accum, "blk", 1 - half)
    terms = jnp.einsum("krc,kcd->rd", coefs, blocks, preferred_element_type=jnp.float32)
    grad_vhat = lax.psum_scatter(terms, "depth", scatter_dimension=0, tiled=True)
    loss = lax.psum(total, ("blk", "depth")) / (rows * nblk * 2 * half)
    offset = lax.axis_index("depth") * slice_rows
    own_unit = lax.dynamic_slice_in_dim(vunit, offset, slice_rows, 0)
    own_norm = lax.dynamic_slice_in_dim(vnorm, offset, slice_rows, 0)
    grad_video = (
        grad_vhat - own_unit * jnp.sum(own_unit * grad_vhat, axis=-1, keepdims=True)
    ) / own_norm
    grad_text = (accum - tunit * jnp.sum(tunit * accum, axis=-1, keepdims=True)) / tnorm
    return (loss, grad_video, grad_text)


def solution(mesh):
    placed = (P("blk", None), P(("blk", "depth"), None), P("blk"), P(("blk", "depth")), P(), P())
    return jax.shard_map(
        shards,
        mesh=mesh,
        in_specs=placed,
        out_specs=(P(), P(("blk", "depth"), None), P(("blk", "depth"), None)),
        check_vma=False,
    )
```

profile of v0, /device:TPU:1, one launch (start us, length us, event | category | flops | bytes accessed | tf_op | source)
XLA Modules:
  0.0 461.0 jit_solution(373949002642764592)
XLA Ops:
  7.2 24.7 %collective-permute-start.4 = (s32[32]{0:T(128)}, s32[32]{0:T(128)S(1)}, u32[]{:S(2)}, u32[]{:S(2)}) collective-permute-start(s32[32]{0:T(128)} %param.11), channel_id=1, source_target_pairs={{0,896},{16,912},{32,928},{48,944},{64,960},{80,976},{96,992},{112... | collective-permute-start | bytes 392 | tf_op jit(solution)/shard_map/ppermute | solution.py:12
  33.9 8.2 %collective-permute-start.3 = (bf16[32,1152]{1,0:T(8,128)(2,1)S(1)}, bf16[32,1152]{1,0:T(8,128)(2,1)S(1)}, u32[]{:S(2)}, u32[]{:S(2)}) collective-permute-start(bf16[32,1152]{1,0:T(8,128)(2,1)S(1)} %fusion.8), channel_id=1, source_target_pairs={{0,896},{16,912},{32,928},{48,944},{64,960},{80,976},{96,992},{112... | collective-permute-start | bytes 221192 | tf_op jit(solution)/shard_map/ppermute | solution.py:12
  46.8 7.5 %collective-permute-done.3 = bf16[32,1152]{1,0:T(8,128)(2,1)S(1)} collective-permute-done((bf16[32,1152]{1,0:T(8,128)(2,1)S(1)}, bf16[32,1152]{1,0:T(8,128)(2,1)S(1)}, u32[]{:S(2)}, u32[]{:S(2)}) %collective-permute-start.3) | collective-permute-done | bytes 73760 | tf_op jit(solution)/shard_map/ppermute | solution.py:12
  56.0 202.4 %while.25 = (s32[]{:T(128)}, bf16[32,1152]{1,0:T(8,128)(2,1)S(1)}, s32[32]{0:T(128)S(1)}, f32[32,1152]{1,0:T(8,128)S(1)}, f32[]{:T(128)}, /*index=5*/bf16[16,512...) while((s32[]{:T(128)}, bf16[32,1152]{1,0:T(8,128)(2,1)S(1)}, ...), condition=%wide.region_5.6_spmd, body=%wide.region_3.5_spmd.sunk | while | flops 76042240 | bytes 4144967 | solution.py:63
  60.1 6.6 %collective-permute-start.2 = (f32[32,1152]{1,0:T(8,128)S(1)}, f32[32,1152]{1,0:T(8,128)S(1)}, u32[]{:S(2)}, u32[]{:S(2)}) collective-permute-start(f32[32,1152]{1,0:T(8,128)S(1)} %get-tuple-element.390), channel_id=1, source_target_pairs={{0,16},{16,32},{32,48},{48,64},{64,80},{80,96},{96,112},{112,128},... | collective-permute-start | bytes 442376 | tf_op jit(solution)/shard_map/while/body/eval_jaxpr/ppermute | solution.py:12
  71.0 2.6 collective-permute-start
  90.3 2.5 collective-permute-done.1
  103.1 2.5 collective-permute-done.1
  115.9 2.5 collective-permute-done.1
  128.7 2.9 collective-permute-done.1
  139.6 3.2 collective-permute-start.2
  148.6 2.3 collective-permute-start
  150.9 2.6 collective-permute-start.1
  164.3 2.8 collective-permute-start.1
  181.9 2.5 collective-permute-done.1
  194.9 2.5 collective-permute-done.1
  208.8 2.5 collective-permute-done.1
  218.4 2.6 collective-permute-start.1
  221.0 3.6 collective-permute-start.2
  229.9 2.4 collective-permute-start
  232.3 2.6 collective-permute-start.1
  247.7 3.3 collective-permute-start.2
  260.7 5.2 %collective-permute-start.5 = (f32[32,1152]{1,0:T(8,128)S(1)}, f32[32,1152]{1,0:T(8,128)S(1)}, u32[]{:S(2)}, u32[]{:S(2)}) collective-permute-start(f32[32,1152]{1,0:T(8,128)S(1)} %get-tuple-element.273), channel_id=1, source_target_pairs={{0,912},{16,928},{32,944},{48,960},{64,976},{80,992},{96,1008},{11... | collective-permute-start | bytes 442376 | tf_op jit(solution)/shard_map/ppermute | solution.py:12
  265.9 182.6 %psum.7 = f32[]{:T(128)} all-reduce(f32[]{:T(128)} %get-tuple-element.270), channel_id=1, replica_groups=mesh['blk'=64,'depth'=16] {'blk','depth'}, use_global_device_ids=true, to_apply=%region_6.7 | all-reduce | flops 1 | bytes 8 | tf_op jit(solution)/shard_map/psum | solution.py:68
  (189 shorter events, 133.0 us)
Async XLA Ops:
  7.2 443.0 %reduce-scatter.2.cloned.1.call-start = ((), (), s32[]{:S(2)}) async-start(), calls=%async_computation.1 | async-start | bytes 2506752 | tf_op jit(solution)/shard_map/reduce_scatter | solution.py:67
  7.2 39.6 %collective-permute-start.4 = (s32[32]{0:T(128)}, s32[32]{0:T(128)S(1)}, u32[]{:S(2)}, u32[]{:S(2)}) collective-permute-start(s32[32]{0:T(128)} %param.11), channel_id=1, source_target_pairs={{0,896},{16,912},{32,928},{48,944},{64,960},{80,976},{96,992},{112... | collective-permute-start | bytes 392 | tf_op jit(solution)/shard_map/ppermute | solution.py:12
  33.9 20.4 %collective-permute-start.3 = (bf16[32,1152]{1,0:T(8,128)(2,1)S(1)}, bf16[32,1152]{1,0:T(8,128)(2,1)S(1)}, u32[]{:S(2)}, u32[]{:S(2)}) collective-permute-start(bf16[32,1152]{1,0:T(8,128)(2,1)S(1)} %fusion.8), channel_id=1, source_target_pairs={{0,896},{16,912},{32,928},{48,944},{64,960},{80,976},{96,992},{112... | collective-permute-start | bytes 221192 | tf_op jit(solution)/shard_map/ppermute | solution.py:12
  56.0 10.8 %collective-permute-start = (bf16[32,1152]{1,0:T(8,128)(2,1)S(1)}, bf16[32,1152]{1,0:T(8,128)(2,1)S(1)}, u32[]{:S(2)}, u32[]{:S(2)}) collective-permute-start(bf16[32,1152]{1,0:T(8,128)(2,1)S(1)} %get-tuple-element.388), channel_id=1, source_target_pairs={{0,16},{16,32},{32,48},{48,64},{64,80},{80,96},{96,112},{112,128},... | collective-permute-start | bytes 221192 | tf_op jit(solution)/shard_map/while/body/eval_jaxpr/ppermute | solution.py:12
  58.0 8.8 %collective-permute-start.1 = (s32[32]{0:T(128)S(1)}, s32[32]{0:T(128)S(1)}, u32[]{:S(2)}, u32[]{:S(2)}) collective-permute-start(s32[32]{0:T(128)S(1)} %get-tuple-element.389), channel_id=1, source_target_pairs={{0,16},{16,32},{32,48},{48,64},{64,80},{80,96},{96,112},{112,128},... | collective-permute-start | bytes 392 | tf_op jit(solution)/shard_map/while/body/eval_jaxpr/ppermute | solution.py:12
  60.1 9.9 %collective-permute-start.2 = (f32[32,1152]{1,0:T(8,128)S(1)}, f32[32,1152]{1,0:T(8,128)S(1)}, u32[]{:S(2)}, u32[]{:S(2)}) collective-permute-start(f32[32,1152]{1,0:T(8,128)S(1)} %get-tuple-element.390), channel_id=1, source_target_pairs={{0,16},{16,32},{32,48},{48,64},{64,80},{80,96},{96,112},{112,128},... | collective-permute-start | bytes 442376 | tf_op jit(solution)/shard_map/while/body/eval_jaxpr/ppermute | solution.py:12
  71.0 9.0 %collective-permute-start = (bf16[32,1152]{1,0:T(8,128)(2,1)S(1)}, bf16[32,1152]{1,0:T(8,128)(2,1)S(1)}, u32[]{:S(2)}, u32[]{:S(2)}) collective-permute-start(bf16[32,1152]{1,0:T(8,128)(2,1)S(1)} %get-tuple-element.388), channel_id=1, source_target_pairs={{0,16},{16,32},{32,48},{48,64},{64,80},{80,96},{96,112},{112,128},... | collective-permute-start | bytes 221192 | tf_op jit(solution)/shard_map/while/body/eval_jaxpr/ppermute | solution.py:12
  84.5 8.3 %collective-permute-start = (bf16[32,1152]{1,0:T(8,128)(2,1)S(1)}, bf16[32,1152]{1,0:T(8,128)(2,1)S(1)}, u32[]{:S(2)}, u32[]{:S(2)}) collective-permute-start(bf16[32,1152]{1,0:T(8,128)(2,1)S(1)} %get-tuple-element.388), channel_id=1, source_target_pairs={{0,16},{16,32},{32,48},{48,64},{64,80},{80,96},{96,112},{112,128},... | collective-permute-start | bytes 221192 | tf_op jit(solution)/shard_map/while/body/eval_jaxpr/ppermute | solution.py:12
  97.3 8.3 %collective-permute-start = (bf16[32,1152]{1,0:T(8,128)(2,1)S(1)}, bf16[32,1152]{1,0:T(8,128)(2,1)S(1)}, u32[]{:S(2)}, u32[]{:S(2)}) collective-permute-start(bf16[32,1152]{1,0:T(8,128)(2,1)S(1)} %get-tuple-element.388), channel_id=1, source_target_pairs={{0,16},{16,32},{32,48},{48,64},{64,80},{80,96},{96,112},{112,128},... | collective-permute-start | bytes 221192 | tf_op jit(solution)/shard_map/while/body/eval_jaxpr/ppermute | solution.py:12
  110.1 8.3 %collective-permute-start = (bf16[32,1152]{1,0:T(8,128)(2,1)S(1)}, bf16[32,1152]{1,0:T(8,128)(2,1)S(1)}, u32[]{:S(2)}, u32[]{:S(2)}) collective-permute-start(bf16[32,1152]{1,0:T(8,128)(2,1)S(1)} %get-tuple-element.388), channel_id=1, source_target_pairs={{0,16},{16,32},{32,48},{48,64},{64,80},{80,96},{96,112},{112,128},... | collective-permute-start | bytes 221192 | tf_op jit(solution)/shard_map/while/body/eval_jaxpr/ppermute | solution.py:12
  122.9 8.7 %collective-permute-start = (bf16[32,1152]{1,0:T(8,128)(2,1)S(1)}, bf16[32,1152]{1,0:T(8,128)(2,1)S(1)}, u32[]{:S(2)}, u32[]{:S(2)}) collective-permute-start(bf16[32,1152]{1,0:T(8,128)(2,1)S(1)} %get-tuple-element.388), channel_id=1, source_target_pairs={{0,16},{16,32},{32,48},{48,64},{64,80},{80,96},{96,112},{112,128},... | collective-permute-start | bytes 221192 | tf_op jit(solution)/shard_map/while/body/eval_jaxpr/ppermute | solution.py:12
  135.8 8.6 %collective-permute-start = (bf16[32,1152]{1,0:T(8,128)(2,1)S(1)}, bf16[32,1152]{1,0:T(8,128)(2,1)S(1)}, u32[]{:S(2)}, u32[]{:S(2)}) collective-permute-start(bf16[32,1152]{1,0:T(8,128)(2,1)S(1)} %get-tuple-element.388), channel_id=1, source_target_pairs={{0,16},{16,32},{32,48},{48,64},{64,80},{80,96},{96,112},{112,128},... | collective-permute-start | bytes 221192 | tf_op jit(solution)/shard_map/while/body/eval_jaxpr/ppermute | solution.py:12
  148.6 8.7 %collective-permute-start = (bf16[32,1152]{1,0:T(8,128)(2,1)S(1)}, bf16[32,1152]{1,0:T(8,128)(2,1)S(1)}, u32[]{:S(2)}, u32[]{:S(2)}) collective-permute-start(bf16[32,1152]{1,0:T(8,128)(2,1)S(1)} %get-tuple-element.388), channel_id=1, source_target_pairs={{0,16},{16,32},{32,48},{48,64},{64,80},{80,96},{96,112},{112,128},... | collective-permute-start | bytes 221192 | tf_op jit(solution)/shard_map/while/body/eval_jaxpr/ppermute | solution.py:12
  162.4 8.3 %collective-permute-start = (bf16[32,1152]{1,0:T(8,128)(2,1)S(1)}, bf16[32,1152]{1,0:T(8,128)(2,1)S(1)}, u32[]{:S(2)}, u32[]{:S(2)}) collective-permute-start(bf16[32,1152]{1,0:T(8,128)(2,1)S(1)} %get-tuple-element.388), channel_id=1, source_target_pairs={{0,16},{16,32},{32,48},{48,64},{64,80},{80,96},{96,112},{112,128},... | collective-permute-start | bytes 221192 | tf_op jit(solution)/shard_map/while/body/eval_jaxpr/ppermute | solution.py:12
  176.1 8.3 %collective-permute-start = (bf16[32,1152]{1,0:T(8,128)(2,1)S(1)}, bf16[32,1152]{1,0:T(8,128)(2,1)S(1)}, u32[]{:S(2)}, u32[]{:S(2)}) collective-permute-start(bf16[32,1152]{1,0:T(8,128)(2,1)S(1)} %get-tuple-element.388), channel_id=1, source_target_pairs={{0,16},{16,32},{32,48},{48,64},{64,80},{80,96},{96,112},{112,128},... | collective-permute-start | bytes 221192 | tf_op jit(solution)/shard_map/while/body/eval_jaxpr/ppermute | solution.py:12
  189.1 8.3 %collective-permute-start = (bf16[32,1152]{1,0:T(8,128)(2,1)S(1)}, bf16[32,1152]{1,0:T(8,128)(2,1)S(1)}, u32[]{:S(2)}, u32[]{:S(2)}) collective-permute-start(bf16[32,1152]{1,0:T(8,128)(2,1)S(1)} %get-tuple-element.388), channel_id=1, source_target_pairs={{0,16},{16,32},{32,48},{48,64},{64,80},{80,96},{96,112},{112,128},... | collective-permute-start | bytes 221192 | tf_op jit(solution)/shard_map/while/body/eval_jaxpr/ppermute | solution.py:12
  193.0 9.0 %collective-permute-start.2 = (f32[32,1152]{1,0:T(8,128)S(1)}, f32[32,1152]{1,0:T(8,128)S(1)}, u32[]{:S(2)}, u32[]{:S(2)}) collective-permute-start(f32[32,1152]{1,0:T(8,128)S(1)} %get-tuple-element.390), channel_id=1, source_target_pairs={{0,16},{16,32},{32,48},{48,64},{64,80},{80,96},{96,112},{112,128},... | collective-permute-start | bytes 442376 | tf_op jit(solution)/shard_map/while/body/eval_jaxpr/ppermute | solution.py:12
  203.0 8.3 %collective-permute-start = (bf16[32,1152]{1,0:T(8,128)(2,1)S(1)}, bf16[32,1152]{1,0:T(8,128)(2,1)S(1)}, u32[]{:S(2)}, u32[]{:S(2)}) collective-permute-start(bf16[32,1152]{1,0:T(8,128)(2,1)S(1)} %get-tuple-element.388), channel_id=1, source_target_pairs={{0,16},{16,32},{32,48},{48,64},{64,80},{80,96},{96,112},{112,128},... | collective-permute-start | bytes 221192 | tf_op jit(solution)/shard_map/while/body/eval_jaxpr/ppermute | solution.py:12
  206.8 8.7 %collective-permute-start.2 = (f32[32,1152]{1,0:T(8,128)S(1)}, f32[32,1152]{1,0:T(8,128)S(1)}, u32[]{:S(2)}, u32[]{:S(2)}) collective-permute-start(f32[32,1152]{1,0:T(8,128)S(1)} %get-tuple-element.390), channel_id=1, source_target_pairs={{0,16},{16,32},{32,48},{48,64},{64,80},{80,96},{96,112},{112,128},... | collective-permute-start | bytes 442376 | tf_op jit(solution)/shard_map/while/body/eval_jaxpr/ppermute | solution.py:12
  216.5 8.3 %collective-permute-start = (bf16[32,1152]{1,0:T(8,128)(2,1)S(1)}, bf16[32,1152]{1,0:T(8,128)(2,1)S(1)}, u32[]{:S(2)}, u32[]{:S(2)}) collective-permute-start(bf16[32,1152]{1,0:T(8,128)(2,1)S(1)} %get-tuple-element.388), channel_id=1, source_target_pairs={{0,16},{16,32},{32,48},{48,64},{64,80},{80,96},{96,112},{112,128},... | collective-permute-start | bytes 221192 | tf_op jit(solution)/shard_map/while/body/eval_jaxpr/ppermute | solution.py:12
  229.9 9.1 %collective-permute-start = (bf16[32,1152]{1,0:T(8,128)(2,1)S(1)}, bf16[32,1152]{1,0:T(8,128)(2,1)S(1)}, u32[]{:S(2)}, u32[]{:S(2)}) collective-permute-start(bf16[32,1152]{1,0:T(8,128)(2,1)S(1)} %get-tuple-element.388), channel_id=1, source_target_pairs={{0,16},{16,32},{32,48},{48,64},{64,80},{80,96},{96,112},{112,128},... | collective-permute-start | bytes 221192 | tf_op jit(solution)/shard_map/while/body/eval_jaxpr/ppermute | solution.py:12
  243.9 8.3 %collective-permute-start = (bf16[32,1152]{1,0:T(8,128)(2,1)S(1)}, bf16[32,1152]{1,0:T(8,128)(2,1)S(1)}, u32[]{:S(2)}, u32[]{:S(2)}) collective-permute-start(bf16[32,1152]{1,0:T(8,128)(2,1)S(1)} %get-tuple-element.388), channel_id=1, source_target_pairs={{0,16},{16,32},{32,48},{48,64},{64,80},{80,96},{96,112},{112,128},... | collective-permute-start | bytes 221192 | tf_op jit(solution)/shard_map/while/body/eval_jaxpr/ppermute | solution.py:12
  247.7 9.7 %collective-permute-start.2 = (f32[32,1152]{1,0:T(8,128)S(1)}, f32[32,1152]{1,0:T(8,128)S(1)}, u32[]{:S(2)}, u32[]{:S(2)}) collective-permute-start(f32[32,1152]{1,0:T(8,128)S(1)} %get-tuple-element.390), channel_id=1, source_target_pairs={{0,16},{16,32},{32,48},{48,64},{64,80},{80,96},{96,112},{112,128},... | collective-permute-start | bytes 442376 | tf_op jit(solution)/shard_map/while/body/eval_jaxpr/ppermute | solution.py:12
  260.7 188.5 %collective-permute-start.5 = (f32[32,1152]{1,0:T(8,128)S(1)}, f32[32,1152]{1,0:T(8,128)S(1)}, u32[]{:S(2)}, u32[]{:S(2)}) collective-permute-start(f32[32,1152]{1,0:T(8,128)S(1)} %get-tuple-element.273), channel_id=1, source_target_pairs={{0,912},{16,928},{32,944},{48,960},{64,976},{80,992},{96,1008},{11... | collective-permute-start | bytes 442376 | tf_op jit(solution)/shard_map/ppermute | solution.py:12
  (28 other events, 414.5 us)
Sparse Core Ops, SparseCore 0:
  260.8 138.2 reduce-scatter.1
where the time goes:
time: 463 us; the launch traced here: 461 us
  blocking collectives  183 us (40%)
  starting transfers between devices  139 us (30%)
  waiting for transfers between devices  45.8 us (10%)
  matrix products  35.4 us (8%)
  loops' own time  29.9 us (6%)
  between operations  17.3 us (4%)
  other arithmetic  10.5 us (2%)
    psum x1, blocking collectives, shards(): loss = lax.psum(total, ('blk', 'depth')) / (rows * nblk * 2 * half)  183 us
    ppermute x48, starting transfers between devices, passed_along(): return lax.ppermute(value, axis, pairs)  139 us
    ppermute x48, waiting for transfers between devices, passed_along(): return lax.ppermute(value, axis, pairs)  45.7 us
    another operation x1, loops' own time, shards(): carry = lax.fori_loop(1, 2 * half, step_one, carry)  29.9 us
    dot_general x16, matrix products, pair_terms(): jnp.einsum('rd,cd->rc', vhat, tblock, preferred_element_type=jnp.float32)  27.5 us
  transfers between devices with their start and end apart: 49, of which 27 were waited for; matrix products, arithmetic and copies ran while one was open for 7% of the time, Pallas kernels for 0%

commit v1 on v0

v1 whole, which is shorter than its diff:
```python
import jax
import jax.numpy as jnp
from jax import lax
from jax.experimental import pallas as pl
from jax.experimental.pallas import tpu as pltpu
from jax.sharding import PartitionSpec as P

EPS = 1e-06
LANES = 128
ID_BASE = 32
BF16 = jnp.bfloat16
F16 = jnp.float16
F32 = jnp.float32
CENTERS = (0, 3, -3, 6, -6)


def passed_along(value, steps):
    count = lax.axis_size("blk")
    pairs = [(source, (source + steps) % count) for source in range(count)]
    return lax.ppermute(value, "blk", pairs)


def unit_rows(x):
    x32 = x.astype(F32)
    norms = jnp.sqrt(jnp.sum(x32 * x32, axis=-1, keepdims=True) + EPS)
    return (x32 / norms, norms)


def coef_kernel(width, params, text_ref, vhat_ref, vids_ref, coef_ref, loss_ref):
    scale, bias = (params[0], params[1])
    marks = text_ref[:, width : width + LANES].astype(F32)
    tids = marks[:, 0:1] * ID_BASE + marks[:, 1:2]
    dots = lax.dot_general(
        text_ref[:, :width],
        vhat_ref[...],
        (((1,), (1,)), ((), ())),
        preferred_element_type=F32,
    )
    logits = scale * dots + bias
    flip = jnp.where(tids == vids_ref[...], -1.0, 1.0)
    z = flip * logits
    e = jnp.exp(-jnp.abs(z))
    losses = jnp.maximum(z, 0.0) + jnp.log1p(e)
    sig = jnp.where(z >= 0, 1.0, e) / (1.0 + e)
    coef_ref[...] = (flip * sig * scale).astype(BF16)
    loss_ref[...] = jnp.sum(losses, axis=0, keepdims=True)


def pair_coefs(params, text, vhat, vids):
    rows, width = vhat.shape
    vmem = pl.BlockSpec(memory_space=pltpu.VMEM)
    return pl.pallas_call(
        lambda *refs: coef_kernel(width, *refs),
        out_shape=(
            jax.ShapeDtypeStruct((text.shape[0], rows), BF16),
            jax.ShapeDtypeStruct((1, rows), F32),
        ),
        in_specs=[pl.BlockSpec(memory_space=pltpu.SMEM), vmem, vmem, vmem],
        out_specs=(vmem, vmem),
        compiler_params=pltpu.CompilerParams(vmem_limit_bytes=24 * 1024 * 1024),
        cost_estimate=pl.CostEstimate(
            flops=2 * text.shape[0] * rows * width,
            bytes_accessed=2 * width * (text.shape[0] + rows),
            transcendentals=3 * text.shape[0] * rows,
        ),
    )(params, text, vhat, vids)


def shards(video, text, video_ids, text_ids, log_scale, bias):
    rows, width = video.shape
    slice_rows = text.shape[0]
    nblk = lax.axis_size("blk")
    ndepth = lax.axis_size("depth")
    half = nblk // 8

    tunit, tnorm = unit_rows(text)
    digits = jnp.stack([text_ids // ID_BASE, text_ids % ID_BASE], axis=1).astype(BF16)
    digits = jnp.pad(digits, ((0, 0), (0, LANES - 2)))
    own = jnp.concatenate([tunit.astype(BF16), digits], axis=1)

    far_up = passed_along(own, -6)
    far_down = passed_along(own, 6)
    up = passed_along(own, -3)
    down = passed_along(own, 3)

    vunit, vnorm = unit_rows(video)
    vhat = vunit.astype(BF16)
    vids = video_ids.astype(F32)[None, :]
    params = jnp.stack([jnp.exp(log_scale[0]), bias[0]])

    bundle = jnp.concatenate([own, up, down, far_up, far_down], axis=0)
    above = passed_along(bundle, -1)
    below = passed_along(bundle, 1)
    last = passed_along(far_up, -2)

    def text_grad(coef):
        return jnp.einsum("cr,rd->cd", coef, vhat, preferred_element_type=F32)

    coef0, loss0 = pair_coefs(params, bundle, vhat, vids)
    grad0 = text_grad(coef0)
    arrived = jnp.concatenate([above, below, last], axis=0)
    coef1, loss1 = pair_coefs(params, arrived, vhat, vids)
    n = bundle.shape[0]
    back_up = passed_along(text_grad(coef1[:n]).astype(F16), 1)
    back_down = passed_along(text_grad(coef1[n : 2 * n]).astype(F16), -1)
    back_last = passed_along(text_grad(coef1[2 * n :]).astype(F16), 2)

    total = jnp.sum(loss0 + loss1)
    total = jnp.full((ndepth, LANES), total)
    total = jnp.sum(lax.all_to_all(total, "depth", 0, 0, tiled=True)[:, 0])
    total = jnp.full((nblk, LANES), total)
    total = jnp.sum(lax.all_to_all(total, "blk", 0, 0, tiled=True)[:, 0])
    loss = total / (rows * nblk * 2 * half)

    coefs = jnp.concatenate([coef0, coef1], axis=0)
    texts = jnp.concatenate([bundle, arrived], axis=0)[:, :width]
    share = jnp.einsum("cr,cd->rd", coefs, texts, preferred_element_type=F32)
    shares = lax.all_to_all(share.astype(F16), "depth", 0, 0, tiled=True)
    grad_vhat = jnp.sum(shares.reshape(ndepth, slice_rows, width).astype(F32), axis=0)

    held = grad0 + back_up.astype(F32) + back_down.astype(F32)
    held = held.reshape(len(CENTERS), slice_rows, width)
    held6 = held[3] + back_last.astype(F32)
    home = [passed_along(held6.astype(F16), 6), passed_along(held[4].astype(F16), -6)]
    home += [passed_along(held[1].astype(F16), 3), passed_along(held[2].astype(F16), -3)]
    grad_that = held[0] + sum(part.astype(F32) for part in home)

    offset = lax.axis_index("depth") * slice_rows
    own_unit, own_norm = unit_rows(lax.dynamic_slice_in_dim(video, offset, slice_rows, 0))
    grad_video = (
        grad_vhat - own_unit * jnp.sum(own_unit * grad_vhat, axis=-1, keepdims=True)
    ) / own_norm
    grad_text = (
        grad_that - tunit * jnp.sum(tunit * grad_that, axis=-1, keepdims=True)
    ) / tnorm
    return (loss, grad_video, grad_text)


def solution(mesh):
    placed = (P("blk", None), P(("blk", "depth"), None), P("blk"), P(("blk", "depth")), P(), P())
    return jax.shard_map(
        shards,
        mesh=mesh,
        in_specs=placed,
        out_specs=(P(), P(("blk", "depth"), None), P(("blk", "depth"), None)),
        check_vma=False,
    )
```

time: 463 us -> 180 us (0.39)
  blocking collectives: 183 us -> 0 us
  starting transfers between devices: 139 us -> 107 us
  loops' own time: 29.9 us -> 0 us
  matrix products: 35.4 us -> 8.04 us
  between operations: 17.3 us -> 3.99 us
  waiting for transfers between devices: 45.8 us -> 33.2 us
  local copies, waits for them, and re-layouts: 0.66 us -> 9.33 us
    psum x1 -> x0, blocking collectives: 183 us -> none  [shards(): loss = lax.psum(total, ('blk', 'depth')) / (rows * nblk * 2 * half)]
    ppermute x48 -> x14, starting transfers between devices: 139 us -> 72.9 us  [passed_along(): return lax.ppermute(value, 'blk', pairs)]
    all_to_all x0 -> x3, starting transfers between devices: none -> 34 us  [the longest x1 13.5 us: shards(): total = jnp.sum(lax.all_to_all(total, 'blk', 0, 0, tiled=True)[:, 0])]
    another operation x1 -> x0, loops' own time: 29.9 us -> none  [shards(): carry = lax.fori_loop(1, 2 * half, step_one, carry)]
    dot_general x33 -> x5, matrix products: 35.4 us -> 8.04 us  [the longest x4 4.87 us: text_grad(): return jnp.einsum('cr,rd->cd', coef, vhat, preferred_element_type=F32)]
    ppermute x48 -> x14, waiting for transfers between devices: 45.7 us -> 23.8 us  [passed_along(): return lax.ppermute(value, 'blk', pairs)]
    all_to_all x0 -> x3, waiting for transfers between devices: none -> 9.47 us  [the longest x1 9.46 us: shards(): total = jnp.sum(lax.all_to_all(total, 'blk', 0, 0, tiled=True)[:, 0])]
    unnamed x6 -> x16, local copies, waits for them, and re-layouts: 0.02 us -> 6.02 us
  transfers between devices with their start and end apart: 49 -> 17, of which waited for: 27 -> 5; matrix products, arithmetic and copies ran while one was open for 7% -> 11% of each run, Pallas kernels for 0% -> 1%
where the time goes in v1:
time: 180 us; the launch traced here: 178 us
  starting transfers between devices  107 us (59%)
  waiting for transfers between devices  33.2 us (18%)
  other arithmetic  13.3 us (7%)
  local copies, waits for them, and re-layouts  9.33 us (5%)
  matrix products  8.04 us (4%)
  between operations  3.99 us (2%)
  Pallas kernels  3.12 us (2%)
    ppermute x14, starting transfers between devices, passed_along(): return lax.ppermute(value, 'blk', pairs)  72.9 us
    ppermute x14, waiting for transfers between devices, passed_along(): return lax.ppermute(value, 'blk', pairs)  23.8 us
    all_to_all x1, starting transfers between devices, shards(): total = jnp.sum(lax.all_to_all(total, 'blk', 0, 0, tiled=True)[:, 0])  13.5 us
    all_to_all x1, starting transfers between devices, shards(): total = jnp.sum(lax.all_to_all(total, 'depth', 0, 0, tiled=True)[:, 0])  11 us
    all_to_all x1, starting transfers between devices, shards(): shares = lax.all_to_all(share.astype(F16), 'depth', 0, 0, tiled=True)  9.48 us
    all_to_all x1, waiting for transfers between devices, shards(): total = jnp.sum(lax.all_to_all(total, 'blk', 0, 0, tiled=True)[:, 0])  9.46 us
    unnamed x16, local copies, waits for them, and re-layouts  6.02 us
    dot_general x4, matrix products, text_grad(): return jnp.einsum('cr,rd->cd', coef, vhat, preferred_element_type=F32)  4.87 us
  transfers between devices with their start and end apart: 17, of which 5 were waited for; matrix products, arithmetic and copies ran while one was open for 11% of the time, Pallas kernels for 1%

profile of v1, /device:TPU:1, one launch (start us, length us, event | category | flops | bytes accessed | tf_op | source)
XLA Modules:
  0.0 177.9 jit_solution(14074815075591354356)
XLA Ops:
  4.2 23.7 %collective-permute-start.2 = (bf16[32,1280]{1,0:T(8,128)(2,1)S(1)}, bf16[32,1280]{1,0:T(8,128)(2,1)S(1)}, u32[]{:S(2)}, u32[]{:S(2)}) collective-permute-start(bf16[32,1280]{1,0:T(8,128)(2,1)S(1)} %get-tuple-element.24), channel_id=1, source_target_pairs={{0,928},{16,944},{32,960},{48,976},{64,992},{80,1008},{96,0},{112,... | collective-permute-start | bytes 245768 | tf_op jit(solution)/shard_map/ppermute | solution.py:20
  27.8 2.3 %collective-permute-start.1 = (bf16[32,1280]{1,0:T(8,128)(2,1)S(1)}, bf16[32,1280]{1,0:T(8,128)(2,1)S(1)}, u32[]{:S(2)}, u32[]{:S(2)}) collective-permute-start(bf16[32,1280]{1,0:T(8,128)(2,1)S(1)} %get-tuple-element.24), channel_id=1, source_target_pairs={{0,48},{16,64},{32,80},{48,96},{64,112},{80,128},{96,144},{112,160... | collective-permute-start | bytes 245768 | tf_op jit(solution)/shard_map/ppermute | solution.py:20
  30.2 6.8 %collective-permute-start = (bf16[32,1280]{1,0:T(8,128)(2,1)S(1)}, bf16[32,1280]{1,0:T(8,128)(2,1)S(1)}, u32[]{:S(2)}, u32[]{:S(2)}) collective-permute-start(bf16[32,1280]{1,0:T(8,128)(2,1)S(1)} %get-tuple-element.24), channel_id=1, source_target_pairs={{0,976},{16,992},{32,1008},{48,0},{64,16},{80,32},{96,48},{112,64}... | collective-permute-start | bytes 245768 | tf_op jit(solution)/shard_map/ppermute | solution.py:20
  37.0 1.9 %collective-permute-start.3 = (bf16[32,1280]{1,0:T(8,128)(2,1)S(1)}, bf16[32,1280]{1,0:T(8,128)(2,1)S(1)}, u32[]{:S(2)}, u32[]{:S(2)}) collective-permute-start(bf16[32,1280]{1,0:T(8,128)(2,1)S(1)} %get-tuple-element.24), channel_id=1, source_target_pairs={{0,96},{16,112},{32,128},{48,144},{64,160},{80,176},{96,192},{112,... | collective-permute-start | bytes 245768 | tf_op jit(solution)/shard_map/ppermute | solution.py:20
  42.5 10.3 %collective-permute-done.3 = bf16[32,1280]{1,0:T(8,128)(2,1)S(1)} collective-permute-done((bf16[32,1280]{1,0:T(8,128)(2,1)S(1)}, bf16[32,1280]{1,0:T(8,128)(2,1)S(1)}, u32[]{:S(2)}, u32[]{:S(2)}) %collective-permute-start.3) | collective-permute-done | bytes 81952 | tf_op jit(solution)/shard_map/ppermute | solution.py:20
  53.5 4.4 %collective-permute-start.5 = (bf16[160,1280]{1,0:T(8,128)(2,1)S(1)}, bf16[160,1280]{1,0:T(8,128)(2,1)S(1)}, u32[]{:S(2)}, u32[]{:S(2)}) collective-permute-start(bf16[160,1280]{1,0:T(8,128)(2,1)S(1)} %get-tuple-element.15.refs_1_), channel_id=1, source_target_pairs={{0,16},{16,32},{32,48},{48,64},{64,80},{80,96},{96,112},{112,128},... | collective-permute-start | bytes 1228808 | tf_op jit(solution)/shard_map/ppermute | solution.py:20
  57.9 3.0 %collective-permute-start.4 = (bf16[160,1280]{1,0:T(8,128)(2,1)S(1)}, bf16[160,1280]{1,0:T(8,128)(2,1)}, u32[]{:S(2)}, u32[]{:S(2)}) collective-permute-start(bf16[160,1280]{1,0:T(8,128)(2,1)S(1)} %get-tuple-element.15.refs_1_), channel_id=1, source_target_pairs={{0,1008},{16,0},{32,16},{48,32},{64,48},{80,64},{96,80},{112,96},{... | collective-permute-start | bytes 1228808 | tf_op jit(solution)/shard_map/ppermute | solution.py:20
  62.8 1.9 %collective-permute-start.6 = (bf16[32,1280]{1,0:T(8,128)(2,1)S(1)}, bf16[32,1280]{1,0:T(8,128)(2,1)S(1)}, u32[]{:S(2)}, u32[]{:S(2)}) collective-permute-start(bf16[32,1280]{1,0:T(8,128)(2,1)S(1)} %collective-permute-done.2), channel_id=1, source_target_pairs={{0,992},{16,1008},{32,0},{48,16},{64,32},{80,48},{96,64},{112,80},... | collective-permute-start | bytes 245768 | tf_op jit(solution)/shard_map/ppermute | solution.py:20
  66.1 4.6 %collective-permute-done.6 = bf16[32,1280]{1,0:T(8,128)(2,1)S(1)} collective-permute-done((bf16[32,1280]{1,0:T(8,128)(2,1)S(1)}, bf16[32,1280]{1,0:T(8,128)(2,1)S(1)}, u32[]{:S(2)}, u32[]{:S(2)}) %collective-permute-start.6) | collective-permute-done | bytes 81952 | tf_op jit(solution)/shard_map/ppermute | solution.py:20
  71.7 1.8 %shard_map.86 = (bf16[352,512]{1,0:T(8,128)(2,1)S(1)}, f32[1,512]{1,0:T(1,128)S(1)}) custom-call(f32[2]{0:T(128)S(1)} %pad_maximum_fusion.1.refs_0_, bf16[352,1280]{1,0:T(8,128)(2,1)S(1)} %pad_maximum_fusion.refs_1_, bf16[512,1152]{1,0:T(8,128)(2,1)S(1)} %fusion.2.refs_2_, f32[1,512]{1,0:T(1,128)S(1)} %bitcast.14), custom_call_target="tpu_custom_call" | custom-call | flops 415236096 | bytes 1990656 | tf_op jit(solution)/shard_map/pallas_call | solution.py:52
  78.0 11.0 %all-to-all-start = ((f32[16,1,128]{2,1,0:T(1,128)}), f32[16,1,128]{2,1,0:T(1,128)S(1)}, u32[]{:S(2)}, u32[]{:S(2)}) async-start(f32[16,1,128]{2,1,0:T(1,128)} %broadcast_in_dim.7), calls=%async_computation | async-start | bytes 16384 | tf_op jit(solution)/shard_map/all_to_all | solution.py:110
  89.0 3.8 %collective-permute-start.9 = (f16[32,1152]{1,0:T(8,128)(2,1)S(1)}, f16[32,1152]{1,0:T(8,128)(2,1)}, u32[]{:S(2)}, u32[]{:S(2)}) collective-permute-start(f16[32,1152]{1,0:T(8,128)(2,1)S(1)} %convolution_convert_fusion.3), channel_id=1, source_target_pairs={{0,32},{16,48},{32,64},{48,80},{64,96},{80,112},{96,128},{112,144}... | collective-permute-start | bytes 221192 | tf_op jit(solution)/shard_map/ppermute | solution.py:20
  92.8 1.9 %collective-permute-start.7 = (f16[160,1152]{1,0:T(8,128)(2,1)}, f16[160,1152]{1,0:T(8,128)(2,1)}, u32[]{:S(2)}, u32[]{:S(2)}) collective-permute-start(f16[160,1152]{1,0:T(8,128)(2,1)} %convolution_convert_fusion.2), channel_id=1, source_target_pairs={{0,16},{16,32},{32,48},{48,64},{64,80},{80,96},{96,112},{112,128},... | collective-permute-start | bytes 1105928 | tf_op jit(solution)/shard_map/ppermute | solution.py:20
  94.8 5.5 %collective-permute-start.8 = (f16[160,1152]{1,0:T(8,128)(2,1)}, f16[160,1152]{1,0:T(8,128)(2,1)}, u32[]{:S(2)}, u32[]{:S(2)}) collective-permute-start(f16[160,1152]{1,0:T(8,128)(2,1)} %convolution_convert_fusion.1), channel_id=1, source_target_pairs={{0,1008},{16,0},{32,16},{48,32},{64,48},{80,64},{96,80},{112,96},{... | collective-permute-start | bytes 1105928 | tf_op jit(solution)/shard_map/ppermute | solution.py:20
  103.5 3.2 %convolution_convert_fusion = f16[512,1152]{1,0:T(8,128)(2,1)} fusion(bf16[512,1280]{1,0:T(8,128)(2,1)} %constant_dynamic-update-slice_fusion.5, bf16[352,512]{1,0:T(8,128)(2,1)S(1)} %get-tuple-element.10, bf16[160,512]{1,0:T(8,128)(2,1)S(1)} %get-tuple-element.9), kind=kOutput, calls=%fused_computation | convolution fusion | flops 605618176 | bytes 2883584 | tf_op jit(solution)/shard_map/cr,cd->rd/dot_general | solution.py:117
  108.5 13.5 %all-to-all-start.1 = ((f32[64,1,128]{2,1,0:T(1,128)}), f32[64,1,128]{2,1,0:T(1,128)S(1)}, u32[]{:S(2)}, u32[]{:S(2)}) async-start(f32[64,1,128]{2,1,0:T(1,128)} %broadcast_in_dim.16), calls=%async_computation.1 | async-start | bytes 65536 | tf_op jit(solution)/shard_map/all_to_all | solution.py:112
  122.0 2.3 %fusion.20 = (f16[160,1152]{1,0:T(8,128)(2,1)}, f32[160,1152]{1,0:T(8,128)S(1)}) fusion(f16[160,1152]{1,0:T(8,128)(2,1)} %collective-permute-done.8, f16[160,1152]{1,0:T(8,128)(2,1)} %collective-permute-done.7, bf16[160,512]{1,0:T(8,128)(2,1)S(1)} %get-tuple-element.9, bf16[512,1152]{1,0:T(8,128)(2,1)S(1)} %fusion.2.refs_2_), kind=kOutput, calls=%fused_computation.67 | convolution fusion | flops 189665280 | bytes 3186688 | tf_op jit(solution)/shard_map/cr,rd->cd/dot_general | solution.py:97
  126.1 8.6 %collective-permute-start.10 = (f16[32,1152]{1,0:T(8,128)(2,1)S(1)}, f16[32,1152]{1,0:T(8,128)(2,1)S(1)}, u32[]{:S(2)}, u32[]{:S(2)}) collective-permute-start(f16[32,1152]{1,0:T(8,128)(2,1)S(1)} %fusion.12), channel_id=1, source_target_pairs={{0,96},{16,112},{32,128},{48,144},{64,160},{80,176},{96,192},{112,... | collective-permute-start | bytes 221192 | tf_op jit(solution)/shard_map/ppermute | solution.py:20
  134.7 9.5 %all-to-all-done.1 = f32[64,1,128]{2,1,0:T(1,128)S(1)} async-done(((f32[64,1,128]{2,1,0:T(1,128)}), f32[64,1,128]{2,1,0:T(1,128)S(1)}, u32[]{:S(2)}, u32[]{:S(2)}) %all-to-all-start.1) | async-done | bytes 32800 | tf_op jit(solution)/shard_map/all_to_all | solution.py:112
  144.2 9.5 %all-to-all-start.2 = ((f16[16,32,1152]{2,1,0:T(8,128)(2,1)}), f16[16,32,1152]{2,1,0:T(8,128)(2,1)S(1)}, u32[]{:S(2)}, u32[]{:S(2)}) async-start(f16[16,32,1152]{2,1,0:T(8,128)(2,1)} %bitcast.15), calls=%async_computation.2 | async-start | bytes 2359296 | tf_op jit(solution)/shard_map/all_to_all | solution.py:118
  153.7 1.9 %collective-permute-start.11 = (f16[32,1152]{1,0:T(8,128)(2,1)S(1)}, f16[32,1152]{1,0:T(8,128)(2,1)S(1)}, u32[]{:S(2)}, u32[]{:S(2)}) collective-permute-start(f16[32,1152]{1,0:T(8,128)(2,1)S(1)} %get-tuple-element.11), channel_id=1, source_target_pairs={{0,928},{16,944},{32,960},{48,976},{64,992},{80,1008},{96,0},{112,... | collective-permute-start | bytes 221192 | tf_op jit(solution)/shard_map/ppermute | solution.py:20
  155.7 2.1 %collective-permute-start.13 = (f16[32,1152]{1,0:T(8,128)(2,1)S(1)}, f16[32,1152]{1,0:T(8,128)(2,1)S(1)}, u32[]{:S(2)}, u32[]{:S(2)}) collective-permute-start(f16[32,1152]{1,0:T(8,128)(2,1)S(1)} %get-tuple-element.12), channel_id=1, source_target_pairs={{0,976},{16,992},{32,1008},{48,0},{64,16},{80,32},{96,48},{112,64}... | collective-permute-start | bytes 221192 | tf_op jit(solution)/shard_map/ppermute | solution.py:20
  157.8 5.0 %collective-permute-start.12 = (f16[32,1152]{1,0:T(8,128)(2,1)S(1)}, f16[32,1152]{1,0:T(8,128)(2,1)S(1)}, u32[]{:S(2)}, u32[]{:S(2)}) collective-permute-start(f16[32,1152]{1,0:T(8,128)(2,1)S(1)} %get-tuple-element.13), channel_id=1, source_target_pairs={{0,48},{16,64},{32,80},{48,96},{64,112},{80,128},{96,144},{112,160... | collective-permute-start | bytes 221192 | tf_op jit(solution)/shard_map/ppermute | solution.py:20
  164.0 8.4 %collective-permute-done.11 = f16[32,1152]{1,0:T(8,128)(2,1)S(1)} collective-permute-done((f16[32,1152]{1,0:T(8,128)(2,1)S(1)}, f16[32,1152]{1,0:T(8,128)(2,1)S(1)}, u32[]{:S(2)}, u32[]{:S(2)}) %collective-permute-start.11) | collective-permute-done | bytes 73760 | tf_op jit(solution)/shard_map/ppermute | solution.py:20
  (61 shorter events, 27.1 us)
Async XLA Ops:
  2.4 58.4 %copy-start = (bf16[512,1152]{1,0:T(8,128)(2,1)S(1)}, bf16[512,1152]{1,0:T(8,128)(2,1)}, u32[]{:S(2)}) copy-start(bf16[512,1152]{1,0:T(8,128)(2,1)} %param.6) | copy-start | bytes 3538948
  4.2 37.7 %collective-permute-start.2 = (bf16[32,1280]{1,0:T(8,128)(2,1)S(1)}, bf16[32,1280]{1,0:T(8,128)(2,1)S(1)}, u32[]{:S(2)}, u32[]{:S(2)}) collective-permute-start(bf16[32,1280]{1,0:T(8,128)(2,1)S(1)} %get-tuple-element.24), channel_id=1, source_target_pairs={{0,928},{16,944},{32,960},{48,976},{64,992},{80,1008},{96,0},{112,... | collective-permute-start | bytes 245768 | tf_op jit(solution)/shard_map/ppermute | solution.py:20
  27.8 13.4 %collective-permute-start.1 = (bf16[32,1280]{1,0:T(8,128)(2,1)S(1)}, bf16[32,1280]{1,0:T(8,128)(2,1)S(1)}, u32[]{:S(2)}, u32[]{:S(2)}) collective-permute-start(bf16[32,1280]{1,0:T(8,128)(2,1)S(1)} %get-tuple-element.24), channel_id=1, source_target_pairs={{0,48},{16,64},{32,80},{48,96},{64,112},{80,128},{96,144},{112,160... | collective-permute-start | bytes 245768 | tf_op jit(solution)/shard_map/ppermute | solution.py:20
  30.2 10.4 %collective-permute-start = (bf16[32,1280]{1,0:T(8,128)(2,1)S(1)}, bf16[32,1280]{1,0:T(8,128)(2,1)S(1)}, u32[]{:S(2)}, u32[]{:S(2)}) collective-permute-start(bf16[32,1280]{1,0:T(8,128)(2,1)S(1)} %get-tuple-element.24), channel_id=1, source_target_pairs={{0,976},{16,992},{32,1008},{48,0},{64,16},{80,32},{96,48},{112,64}... | collective-permute-start | bytes 245768 | tf_op jit(solution)/shard_map/ppermute | solution.py:20
  37.0 15.8 %collective-permute-start.3 = (bf16[32,1280]{1,0:T(8,128)(2,1)S(1)}, bf16[32,1280]{1,0:T(8,128)(2,1)S(1)}, u32[]{:S(2)}, u32[]{:S(2)}) collective-permute-start(bf16[32,1280]{1,0:T(8,128)(2,1)S(1)} %get-tuple-element.24), channel_id=1, source_target_pairs={{0,96},{16,112},{32,128},{48,144},{64,160},{80,176},{96,192},{112,... | collective-permute-start | bytes 245768 | tf_op jit(solution)/shard_map/ppermute | solution.py:20
  52.8 9.8 %copy-start.4 = (s32[512]{0:T(512)S(1)}, s32[512]{0:T(512)}, u32[]{:S(2)}) copy-start(s32[512]{0:T(512)} %param.8) | copy-start | bytes 6148
  53.5 17.2 %collective-permute-start.5 = (bf16[160,1280]{1,0:T(8,128)(2,1)S(1)}, bf16[160,1280]{1,0:T(8,128)(2,1)S(1)}, u32[]{:S(2)}, u32[]{:S(2)}) collective-permute-start(bf16[160,1280]{1,0:T(8,128)(2,1)S(1)} %get-tuple-element.15.refs_1_), channel_id=1, source_target_pairs={{0,16},{16,32},{32,48},{48,64},{64,80},{80,96},{96,112},{112,128},... | collective-permute-start | bytes 1228808 | tf_op jit(solution)/shard_map/ppermute | solution.py:20
  57.9 12.8 %collective-permute-start.4 = (bf16[160,1280]{1,0:T(8,128)(2,1)S(1)}, bf16[160,1280]{1,0:T(8,128)(2,1)}, u32[]{:S(2)}, u32[]{:S(2)}) collective-permute-start(bf16[160,1280]{1,0:T(8,128)(2,1)S(1)} %get-tuple-element.15.refs_1_), channel_id=1, source_target_pairs={{0,1008},{16,0},{32,16},{48,32},{64,48},{80,64},{96,80},{112,96},{... | collective-permute-start | bytes 1228808 | tf_op jit(solution)/shard_map/ppermute | solution.py:20
  62.8 7.9 %collective-permute-start.6 = (bf16[32,1280]{1,0:T(8,128)(2,1)S(1)}, bf16[32,1280]{1,0:T(8,128)(2,1)S(1)}, u32[]{:S(2)}, u32[]{:S(2)}) collective-permute-start(bf16[32,1280]{1,0:T(8,128)(2,1)S(1)} %collective-permute-done.2), channel_id=1, source_target_pairs={{0,992},{16,1008},{32,0},{48,16},{64,32},{80,48},{96,64},{112,80},... | collective-permute-start | bytes 245768 | tf_op jit(solution)/shard_map/ppermute | solution.py:20
  78.0 28.7 %all-to-all-start = ((f32[16,1,128]{2,1,0:T(1,128)}), f32[16,1,128]{2,1,0:T(1,128)S(1)}, u32[]{:S(2)}, u32[]{:S(2)}) async-start(f32[16,1,128]{2,1,0:T(1,128)} %broadcast_in_dim.7), calls=%async_computation | async-start | bytes 16384 | tf_op jit(solution)/shard_map/all_to_all | solution.py:110
  89.0 35.3 %collective-permute-start.9 = (f16[32,1152]{1,0:T(8,128)(2,1)S(1)}, f16[32,1152]{1,0:T(8,128)(2,1)}, u32[]{:S(2)}, u32[]{:S(2)}) collective-permute-start(f16[32,1152]{1,0:T(8,128)(2,1)S(1)} %convolution_convert_fusion.3), channel_id=1, source_target_pairs={{0,32},{16,48},{32,64},{48,80},{64,96},{80,112},{96,128},{112,144}... | collective-permute-start | bytes 221192 | tf_op jit(solution)/shard_map/ppermute | solution.py:20
  92.8 29.1 %collective-permute-start.7 = (f16[160,1152]{1,0:T(8,128)(2,1)}, f16[160,1152]{1,0:T(8,128)(2,1)}, u32[]{:S(2)}, u32[]{:S(2)}) collective-permute-start(f16[160,1152]{1,0:T(8,128)(2,1)} %convolution_convert_fusion.2), channel_id=1, source_target_pairs={{0,16},{16,32},{32,48},{48,64},{64,80},{80,96},{96,112},{112,128},... | collective-permute-start | bytes 1105928 | tf_op jit(solution)/shard_map/ppermute | solution.py:20
  94.8 27.2 %collective-permute-start.8 = (f16[160,1152]{1,0:T(8,128)(2,1)}, f16[160,1152]{1,0:T(8,128)(2,1)}, u32[]{:S(2)}, u32[]{:S(2)}) collective-permute-start(f16[160,1152]{1,0:T(8,128)(2,1)} %convolution_convert_fusion.1), channel_id=1, source_target_pairs={{0,1008},{16,0},{32,16},{48,32},{64,48},{80,64},{96,80},{112,96},{... | collective-permute-start | bytes 1105928 | tf_op jit(solution)/shard_map/ppermute | solution.py:20
  108.5 35.7 %all-to-all-start.1 = ((f32[64,1,128]{2,1,0:T(1,128)}), f32[64,1,128]{2,1,0:T(1,128)S(1)}, u32[]{:S(2)}, u32[]{:S(2)}) async-start(f32[64,1,128]{2,1,0:T(1,128)} %broadcast_in_dim.16), calls=%async_computation.1 | async-start | bytes 65536 | tf_op jit(solution)/shard_map/all_to_all | solution.py:112
  124.3 0.9 copy-start.1
  125.1 28.5 %copy-start.3 = (f16[160,1152]{1,0:T(8,128)(2,1)S(1)}, f16[160,1152]{1,0:T(8,128)(2,1)}, u32[]{:S(2)}) copy-start(f16[160,1152]{1,0:T(8,128)(2,1)} %get-tuple-element.27) | copy-start | bytes 1105924
  126.1 37.9 %collective-permute-start.10 = (f16[32,1152]{1,0:T(8,128)(2,1)S(1)}, f16[32,1152]{1,0:T(8,128)(2,1)S(1)}, u32[]{:S(2)}, u32[]{:S(2)}) collective-permute-start(f16[32,1152]{1,0:T(8,128)(2,1)S(1)} %fusion.12), channel_id=1, source_target_pairs={{0,96},{16,112},{32,128},{48,144},{64,160},{80,176},{96,192},{112,... | collective-permute-start | bytes 221192 | tf_op jit(solution)/shard_map/ppermute | solution.py:20
  144.2 28.7 %copy-start.2 = (bf16[32,1152]{1,0:T(8,128)(2,1)S(1)}, bf16[32,1152]{1,0:T(8,128)(2,1)}, u32[]{:S(2)}) copy-start(bf16[32,1152]{1,0:T(8,128)(2,1)} %param.7) | copy-start | bytes 221188
  144.2 31.5 %all-to-all-start.2 = ((f16[16,32,1152]{2,1,0:T(8,128)(2,1)}), f16[16,32,1152]{2,1,0:T(8,128)(2,1)S(1)}, u32[]{:S(2)}, u32[]{:S(2)}) async-start(f16[16,32,1152]{2,1,0:T(8,128)(2,1)} %bitcast.15), calls=%async_computation.2 | async-start | bytes 2359296 | tf_op jit(solution)/shard_map/all_to_all | solution.py:118
  153.7 18.7 %collective-permute-start.11 = (f16[32,1152]{1,0:T(8,128)(2,1)S(1)}, f16[32,1152]{1,0:T(8,128)(2,1)S(1)}, u32[]{:S(2)}, u32[]{:S(2)}) collective-permute-start(f16[32,1152]{1,0:T(8,128)(2,1)S(1)} %get-tuple-element.11), channel_id=1, source_target_pairs={{0,928},{16,944},{32,960},{48,976},{64,992},{80,1008},{96,0},{112,... | collective-permute-start | bytes 221192 | tf_op jit(solution)/shard_map/ppermute | solution.py:20
  155.7 17.2 %collective-permute-start.13 = (f16[32,1152]{1,0:T(8,128)(2,1)S(1)}, f16[32,1152]{1,0:T(8,128)(2,1)S(1)}, u32[]{:S(2)}, u32[]{:S(2)}) collective-permute-start(f16[32,1152]{1,0:T(8,128)(2,1)S(1)} %get-tuple-element.12), channel_id=1, source_target_pairs={{0,976},{16,992},{32,1008},{48,0},{64,16},{80,32},{96,48},{112,64}... | collective-permute-start | bytes 221192 | tf_op jit(solution)/shard_map/ppermute | solution.py:20
  157.8 15.1 %collective-permute-start.12 = (f16[32,1152]{1,0:T(8,128)(2,1)S(1)}, f16[32,1152]{1,0:T(8,128)(2,1)S(1)}, u32[]{:S(2)}, u32[]{:S(2)}) collective-permute-start(f16[32,1152]{1,0:T(8,128)(2,1)S(1)} %get-tuple-element.13), channel_id=1, source_target_pairs={{0,48},{16,64},{32,80},{48,96},{64,112},{80,128},{96,144},{112,160... | collective-permute-start | bytes 221192 | tf_op jit(solution)/shard_map/ppermute | solution.py:20

commit v2 on v1

--- a/solution.py
+++ b/solution.py
@@ -11,7 +11,6 @@
 BF16 = jnp.bfloat16
 F16 = jnp.float16
 F32 = jnp.float32
-CENTERS = (0, 3, -3, 6, -6)
 
 
 def passed_along(value, steps):
@@ -66,67 +65,102 @@
     )(params, text, vhat, vids)
 
 
+def own_kernel(width, text_ref, ids_ref, own_ref):
+    x32 = text_ref[...].astype(F32)
+    norms = jnp.sqrt(jnp.sum(x32 * x32, axis=-1, keepdims=True) + EPS)
+    own_ref[:, :width] = (x32 / norms).astype(BF16)
+    n = text_ref.shape[0]
+    row = lax.broadcasted_iota(jnp.int32, (n, n), 0)
+    col = lax.broadcasted_iota(jnp.int32, (n, n), 1)
+    ids = jnp.sum(jnp.where(row == col, ids_ref[...], 0.0), axis=1, keepdims=True)
+    high = jnp.floor(ids / ID_BASE)
+    lane = lax.broadcasted_iota(jnp.int32, (n, LANES), 1)
+    digits = jnp.where(lane == 0, high, ids - ID_BASE * high)
+    own_ref[:, width:] = digits.astype(BF16)
+
+
+def own_unit_slice(text, ids):
+    n, width = text.shape
+    vmem = pl.BlockSpec(memory_space=pltpu.VMEM)
+    return pl.pallas_call(
+        lambda *refs: own_kernel(width, *refs),
+        out_shape=jax.ShapeDtypeStruct((n, width + LANES), BF16),
+        in_specs=[vmem, vmem],
+        out_specs=vmem,
+    )(text, ids.astype(F32)[None, :])
+
+
 def shards(video, text, video_ids, text_ids, log_scale, bias):
     rows, width = video.shape
-    slice_rows = text.shape[0]
+    n = text.shape[0]
     nblk = lax.axis_size("blk")
     ndepth = lax.axis_size("depth")
     half = nblk // 8
 
-    tunit, tnorm = unit_rows(text)
-    digits = jnp.stack([text_ids // ID_BASE, text_ids % ID_BASE], axis=1).astype(BF16)
-    digits = jnp.pad(digits, ((0, 0), (0, LANES - 2)))
-    own = jnp.concatenate([tunit.astype(BF16), digits], axis=1)
+    own = own_unit_slice(text, text_ids)
+    up5 = passed_along(own, -5)
+    down4 = passed_along(own, 4)
 
-    far_up = passed_along(own, -6)
-    far_down = passed_along(own, 6)
-    up = passed_along(own, -3)
-    down = passed_along(own, 3)
-
-    vunit, vnorm = unit_rows(video)
+    vunit, _ = unit_rows(video)
     vhat = vunit.astype(BF16)
     vids = video_ids.astype(F32)[None, :]
     params = jnp.stack([jnp.exp(log_scale[0]), bias[0]])
 
-    bundle = jnp.concatenate([own, up, down, far_up, far_down], axis=0)
-    above = passed_along(bundle, -1)
-    below = passed_along(bundle, 1)
-    last = passed_along(far_up, -2)
+    up27 = passed_along(jnp.concatenate([own, up5], axis=0), -2)
+    down26 = passed_along(jnp.concatenate([own, down4], axis=0), 2)
+    ups = passed_along(jnp.concatenate([own, up27, up5], axis=0), -1)
+    downs = passed_along(jnp.concatenate([own, down4, down26, up5], axis=0), 1)
 
     def text_grad(coef):
         return jnp.einsum("cr,rd->cd", coef, vhat, preferred_element_type=F32)
 
-    coef0, loss0 = pair_coefs(params, bundle, vhat, vids)
-    grad0 = text_grad(coef0)
-    arrived = jnp.concatenate([above, below, last], axis=0)
+    held_text = jnp.concatenate([own, up27, up5, down4, down26], axis=0)
+    arrived = jnp.concatenate([ups, downs], axis=0)
+    coef0, loss0 = pair_coefs(params, held_text, vhat, vids)
     coef1, loss1 = pair_coefs(params, arrived, vhat, vids)
-    n = bundle.shape[0]
-    back_up = passed_along(text_grad(coef1[:n]).astype(F16), 1)
-    back_down = passed_along(text_grad(coef1[n : 2 * n]).astype(F16), -1)
-    back_last = passed_along(text_grad(coef1[2 * n :]).astype(F16), 2)
 
-    total = jnp.sum(loss0 + loss1)
-    total = jnp.full((ndepth, LANES), total)
-    total = jnp.sum(lax.all_to_all(total, "depth", 0, 0, tiled=True)[:, 0])
+    total = jnp.sum(loss0 + loss1) / (rows * nblk * 2 * half)
     total = jnp.full((nblk, LANES), total)
     total = jnp.sum(lax.all_to_all(total, "blk", 0, 0, tiled=True)[:, 0])
-    loss = total / (rows * nblk * 2 * half)
+
+    held = text_grad(coef0)
+    back_up = passed_along(text_grad(coef1[: 4 * n]).astype(F16), 1)
+    back_down = passed_along(text_grad(coef1[4 * n :]).astype(F16), -1)
 
     coefs = jnp.concatenate([coef0, coef1], axis=0)
-    texts = jnp.concatenate([bundle, arrived], axis=0)[:, :width]
-    share = jnp.einsum("cr,cd->rd", coefs, texts, preferred_element_type=F32)
-    shares = lax.all_to_all(share.astype(F16), "depth", 0, 0, tiled=True)
-    grad_vhat = jnp.sum(shares.reshape(ndepth, slice_rows, width).astype(F32), axis=0)
+    texts = jnp.concatenate([held_text, arrived], axis=0)
+    share = jnp.einsum("cr,cd->rd", coefs, texts, preferred_element_type=F32).astype(F16)
+    first = total.astype(F16)
+    rest = (total - first.astype(F32)) * 2.0**11
+    second = rest.astype(F16)
+    third = ((rest - second.astype(F32)) * 2.0**11).astype(F16)
+    lane = lax.broadcasted_iota(jnp.int32, (rows, LANES), 1)
+    digits = jnp.where(lane == 0, first, jnp.where(lane == 1, second, third))
+    share = lax.dynamic_update_slice(share, digits, (0, width))
+    shares = lax.all_to_all(share, "depth", 0, 0, tiled=True)
+    shares = shares.reshape(ndepth, n, width + LANES)
+    grad_vhat = jnp.sum(shares[:, :, :width].astype(F32), axis=0)
+    digits = jnp.sum(shares[:, 0, width : width + 3].astype(F32), axis=0)
+    loss = digits[0] + digits[1] * 2.0**-11 + digits[2] * 2.0**-22
 
-    held = grad0 + back_up.astype(F32) + back_down.astype(F32)
-    held = held.reshape(len(CENTERS), slice_rows, width)
-    held6 = held[3] + back_last.astype(F32)
-    home = [passed_along(held6.astype(F16), 6), passed_along(held[4].astype(F16), -6)]
-    home += [passed_along(held[1].astype(F16), 3), passed_along(held[2].astype(F16), -3)]
-    grad_that = held[0] + sum(part.astype(F32) for part in home)
+    held = held.reshape(7, n, width)
+    back_up = back_up.astype(F32).reshape(4, n, width)
+    back_down = back_down.astype(F32).reshape(5, n, width)
+    to_up = held[1:3] + back_up[1:3]
+    to_down = held[5:7] + back_down[2:4]
+    home5 = held[3] + back_up[3] + back_down[4]
+    home4 = held[4] + back_down[1]
+    home = held[0] + back_up[0] + back_down[0]
+    back_up = passed_along(to_up.astype(F16), 2).astype(F32)
+    back_down = passed_along(to_down.astype(F16), -2).astype(F32)
+    home5 = passed_along((home5 + back_up[1]).astype(F16), 5)
+    home4 = passed_along((home4 + back_down[1]).astype(F16), -4)
+    home = home + back_up[0] + back_down[0]
+    grad_that = home + home5.astype(F32) + home4.astype(F32)
 
-    offset = lax.axis_index("depth") * slice_rows
-    own_unit, own_norm = unit_rows(lax.dynamic_slice_in_dim(video, offset, slice_rows, 0))
+    tunit, tnorm = unit_rows(text)
+    offset = lax.axis_index("depth") * n
+    own_unit, own_norm = unit_rows(lax.dynamic_slice_in_dim(video, offset, n, 0))
     grad_video = (
         grad_vhat - own_unit * jnp.sum(own_unit * grad_vhat, axis=-1, keepdims=True)
     ) / own_norm

time: 180 us -> 166 us (0.922)
  starting transfers between devices: 107 us -> 89.3 us
  between operations: 3.99 us -> 7.31 us
  matrix products: 8.04 us -> 6.19 us
    all_to_all x2 -> x1, starting transfers between devices: 20.5 us -> 11 us  [shards(): shares = lax.all_to_all(share, 'depth', 0, 0, tiled=True)]
    ppermute x14 -> x12, starting transfers between devices: 72.9 us -> 64.2 us  [passed_along(): return lax.ppermute(value, 'blk', pairs)]
    convert_element_type x2 -> x6, other arithmetic: 2.02 us -> 6.04 us  [the longest x2 1.73 us: shards(): back_up = passed_along(to_up.astype(F16), 2).astype(F32)]
    dot_general x4 -> x3, matrix products: 4.87 us -> 2.9 us  [text_grad(): return jnp.einsum('cr,rd->cd', coef, vhat, preferred_element_type=F32)]
    concatenate x1 -> x2, local copies, waits for them, and re-layouts: 0.64 us -> 2.47 us  [the longest x1 1.78 us: shards(): texts = jnp.concatenate([held_text, arrived], axis=0)]
    unnamed x16 -> x23, local copies, waits for them, and re-layouts: 6.02 us -> 5.22 us
    ppermute x14 -> x12, waiting for transfers between devices: 23.8 us -> 24.1 us  [passed_along(): return lax.ppermute(value, 'blk', pairs)]
  transfers between devices with their start and end apart: 17 -> 14, of which waited for: 5 -> 6; matrix products, arithmetic and copies ran while one was open for 11% -> 13% of each run, Pallas kernels for 1% -> 1%
where the time goes in v2:
time: 166 us; the launch traced here: 165 us
  starting transfers between devices  89.3 us (54%)
  waiting for transfers between devices  33.8 us (20%)
  other arithmetic  14.7 us (9%)
  local copies, waits for them, and re-layouts  8.97 us (5%)
  between operations  7.31 us (4%)
  matrix products  6.19 us (4%)
  Pallas kernels  4.66 us (3%)
    ppermute x12, starting transfers between devices, passed_along(): return lax.ppermute(value, 'blk', pairs)  64.2 us
    ppermute x12, waiting for transfers between devices, passed_along(): return lax.ppermute(value, 'blk', pairs)  24.1 us
    all_to_all x1, starting transfers between devices, shards(): total = jnp.sum(lax.all_to_all(total, 'blk', 0, 0, tiled=True)[:, 0])  14.1 us
    all_to_all x1, starting transfers between devices, shards(): shares = lax.all_to_all(share, 'depth', 0, 0, tiled=True)  11 us
    all_to_all x1, waiting for transfers between devices, shards(): total = jnp.sum(lax.all_to_all(total, 'blk', 0, 0, tiled=True)[:, 0])  9.73 us
    unnamed x23, local copies, waits for them, and re-layouts  5.22 us
  transfers between devices with their start and end apart: 14, of which 6 were waited for; matrix products, arithmetic and copies ran while one was open for 13% of the time, Pallas kernels for 1%

profile of v2, /device:TPU:1, one launch (start us, length us, event | category | flops | bytes accessed | tf_op | source)
XLA Modules:
  0.0 165.0 jit_solution(14608527795442287117)
XLA Ops:
  1.9 1.6 shard_map.85
  3.5 9.6 %collective-permute-start.2 = (bf16[32,1280]{1,0:T(8,128)(2,1)}, bf16[32,1280]{1,0:T(8,128)(2,1)S(1)}, u32[]{:S(2)}, u32[]{:S(2)}) collective-permute-start(bf16[32,1280]{1,0:T(8,128)(2,1)} %shard_map.85), channel_id=1, source_target_pairs={{0,64},{16,80},{32,96},{48,112},{64,128},{80,144},{96,160},{112,17... | collective-permute-start | bytes 245768 | tf_op jit(solution)/shard_map/ppermute | solution.py:19
  13.2 17.6 %collective-permute-start = (bf16[32,1280]{1,0:T(8,128)(2,1)}, bf16[32,1280]{1,0:T(8,128)(2,1)S(1)}, u32[]{:S(2)}, u32[]{:S(2)}) collective-permute-start(bf16[32,1280]{1,0:T(8,128)(2,1)} %shard_map.85), channel_id=1, source_target_pairs={{0,944},{16,960},{32,976},{48,992},{64,1008},{80,0},{96,16},{112,3... | collective-permute-start | bytes 245768 | tf_op jit(solution)/shard_map/ppermute | solution.py:19
  33.7 1.6 fusion
  37.3 1.9 %collective-permute-start.1 = (bf16[64,1280]{1,0:T(8,128)(2,1)S(1)}, bf16[64,1280]{1,0:T(8,128)(2,1)S(1)}, u32[]{:S(2)}, u32[]{:S(2)}) collective-permute-start(bf16[64,1280]{1,0:T(8,128)(2,1)S(1)} %get-tuple-element.28), channel_id=1, source_target_pairs={{0,992},{16,1008},{32,0},{48,16},{64,32},{80,48},{96,64},{112,80},... | collective-permute-start | bytes 491528 | tf_op jit(solution)/shard_map/ppermute | solution.py:19
  39.5 4.2 %collective-permute-start.3 = (bf16[64,1280]{1,0:T(8,128)(2,1)S(1)}, bf16[64,1280]{1,0:T(8,128)(2,1)S(1)}, u32[]{:S(2)}, u32[]{:S(2)}) collective-permute-start(bf16[64,1280]{1,0:T(8,128)(2,1)S(1)} %get-tuple-element.27), channel_id=1, source_target_pairs={{0,32},{16,48},{32,64},{48,80},{64,96},{80,112},{96,128},{112,144}... | collective-permute-start | bytes 491528 | tf_op jit(solution)/shard_map/ppermute | solution.py:19
  43.7 5.3 %collective-permute-done.1 = bf16[64,1280]{1,0:T(8,128)(2,1)S(1)} collective-permute-done((bf16[64,1280]{1,0:T(8,128)(2,1)S(1)}, bf16[64,1280]{1,0:T(8,128)(2,1)S(1)}, u32[]{:S(2)}, u32[]{:S(2)}) %collective-permute-start.1) | collective-permute-done | bytes 163872 | tf_op jit(solution)/shard_map/ppermute | solution.py:19
  49.0 1.9 %collective-permute-start.4 = (bf16[128,1280]{1,0:T(8,128)(2,1)S(1)}, bf16[128,1280]{1,0:T(8,128)(2,1)S(1)}, u32[]{:S(2)}, u32[]{:S(2)}) collective-permute-start(bf16[128,1280]{1,0:T(8,128)(2,1)S(1)} %pad_maximum_fusion.2), channel_id=1, source_target_pairs={{0,1008},{16,0},{32,16},{48,32},{64,48},{80,64},{96,80},{112,96},{... | collective-permute-start | bytes 983048 | tf_op jit(solution)/shard_map/ppermute | solution.py:19
  50.9 4.6 %collective-permute-start.5 = (bf16[160,1280]{1,0:T(8,128)(2,1)S(1)}, bf16[160,1280]{1,0:T(8,128)(2,1)S(1)}, u32[]{:S(2)}, u32[]{:S(2)}) collective-permute-start(bf16[160,1280]{1,0:T(8,128)(2,1)S(1)} %pad_maximum_fusion.1), channel_id=1, source_target_pairs={{0,16},{16,32},{32,48},{48,64},{64,80},{80,96},{96,112},{112,128},... | collective-permute-start | bytes 1228808 | tf_op jit(solution)/shard_map/ppermute | solution.py:19
  61.9 7.4 %collective-permute-done.5 = bf16[160,1280]{1,0:T(8,128)(2,1)S(1)} collective-permute-done((bf16[160,1280]{1,0:T(8,128)(2,1)S(1)}, bf16[160,1280]{1,0:T(8,128)(2,1)S(1)}, u32[]{:S(2)}, u32[]{:S(2)}) %collective-permute-start.5) | collective-permute-done | bytes 409632 | tf_op jit(solution)/shard_map/ppermute | solution.py:19
  69.3 1.6 shard_map.87
  74.3 14.1 %all-to-all-start = ((f32[64,1,128]{2,1,0:T(1,128)}), f32[64,1,128]{2,1,0:T(1,128)S(1)}, u32[]{:S(2)}, u32[]{:S(2)}) async-start(f32[64,1,128]{2,1,0:T(1,128)} %broadcast_in_dim.28), calls=%async_computation | async-start | bytes 65536 | tf_op jit(solution)/shard_map/all_to_all | solution.py:124
  88.4 2.9 %collective-permute-start.6 = (f16[128,1152]{1,0:T(8,128)(2,1)}, f16[128,1152]{1,0:T(8,128)(2,1)}, u32[]{:S(2)}, u32[]{:S(2)}) collective-permute-start(f16[128,1152]{1,0:T(8,128)(2,1)} %convolution_convert_fusion.2), channel_id=1, source_target_pairs={{0,16},{16,32},{32,48},{48,64},{64,80},{80,96},{96,112},{112,128},... | collective-permute-start | bytes 884744 | tf_op jit(solution)/shard_map/ppermute | solution.py:19
  91.3 4.5 %collective-permute-start.7 = (f16[160,1152]{1,0:T(8,128)(2,1)S(1)}, f16[160,1152]{1,0:T(8,128)(2,1)}, u32[]{:S(2)}, u32[]{:S(2)}) collective-permute-start(f16[160,1152]{1,0:T(8,128)(2,1)S(1)} %convolution_convert_fusion.1), channel_id=1, source_target_pairs={{0,1008},{16,0},{32,16},{48,32},{64,48},{80,64},{96,80},{112,96},{... | collective-permute-start | bytes 1105928 | tf_op jit(solution)/shard_map/ppermute | solution.py:19
  95.8 1.8 %constant_dynamic-update-slice_fusion.5 = bf16[512,1280]{1,0:T(8,128)(2,1)} fusion(bf16[512,1280]{1,0:T(8,128)(2,1)} %constant_dynamic-update-slice_fusion.6, bf16[160,1280]{1,0:T(8,128)(2,1)} %copy-done.5), kind=kLoop, calls=%fused_computation.56 | loop fusion | bytes 819200 | tf_op jit(solution)/shard_map/concatenate | solution.py:131
  97.6 3.3 %convolution_convert_fusion = f16[512,1280]{1,0:T(8,128)(2,1)} fusion(bf16[512,1280]{1,0:T(8,128)(2,1)} %constant_dynamic-update-slice_fusion.5, bf16[288,512]{1,0:T(8,128)(2,1)S(1)} %get-tuple-element.8, bf16[224,512]{1,0:T(8,128)(2,1)S(1)} %get-tuple-element.7), kind=kOutput, calls=%fused_computation | convolution fusion | flops 672792576 | bytes 3145728 | tf_op jit(solution)/shard_map/cr,cd->rd/dot_general | solution.py:132
  100.8 9.7 %all-to-all-done = f32[64,1,128]{2,1,0:T(1,128)S(1)} async-done(((f32[64,1,128]{2,1,0:T(1,128)}), f32[64,1,128]{2,1,0:T(1,128)S(1)}, u32[]{:S(2)}, u32[]{:S(2)}) %all-to-all-start) | async-done | bytes 32800 | tf_op jit(solution)/shard_map/all_to_all | solution.py:124
  116.5 2.2 %collective-permute-start.8 = (f16[2,32,1152]{2,1,0:T(8,128)(2,1)}, f16[2,32,1152]{2,1,0:T(8,128)(2,1)}, u32[]{:S(2)}, u32[]{:S(2)}) collective-permute-start(f16[2,32,1152]{2,1,0:T(8,128)(2,1)} %bitcast.5), channel_id=1, source_target_pairs={{0,32},{16,48},{32,64},{48,80},{64,96},{80,112},{96,128},{112,144}... | collective-permute-start | bytes 442376 | tf_op jit(solution)/shard_map/ppermute | solution.py:19
  118.7 6.1 %collective-permute-start.9 = (f16[2,32,1152]{2,1,0:T(8,128)(2,1)}, f16[2,32,1152]{2,1,0:T(8,128)(2,1)}, u32[]{:S(2)}, u32[]{:S(2)}) collective-permute-start(f16[2,32,1152]{2,1,0:T(8,128)(2,1)} %bitcast.7), channel_id=1, source_target_pairs={{0,992},{16,1008},{32,0},{48,16},{64,32},{80,48},{96,64},{112,80},... | collective-permute-start | bytes 442376 | tf_op jit(solution)/shard_map/ppermute | solution.py:19
  125.5 11.0 %all-to-all-start.1 = ((f16[16,32,1280]{2,1,0:T(8,128)(2,1)}), f16[16,32,1280]{2,1,0:T(8,128)(2,1)S(1)}, u32[]{:S(2)}, u32[]{:S(2)}) async-start(f16[16,32,1280]{2,1,0:T(8,128)(2,1)} %bitcast.43), calls=%async_computation.1 | async-start | bytes 2621440 | tf_op jit(solution)/shard_map/all_to_all | solution.py:140
  139.5 1.9 %collective-permute-start.11 = (f16[32,1152]{1,0:T(8,128)(2,1)S(1)}, f16[32,1152]{1,0:T(8,128)(2,1)S(1)}, u32[]{:S(2)}, u32[]{:S(2)}) collective-permute-start(f16[32,1152]{1,0:T(8,128)(2,1)S(1)} %get-tuple-element.14), channel_id=1, source_target_pairs={{0,960},{16,976},{32,992},{48,1008},{64,0},{80,16},{96,32},{112,48... | collective-permute-start | bytes 221192 | tf_op jit(solution)/shard_map/ppermute | solution.py:19
  141.4 6.7 %collective-permute-start.10 = (f16[32,1152]{1,0:T(8,128)(2,1)S(1)}, f16[32,1152]{1,0:T(8,128)(2,1)S(1)}, u32[]{:S(2)}, u32[]{:S(2)}) collective-permute-start(f16[32,1152]{1,0:T(8,128)(2,1)S(1)} %get-tuple-element.13), channel_id=1, source_target_pairs={{0,80},{16,96},{32,112},{48,128},{64,144},{80,160},{96,176},{112,1... | collective-permute-start | bytes 221192 | tf_op jit(solution)/shard_map/ppermute | solution.py:19
  148.1 3.7 %collective-permute-done.11 = f16[32,1152]{1,0:T(8,128)(2,1)S(1)} collective-permute-done((f16[32,1152]{1,0:T(8,128)(2,1)S(1)}, f16[32,1152]{1,0:T(8,128)(2,1)S(1)}, u32[]{:S(2)}, u32[]{:S(2)}) %collective-permute-start.11) | collective-permute-done | bytes 73760 | tf_op jit(solution)/shard_map/ppermute | solution.py:19
  151.9 6.3 %collective-permute-done.10 = f16[32,1152]{1,0:T(8,128)(2,1)S(1)} collective-permute-done((f16[32,1152]{1,0:T(8,128)(2,1)S(1)}, f16[32,1152]{1,0:T(8,128)(2,1)S(1)}, u32[]{:S(2)}, u32[]{:S(2)}) %collective-permute-start.10) | collective-permute-done | bytes 73760 | tf_op jit(solution)/shard_map/ppermute | solution.py:19
  (69 shorter events, 26.2 us)
Async XLA Ops:
  0.6 34.6 %copy-start = (bf16[512,1152]{1,0:T(8,128)(2,1)S(1)}, bf16[512,1152]{1,0:T(8,128)(2,1)}, u32[]{:S(2)}) copy-start(bf16[512,1152]{1,0:T(8,128)(2,1)} %param.6) | copy-start | bytes 3538948
  3.5 32.3 %collective-permute-start.2 = (bf16[32,1280]{1,0:T(8,128)(2,1)}, bf16[32,1280]{1,0:T(8,128)(2,1)S(1)}, u32[]{:S(2)}, u32[]{:S(2)}) collective-permute-start(bf16[32,1280]{1,0:T(8,128)(2,1)} %shard_map.85), channel_id=1, source_target_pairs={{0,64},{16,80},{32,96},{48,112},{64,128},{80,144},{96,160},{112,17... | collective-permute-start | bytes 245768 | tf_op jit(solution)/shard_map/ppermute | solution.py:19
  13.2 24.1 %collective-permute-start = (bf16[32,1280]{1,0:T(8,128)(2,1)}, bf16[32,1280]{1,0:T(8,128)(2,1)S(1)}, u32[]{:S(2)}, u32[]{:S(2)}) collective-permute-start(bf16[32,1280]{1,0:T(8,128)(2,1)} %shard_map.85), channel_id=1, source_target_pairs={{0,944},{16,960},{32,976},{48,992},{64,1008},{80,0},{96,16},{112,3... | collective-permute-start | bytes 245768 | tf_op jit(solution)/shard_map/ppermute | solution.py:19
  35.2 2.0 %copy-start.4 = (bf16[32,1280]{1,0:T(8,128)(2,1)S(1)}, bf16[32,1280]{1,0:T(8,128)(2,1)}, u32[]{:S(2)}) copy-start(bf16[32,1280]{1,0:T(8,128)(2,1)} %shard_map.85) | copy-start | bytes 245764
  35.3 4.1 %copy-start.8 = (s32[512]{0:T(512)S(1)}, s32[512]{0:T(512)}, u32[]{:S(2)}) copy-start(s32[512]{0:T(512)} %param.8) | copy-start | bytes 6148
  35.3 4.0 %copy-start.6 = (bf16[32,1152]{1,0:T(8,128)(2,1)S(1)}, bf16[32,1152]{1,0:T(8,128)(2,1)}, u32[]{:S(2)}) copy-start(bf16[32,1152]{1,0:T(8,128)(2,1)} %refs_0_.1) | copy-start | bytes 221188
  37.3 11.7 %collective-permute-start.1 = (bf16[64,1280]{1,0:T(8,128)(2,1)S(1)}, bf16[64,1280]{1,0:T(8,128)(2,1)S(1)}, u32[]{:S(2)}, u32[]{:S(2)}) collective-permute-start(bf16[64,1280]{1,0:T(8,128)(2,1)S(1)} %get-tuple-element.28), channel_id=1, source_target_pairs={{0,992},{16,1008},{32,0},{48,16},{64,32},{80,48},{96,64},{112,80},... | collective-permute-start | bytes 491528 | tf_op jit(solution)/shard_map/ppermute | solution.py:19
  39.5 11.5 %collective-permute-start.3 = (bf16[64,1280]{1,0:T(8,128)(2,1)S(1)}, bf16[64,1280]{1,0:T(8,128)(2,1)S(1)}, u32[]{:S(2)}, u32[]{:S(2)}) collective-permute-start(bf16[64,1280]{1,0:T(8,128)(2,1)S(1)} %get-tuple-element.27), channel_id=1, source_target_pairs={{0,32},{16,48},{32,64},{48,80},{64,96},{80,112},{96,128},{112,144}... | collective-permute-start | bytes 491528 | tf_op jit(solution)/shard_map/ppermute | solution.py:19
  49.0 12.2 %collective-permute-start.4 = (bf16[128,1280]{1,0:T(8,128)(2,1)S(1)}, bf16[128,1280]{1,0:T(8,128)(2,1)S(1)}, u32[]{:S(2)}, u32[]{:S(2)}) collective-permute-start(bf16[128,1280]{1,0:T(8,128)(2,1)S(1)} %pad_maximum_fusion.2), channel_id=1, source_target_pairs={{0,1008},{16,0},{32,16},{48,32},{64,48},{80,64},{96,80},{112,96},{... | collective-permute-start | bytes 983048 | tf_op jit(solution)/shard_map/ppermute | solution.py:19
  50.9 18.3 %collective-permute-start.5 = (bf16[160,1280]{1,0:T(8,128)(2,1)S(1)}, bf16[160,1280]{1,0:T(8,128)(2,1)S(1)}, u32[]{:S(2)}, u32[]{:S(2)}) collective-permute-start(bf16[160,1280]{1,0:T(8,128)(2,1)S(1)} %pad_maximum_fusion.1), channel_id=1, source_target_pairs={{0,16},{16,32},{32,48},{48,64},{64,80},{80,96},{96,112},{112,128},... | collective-permute-start | bytes 1228808 | tf_op jit(solution)/shard_map/ppermute | solution.py:19
  69.3 1.6 copy-start.5
  74.3 36.3 %all-to-all-start = ((f32[64,1,128]{2,1,0:T(1,128)}), f32[64,1,128]{2,1,0:T(1,128)S(1)}, u32[]{:S(2)}, u32[]{:S(2)}) async-start(f32[64,1,128]{2,1,0:T(1,128)} %broadcast_in_dim.28), calls=%async_computation | async-start | bytes 65536 | tf_op jit(solution)/shard_map/all_to_all | solution.py:124
  88.4 24.2 %collective-permute-start.6 = (f16[128,1152]{1,0:T(8,128)(2,1)}, f16[128,1152]{1,0:T(8,128)(2,1)}, u32[]{:S(2)}, u32[]{:S(2)}) collective-permute-start(f16[128,1152]{1,0:T(8,128)(2,1)} %convolution_convert_fusion.2), channel_id=1, source_target_pairs={{0,16},{16,32},{32,48},{48,64},{64,80},{80,96},{96,112},{112,128},... | collective-permute-start | bytes 884744 | tf_op jit(solution)/shard_map/ppermute | solution.py:19
  91.3 22.3 %collective-permute-start.7 = (f16[160,1152]{1,0:T(8,128)(2,1)S(1)}, f16[160,1152]{1,0:T(8,128)(2,1)}, u32[]{:S(2)}, u32[]{:S(2)}) collective-permute-start(f16[160,1152]{1,0:T(8,128)(2,1)S(1)} %convolution_convert_fusion.1), channel_id=1, source_target_pairs={{0,1008},{16,0},{32,16},{48,32},{64,48},{80,64},{96,80},{112,96},{... | collective-permute-start | bytes 1105928 | tf_op jit(solution)/shard_map/ppermute | solution.py:19
  100.8 14.9 %copy-start.1 = (f32[224,1152]{1,0:T(8,128)S(1)}, f32[224,1152]{1,0:T(8,128)}, u32[]{:S(2)}) copy-start(f32[224,1152]{1,0:T(8,128)} %fusion.23) | copy-start | bytes 3096580
  113.5 11.9 %copy-start.3 = (f32[128,1152]{1,0:T(8,128)}, f32[128,1152]{1,0:T(8,128)S(1)}, u32[]{:S(2)}) copy-start(f32[128,1152]{1,0:T(8,128)S(1)} %convert_element_type.99) | copy-start | bytes 1769476
  114.8 0.9 copy-start.2
  116.5 20.0 %collective-permute-start.8 = (f16[2,32,1152]{2,1,0:T(8,128)(2,1)}, f16[2,32,1152]{2,1,0:T(8,128)(2,1)}, u32[]{:S(2)}, u32[]{:S(2)}) collective-permute-start(f16[2,32,1152]{2,1,0:T(8,128)(2,1)} %bitcast.5), channel_id=1, source_target_pairs={{0,32},{16,48},{32,64},{48,80},{64,96},{80,112},{96,128},{112,144}... | collective-permute-start | bytes 442376 | tf_op jit(solution)/shard_map/ppermute | solution.py:19
  118.7 18.7 %collective-permute-start.9 = (f16[2,32,1152]{2,1,0:T(8,128)(2,1)}, f16[2,32,1152]{2,1,0:T(8,128)(2,1)}, u32[]{:S(2)}, u32[]{:S(2)}) collective-permute-start(f16[2,32,1152]{2,1,0:T(8,128)(2,1)} %bitcast.7), channel_id=1, source_target_pairs={{0,992},{16,1008},{32,0},{48,16},{64,32},{80,48},{96,64},{112,80},... | collective-permute-start | bytes 442376 | tf_op jit(solution)/shard_map/ppermute | solution.py:19
  125.5 34.7 %all-to-all-start.1 = ((f16[16,32,1280]{2,1,0:T(8,128)(2,1)}), f16[16,32,1280]{2,1,0:T(8,128)(2,1)S(1)}, u32[]{:S(2)}, u32[]{:S(2)}) async-start(f16[16,32,1280]{2,1,0:T(8,128)(2,1)} %bitcast.43), calls=%async_computation.1 | async-start | bytes 2621440 | tf_op jit(solution)/shard_map/all_to_all | solution.py:140
  136.4 21.7 %copy-start.7 = (bf16[32,1152]{1,0:T(8,128)(2,1)S(1)}, bf16[32,1152]{1,0:T(8,128)(2,1)}, u32[]{:S(2)}) copy-start(bf16[32,1152]{1,0:T(8,128)(2,1)} %refs_0_.1) | copy-start | bytes 221188
  139.5 12.4 %collective-permute-start.11 = (f16[32,1152]{1,0:T(8,128)(2,1)S(1)}, f16[32,1152]{1,0:T(8,128)(2,1)S(1)}, u32[]{:S(2)}, u32[]{:S(2)}) collective-permute-start(f16[32,1152]{1,0:T(8,128)(2,1)S(1)} %get-tuple-element.14), channel_id=1, source_target_pairs={{0,960},{16,976},{32,992},{48,1008},{64,0},{80,16},{96,32},{112,48... | collective-permute-start | bytes 221192 | tf_op jit(solution)/shard_map/ppermute | solution.py:19
  141.4 16.7 %collective-permute-start.10 = (f16[32,1152]{1,0:T(8,128)(2,1)S(1)}, f16[32,1152]{1,0:T(8,128)(2,1)S(1)}, u32[]{:S(2)}, u32[]{:S(2)}) collective-permute-start(f16[32,1152]{1,0:T(8,128)(2,1)S(1)} %get-tuple-element.13), channel_id=1, source_target_pairs={{0,80},{16,96},{32,112},{48,128},{64,144},{80,160},{96,176},{112,1... | collective-permute-start | bytes 221192 | tf_op jit(solution)/shard_map/ppermute | solution.py:19

commit v3 on v2

--- a/solution.py
+++ b/solution.py
@@ -25,8 +25,8 @@
     return (x32 / norms, norms)
 
 
-def coef_kernel(width, params, text_ref, vhat_ref, vids_ref, coef_ref, loss_ref):
-    scale, bias = (params[0], params[1])
+def coef_kernel(width, params, text_ref, vhat_ref, vids_ref, before_ref, coef_ref, loss_ref):
+    scale, bias, part = (params[0], params[1], params[2])
     marks = text_ref[:, width : width + LANES].astype(F32)
     tids = marks[:, 0:1] * ID_BASE + marks[:, 1:2]
     dots = lax.dot_general(
@@ -42,19 +42,21 @@
     losses = jnp.maximum(z, 0.0) + jnp.log1p(e)
     sig = jnp.where(z >= 0, 1.0, e) / (1.0 + e)
     coef_ref[...] = (flip * sig * scale).astype(BF16)
-    loss_ref[...] = jnp.sum(losses, axis=0, keepdims=True)
-
-
-def pair_coefs(params, text, vhat, vids):
+    total = jnp.sum(losses, axis=0, keepdims=True)
+    total = jnp.sum(total, axis=1, keepdims=True) * part
+    loss_ref[...] = before_ref[...] + total
+
+
+def pair_coefs(params, text, vhat, vids, before):
     rows, width = vhat.shape
     vmem = pl.BlockSpec(memory_space=pltpu.VMEM)
     return pl.pallas_call(
         lambda *refs: coef_kernel(width, *refs),
         out_shape=(
             jax.ShapeDtypeStruct((text.shape[0], rows), BF16),
-            jax.ShapeDtypeStruct((1, rows), F32),
+            jax.ShapeDtypeStruct(before.shape, F32),
         ),
-        in_specs=[pl.BlockSpec(memory_space=pltpu.SMEM), vmem, vmem, vmem],
+        in_specs=[pl.BlockSpec(memory_space=pltpu.SMEM), vmem, vmem, vmem, vmem],
         out_specs=(vmem, vmem),
         compiler_params=pltpu.CompilerParams(vmem_limit_bytes=24 * 1024 * 1024),
         cost_estimate=pl.CostEstimate(
@@ -62,7 +64,7 @@
             bytes_accessed=2 * width * (text.shape[0] + rows),
             transcendentals=3 * text.shape[0] * rows,
         ),
-    )(params, text, vhat, vids)
+    )(params, text, vhat, vids, before)
 
 
 def own_kernel(width, text_ref, ids_ref, own_ref):
@@ -72,7 +74,8 @@
     n = text_ref.shape[0]
     row = lax.broadcasted_iota(jnp.int32, (n, n), 0)
     col = lax.broadcasted_iota(jnp.int32, (n, n), 1)
-    ids = jnp.sum(jnp.where(row == col, ids_ref[...], 0.0), axis=1, keepdims=True)
+    ids = jnp.where(row == col, ids_ref[...].astype(F32), 0.0)
+    ids = jnp.sum(ids, axis=1, keepdims=True)
     high = jnp.floor(ids / ID_BASE)
     lane = lax.broadcasted_iota(jnp.int32, (n, LANES), 1)
     digits = jnp.where(lane == 0, high, ids - ID_BASE * high)
@@ -87,7 +90,13 @@
         out_shape=jax.ShapeDtypeStruct((n, width + LANES), BF16),
         in_specs=[vmem, vmem],
         out_specs=vmem,
-    )(text, ids.astype(F32)[None, :])
+    )(text, ids[None, :])
+
+
+def exchanged(value, side):
+    count = lax.axis_size("blk")
+    pairs = [(b, (b + (1 if (b + side) % 2 == 0 else -1)) % count) for b in range(count)]
+    return lax.ppermute(value, "blk", pairs)
 
 
 def shards(video, text, video_ids, text_ids, log_scale, bias):
@@ -96,6 +105,7 @@
     nblk = lax.axis_size("blk")
     ndepth = lax.axis_size("depth")
     half = nblk // 8
+    even = lax.axis_index("blk") % 2 == 0
 
     own = own_unit_slice(text, text_ids)
     up5 = passed_along(own, -5)
@@ -104,32 +114,53 @@
     vunit, _ = unit_rows(video)
     vhat = vunit.astype(BF16)
     vids = video_ids.astype(F32)[None, :]
-    params = jnp.stack([jnp.exp(log_scale[0]), bias[0]])
+    part = jnp.float32(1.0 / (rows * nblk * 2 * half))
+    params = jnp.stack([jnp.exp(log_scale[0]), bias[0], part])
 
     up27 = passed_along(jnp.concatenate([own, up5], axis=0), -2)
     down26 = passed_along(jnp.concatenate([own, down4], axis=0), 2)
-    ups = passed_along(jnp.concatenate([own, up27, up5], axis=0), -1)
-    downs = passed_along(jnp.concatenate([own, down4, down26, up5], axis=0), 1)
+    for_lower = jnp.concatenate([own, up27[:n], up5, up27[n:], up5], axis=0)
+    for_upper = jnp.concatenate([own, down4, down26, up5], axis=0)
+    side0 = exchanged(jnp.where(even, for_upper, for_lower), 0)
+    side1 = exchanged(jnp.where(even, for_lower, for_upper), 1)
 
     def text_grad(coef):
         return jnp.einsum("cr,rd->cd", coef, vhat, preferred_element_type=F32)
 
+    def video_grad(coef, texts):
+        return jnp.einsum("cr,cd->rd", coef, texts, preferred_element_type=F32)
+
     held_text = jnp.concatenate([own, up27, up5, down4, down26], axis=0)
-    arrived = jnp.concatenate([ups, downs], axis=0)
-    coef0, loss0 = pair_coefs(params, held_text, vhat, vids)
-    coef1, loss1 = pair_coefs(params, arrived, vhat, vids)
-
-    total = jnp.sum(loss0 + loss1) / (rows * nblk * 2 * half)
-    total = jnp.full((nblk, LANES), total)
-    total = jnp.sum(lax.all_to_all(total, "blk", 0, 0, tiled=True)[:, 0])
-
+    coef0, total = pair_coefs(params, held_text, vhat, vids, jnp.zeros((nblk, LANES), F32))
+    share0 = video_grad(coef0, held_text)
     held = text_grad(coef0)
-    back_up = passed_along(text_grad(coef1[: 4 * n]).astype(F16), 1)
-    back_down = passed_along(text_grad(coef1[4 * n :]).astype(F16), -1)
-
-    coefs = jnp.concatenate([coef0, coef1], axis=0)
-    texts = jnp.concatenate([held_text, arrived], axis=0)
-    share = jnp.einsum("cr,cd->rd", coefs, texts, preferred_element_type=F32).astype(F16)
+
+    fifth = jnp.where(even, side1[4 * n :], side0[4 * n :])
+    arrived = jnp.concatenate([side0[: 4 * n], side1[: 4 * n], fifth], axis=0)
+    coef1, total = pair_coefs(params, arrived, vhat, vids, total)
+
+    coef_side0 = jnp.concatenate([coef1[: 4 * n], coef1[8 * n :]], axis=0)
+    back0 = exchanged(text_grad(coef_side0).astype(F16), 0)
+    back1 = exchanged(text_grad(coef1[4 * n :]).astype(F16), 1)
+
+    share = (share0 + video_grad(coef1, arrived)).astype(F16)
+    share, total = lax.optimization_barrier((share, total))
+    totals = lax.all_to_all(total, "blk", 0, 0, tiled=True)
+
+    def unit_of(value, i):
+        return value[i * n : (i + 1) * n].astype(F32)
+
+    def of_sides(i, j):
+        low = jnp.where(even, unit_of(back1, i), unit_of(back0, i)) if i is not None else 0.0
+        high = jnp.where(even, unit_of(back0, j), unit_of(back1, j)) if j is not None else 0.0
+        return low + high
+
+    to_up = [unit_of(held, 1) + of_sides(1, None), unit_of(held, 2) + of_sides(3, None)]
+    to_down = [unit_of(held, 5) + of_sides(None, 2), unit_of(held, 6) + of_sides(None, 3)]
+    back_up = passed_along(jnp.concatenate(to_up, axis=0).astype(F16), 2)
+    back_down = passed_along(jnp.concatenate(to_down, axis=0).astype(F16), -2)
+    totals, _, _ = lax.optimization_barrier((totals, back_up, back_down))
+    total = jnp.sum(totals[:, 0])
     first = total.astype(F16)
     rest = (total - first.astype(F32)) * 2.0**11
     second = rest.astype(F16)
@@ -143,19 +174,11 @@
     digits = jnp.sum(shares[:, 0, width : width + 3].astype(F32), axis=0)
     loss = digits[0] + digits[1] * 2.0**-11 + digits[2] * 2.0**-22
 
-    held = held.reshape(7, n, width)
-    back_up = back_up.astype(F32).reshape(4, n, width)
-    back_down = back_down.astype(F32).reshape(5, n, width)
-    to_up = held[1:3] + back_up[1:3]
-    to_down = held[5:7] + back_down[2:4]
-    home5 = held[3] + back_up[3] + back_down[4]
-    home4 = held[4] + back_down[1]
-    home = held[0] + back_up[0] + back_down[0]
-    back_up = passed_along(to_up.astype(F16), 2).astype(F32)
-    back_down = passed_along(to_down.astype(F16), -2).astype(F32)
-    home5 = passed_along((home5 + back_up[1]).astype(F16), 5)
-    home4 = passed_along((home4 + back_down[1]).astype(F16), -4)
-    home = home + back_up[0] + back_down[0]
+    home5 = unit_of(held, 3) + of_sides(2, 4) + unit_of(back_up, 1)
+    home4 = unit_of(held, 4) + of_sides(None, 1) + unit_of(back_down, 1)
+    home = unit_of(held, 0) + of_sides(0, 0) + unit_of(back_up, 0) + unit_of(back_down, 0)
+    home5 = passed_along(home5.astype(F16), 5)
+    home4 = passed_along(home4.astype(F16), -4)
     grad_that = home + home5.astype(F32) + home4.astype(F32)
 
     tunit, tnorm = unit_rows(text)

time: 166 us -> 158 us (0.952)
  local copies, waits for them, and re-layouts: 8.97 us -> 4.41 us
  other arithmetic: 14.7 us -> 10.9 us
  waiting for transfers between devices: 33.8 us -> 35.9 us
  starting transfers between devices: 89.3 us -> 87.5 us
    ppermute x0 -> x4, starting transfers between devices: none -> 15.6 us  [exchanged(): return lax.ppermute(value, 'blk', pairs)]
    ppermute x12 -> x8, starting transfers between devices: 64.2 us -> 53.1 us  [passed_along(): return lax.ppermute(value, 'blk', pairs)]
    ppermute x12 -> x8, waiting for transfers between devices: 24.1 us -> 18 us  [passed_along(): return lax.ppermute(value, 'blk', pairs)]
    all_to_all x1, starting transfers between devices: 14.1 us -> 8.21 us  [shards(): totals = lax.all_to_all(total, 'blk', 0, 0, tiled=True)]
    ppermute x0 -> x4, waiting for transfers between devices: none -> 5 us  [exchanged(): return lax.ppermute(value, 'blk', pairs)]
    convert_element_type x6 -> x1, other arithmetic: 6.04 us -> 1.27 us  [shards(): home5 = passed_along(home5.astype(F16), 5)]
    all_to_all x1, waiting for transfers between devices: 9.73 us -> 12.9 us  [shards(): totals = lax.all_to_all(total, 'blk', 0, 0, tiled=True)]
    unnamed x23 -> x26, local copies, waits for them, and re-layouts: 5.22 us -> 3.08 us
  transfers between devices with their start and end apart: 14 -> 14, of which waited for: 6 -> 8; matrix products, arithmetic and copies ran while one was open for 13% -> 9% of each run, Pallas kernels for 1% -> 1%
where the time goes in v3:
time: 158 us; the launch traced here: 157 us
  starting transfers between devices  87.5 us (55%)
  waiting for transfers between devices  35.9 us (23%)
  other arithmetic  10.9 us (7%)
  between operations  6.64 us (4%)
  matrix products  6.22 us (4%)
  Pallas kernels  5.53 us (4%)
  local copies, waits for them, and re-layouts  4.41 us (3%)
    ppermute x8, starting transfers between devices, passed_along(): return lax.ppermute(value, 'blk', pairs)  53.1 us
    ppermute x8, waiting for transfers between devices, passed_along(): return lax.ppermute(value, 'blk', pairs)  18 us
    ppermute x4, starting transfers between devices, exchanged(): return lax.ppermute(value, 'blk', pairs)  15.6 us
    all_to_all x1, waiting for transfers between devices, shards(): totals = lax.all_to_all(total, 'blk', 0, 0, tiled=True)  12.9 us
    all_to_all x1, starting transfers between devices, shards(): shares = lax.all_to_all(share, 'depth', 0, 0, tiled=True)  10.6 us
    all_to_all x1, starting transfers between devices, shards(): totals = lax.all_to_all(total, 'blk', 0, 0, tiled=True)  8.21 us
    ppermute x4, waiting for transfers between devices, exchanged(): return lax.ppermute(value, 'blk', pairs)  5 us
    pallas_call x2, Pallas kernels, pair_coefs(): pl.pallas_call(lambda *refs: coef_kernel(width, *refs), out_shape=(jax.Sh...  3.8 us
  transfers between devices with their start and end apart: 14, of which 8 were waited for; matrix products, arithmetic and copies ran while one was open for 9% of the time, Pallas kernels for 1%

profile of v3, /device:TPU:1, one launch (start us, length us, event | category | flops | bytes accessed | tf_op | source)
XLA Modules:
  0.0 157.1 jit_solution(18049663169778180823)
XLA Ops:
  0.6 1.7 %shard_map.85 = bf16[32,1280]{1,0:T(8,128)(2,1)} custom-call(bf16[32,1152]{1,0:T(8,128)(2,1)} %refs_0_.1, s32[1,32]{1,0:T(1,128)} %bitcast.18), custom_call_target="tpu_custom_call" | custom-call | tf_op jit(solution)/shard_map/pallas_call | solution.py:88
  2.4 23.2 %collective-permute-start = (bf16[32,1280]{1,0:T(8,128)(2,1)}, bf16[32,1280]{1,0:T(8,128)(2,1)S(1)}, u32[]{:S(2)}, u32[]{:S(2)}) collective-permute-start(bf16[32,1280]{1,0:T(8,128)(2,1)} %shard_map.85), channel_id=1, source_target_pairs={{0,944},{16,960},{32,976},{48,992},{64,1008},{80,0},{96,16},{112,3... | collective-permute-start | bytes 245768 | tf_op jit(solution)/shard_map/ppermute | solution.py:19
  25.6 4.0 %collective-permute-start.2 = (bf16[32,1280]{1,0:T(8,128)(2,1)}, bf16[32,1280]{1,0:T(8,128)(2,1)S(1)}, u32[]{:S(2)}, u32[]{:S(2)}) collective-permute-start(bf16[32,1280]{1,0:T(8,128)(2,1)} %shard_map.85), channel_id=1, source_target_pairs={{0,64},{16,80},{32,96},{48,112},{64,128},{80,144},{96,160},{112,17... | collective-permute-start | bytes 245768 | tf_op jit(solution)/shard_map/ppermute | solution.py:19
  29.6 1.6 %fusion.1 = f32[512]{0:T(512)S(1)} fusion(bf16[512,1152]{1,0:T(8,128)(2,1)} %param.6), kind=kLoop, calls=%fused_computation.6 | loop fusion | flops 1768960 | bytes 1181696 | tf_op jit(solution)/shard_map/reduce_sum | solution.py:24
  34.1 7.5 %collective-permute-done.2 = bf16[32,1280]{1,0:T(8,128)(2,1)S(1)} collective-permute-done((bf16[32,1280]{1,0:T(8,128)(2,1)}, bf16[32,1280]{1,0:T(8,128)(2,1)S(1)}, u32[]{:S(2)}, u32[]{:S(2)}) %collective-permute-start.2) | collective-permute-done | bytes 81952 | tf_op jit(solution)/shard_map/ppermute | solution.py:19
  42.4 1.9 %collective-permute-start.1 = (bf16[64,1280]{1,0:T(8,128)(2,1)}, bf16[64,1280]{1,0:T(8,128)(2,1)S(1)}, u32[]{:S(2)}, u32[]{:S(2)}) collective-permute-start(bf16[64,1280]{1,0:T(8,128)(2,1)} %get-tuple-element.32), channel_id=1, source_target_pairs={{0,992},{16,1008},{32,0},{48,16},{64,32},{80,48},{96,64},{112,80},... | collective-permute-start | bytes 491528 | tf_op jit(solution)/shard_map/ppermute | solution.py:19
  44.6 4.3 %collective-permute-start.3 = (bf16[64,1280]{1,0:T(8,128)(2,1)}, bf16[64,1280]{1,0:T(8,128)(2,1)S(1)}, u32[]{:S(2)}, u32[]{:S(2)}) collective-permute-start(bf16[64,1280]{1,0:T(8,128)(2,1)} %get-tuple-element.31), channel_id=1, source_target_pairs={{0,32},{16,48},{32,64},{48,80},{64,96},{80,112},{96,128},{112,144}... | collective-permute-start | bytes 491528 | tf_op jit(solution)/shard_map/ppermute | solution.py:19
  48.8 3.6 %collective-permute-done.1 = bf16[64,1280]{1,0:T(8,128)(2,1)S(1)} collective-permute-done((bf16[64,1280]{1,0:T(8,128)(2,1)}, bf16[64,1280]{1,0:T(8,128)(2,1)S(1)}, u32[]{:S(2)}, u32[]{:S(2)}) %collective-permute-start.1) | collective-permute-done | bytes 163872 | tf_op jit(solution)/shard_map/ppermute | solution.py:19
  56.8 2.9 %collective-permute-start.4 = (bf16[160,1280]{1,0:T(8,128)(2,1)S(1)}, bf16[160,1280]{1,0:T(8,128)(2,1)S(1)}, u32[]{:S(2)}, u32[]{:S(2)}) collective-permute-start(bf16[160,1280]{1,0:T(8,128)(2,1)S(1)} %get-tuple-element.26), channel_id=1, source_target_pairs={{0,16},{16,0},{32,48},{48,32},{64,80},{80,64},{96,112},{112,96},{1... | collective-permute-start | bytes 1228808 | tf_op jit(solution)/shard_map/ppermute | solution.py:99
  59.7 4.6 %collective-permute-start.5 = (bf16[160,1280]{1,0:T(8,128)(2,1)S(1)}, bf16[160,1280]{1,0:T(8,128)(2,1)S(1)}, u32[]{:S(2)}, u32[]{:S(2)}) collective-permute-start(bf16[160,1280]{1,0:T(8,128)(2,1)S(1)} %get-tuple-element.25), channel_id=1, source_target_pairs={{0,1008},{16,32},{32,16},{48,64},{64,48},{80,96},{96,80},{112,128}... | collective-permute-start | bytes 1228808 | tf_op jit(solution)/shard_map/ppermute | solution.py:99
  64.4 1.5 shard_map.86
  67.5 4.8 %collective-permute-done.5 = bf16[160,1280]{1,0:T(8,128)(2,1)S(1)} collective-permute-done((bf16[160,1280]{1,0:T(8,128)(2,1)S(1)}, bf16[160,1280]{1,0:T(8,128)(2,1)S(1)}, u32[]{:S(2)}, u32[]{:S(2)}) %collective-permute-start.5) | collective-permute-done | bytes 409632 | tf_op jit(solution)/shard_map/ppermute | solution.py:99
  72.4 2.3 %shard_map.87 = (bf16[288,512]{1,0:T(8,128)(2,1)S(1)}, f32[64,128]{1,0:T(8,128)}) custom-call(f32[3]{0:T(128)S(1)} %pad_maximum_fusion.6.refs_0_, bf16[288,1280]{1,0:T(8,128)(2,1)S(1)} %pad_maximum_fusion.refs_1_, bf16[512,1152]{1,0:T(8,128)(2,1)S(1)} %fusion.2.refs_2_, f32[1,512]{1,0:T(1,128)S(1)} %bitcast.16, f32[64,128]{1,0:T(8,128)S(1)} %get-tuple-element.11.refs_4_), custom_call_target="tpu_custom_call" | custom-call | flops 339738624 | bytes 1843200 | tf_op jit(solution)/shard_map/pallas_call | solution.py:53
  77.0 1.9 %collective-permute-start.7 = (f16[160,1152]{1,0:T(8,128)(2,1)}, f16[160,1152]{1,0:T(8,128)(2,1)S(1)}, u32[]{:S(2)}, u32[]{:S(2)}) collective-permute-start(f16[160,1152]{1,0:T(8,128)(2,1)} %convolution_convert_fusion), channel_id=1, source_target_pairs={{0,16},{16,0},{32,48},{48,32},{64,80},{80,64},{96,112},{112,96},{1... | collective-permute-start | bytes 1105928 | tf_op jit(solution)/shard_map/ppermute | solution.py:99
  78.9 6.2 %collective-permute-start.6 = (f16[160,1152]{1,0:T(8,128)(2,1)}, f16[160,1152]{1,0:T(8,128)(2,1)S(1)}, u32[]{:S(2)}, u32[]{:S(2)}) collective-permute-start(f16[160,1152]{1,0:T(8,128)(2,1)} %convolution_convert_fusion.1), channel_id=1, source_target_pairs={{0,1008},{16,32},{32,16},{48,64},{64,48},{80,96},{96,80},{112,128}... | collective-permute-start | bytes 1105928 | tf_op jit(solution)/shard_map/ppermute | solution.py:99
  86.0 1.6 %fusion = f16[512,1280]{1,0:T(8,128)(2,1)} fusion(f32[512,1280]{1,0:T(8,128)S(1)} %fusion.32, bf16[224,512]{1,0:T(8,128)(2,1)S(1)} %get-tuple-element.10, bf16[224,1280]{1,0:T(8,128)(2,1)S(1)} %constant_dynamic-update-slice_fusion.refs_1_), kind=kOutput, calls=%fused_computation.1 | convolution fusion | flops 294912000 | bytes 4734976 | tf_op jit(solution)/shard_map/cr,cd->rd/dot_general | solution.py:131
  87.7 8.2 %all-to-all-start = ((f32[64,1,128]{2,1,0:T(1,128)}), f32[64,1,128]{2,1,0:T(1,128)S(1)}, u32[]{:S(2)}, u32[]{:S(2)}) async-start(f32[64,1,128]{2,1,0:T(1,128)} %bitcast.3), calls=%async_computation | async-start | bytes 65536 | tf_op jit(solution)/shard_map/all_to_all | solution.py:148
  96.1 6.2 %collective-permute-start.9 = (f16[64,1152]{1,0:T(8,128)(2,1)S(1)}, f16[64,1152]{1,0:T(8,128)(2,1)S(1)}, u32[]{:S(2)}, u32[]{:S(2)}) collective-permute-start(f16[64,1152]{1,0:T(8,128)(2,1)S(1)} %pad_maximum_fusion.5), channel_id=1, source_target_pairs={{0,992},{16,1008},{32,0},{48,16},{64,32},{80,48},{96,64},{112,80},... | collective-permute-start | bytes 442376 | tf_op jit(solution)/shard_map/ppermute | solution.py:19
  103.1 1.9 %collective-permute-start.8 = (f16[64,1152]{1,0:T(8,128)(2,1)}, f16[64,1152]{1,0:T(8,128)(2,1)S(1)}, u32[]{:S(2)}, u32[]{:S(2)}) collective-permute-start(f16[64,1152]{1,0:T(8,128)(2,1)} %pad_maximum_fusion.4), channel_id=1, source_target_pairs={{0,32},{16,48},{32,64},{48,80},{64,96},{80,112},{96,128},{112,144}... | collective-permute-start | bytes 442376 | tf_op jit(solution)/shard_map/ppermute | solution.py:19
  105.1 12.9 %all-to-all-done = f32[64,1,128]{2,1,0:T(1,128)S(1)} async-done(((f32[64,1,128]{2,1,0:T(1,128)}), f32[64,1,128]{2,1,0:T(1,128)S(1)}, u32[]{:S(2)}, u32[]{:S(2)}) %all-to-all-start) | async-done | bytes 32800 | tf_op jit(solution)/shard_map/all_to_all | solution.py:148
  120.7 10.6 %all-to-all-start.1 = ((f16[16,32,1280]{2,1,0:T(8,128)(2,1)}), f16[16,32,1280]{2,1,0:T(8,128)(2,1)S(1)}, u32[]{:S(2)}, u32[]{:S(2)}) async-start(f16[16,32,1280]{2,1,0:T(8,128)(2,1)} %bitcast.5), calls=%async_computation.1 | async-start | bytes 2621440 | tf_op jit(solution)/shard_map/all_to_all | solution.py:171
  132.6 3.6 %collective-permute-start.10 = (f16[32,1152]{1,0:T(8,128)(2,1)S(1)}, f16[32,1152]{1,0:T(8,128)(2,1)S(1)}, u32[]{:S(2)}, u32[]{:S(2)}) collective-permute-start(f16[32,1152]{1,0:T(8,128)(2,1)S(1)} %get-tuple-element.19), channel_id=1, source_target_pairs={{0,80},{16,96},{32,112},{48,128},{64,144},{80,160},{96,176},{112,1... | collective-permute-start | bytes 221192 | tf_op jit(solution)/shard_map/ppermute | solution.py:19
  136.1 8.1 %collective-permute-start.11 = (f16[32,1152]{1,0:T(8,128)(2,1)S(1)}, f16[32,1152]{1,0:T(8,128)(2,1)S(1)}, u32[]{:S(2)}, u32[]{:S(2)}) collective-permute-start(f16[32,1152]{1,0:T(8,128)(2,1)S(1)} %get-tuple-element.20), channel_id=1, source_target_pairs={{0,960},{16,976},{32,992},{48,1008},{64,0},{80,16},{96,32},{112,48... | collective-permute-start | bytes 221192 | tf_op jit(solution)/shard_map/ppermute | solution.py:19
  144.2 6.1 %collective-permute-done.10 = f16[32,1152]{1,0:T(8,128)(2,1)S(1)} collective-permute-done((f16[32,1152]{1,0:T(8,128)(2,1)S(1)}, f16[32,1152]{1,0:T(8,128)(2,1)S(1)}, u32[]{:S(2)}, u32[]{:S(2)}) %collective-permute-start.10) | collective-permute-done | bytes 73760 | tf_op jit(solution)/shard_map/ppermute | solution.py:19
  (73 shorter events, 19.3 us)
Async XLA Ops:
  0.6 30.6 %copy-start = (bf16[512,1152]{1,0:T(8,128)(2,1)S(1)}, bf16[512,1152]{1,0:T(8,128)(2,1)}, u32[]{:S(2)}) copy-start(bf16[512,1152]{1,0:T(8,128)(2,1)} %param.6) | copy-start | bytes 3538948
  2.4 31.8 %collective-permute-start = (bf16[32,1280]{1,0:T(8,128)(2,1)}, bf16[32,1280]{1,0:T(8,128)(2,1)S(1)}, u32[]{:S(2)}, u32[]{:S(2)}) collective-permute-start(bf16[32,1280]{1,0:T(8,128)(2,1)} %shard_map.85), channel_id=1, source_target_pairs={{0,944},{16,960},{32,976},{48,992},{64,1008},{80,0},{96,16},{112,3... | collective-permute-start | bytes 245768 | tf_op jit(solution)/shard_map/ppermute | solution.py:19
  25.6 16.1 %collective-permute-start.2 = (bf16[32,1280]{1,0:T(8,128)(2,1)}, bf16[32,1280]{1,0:T(8,128)(2,1)S(1)}, u32[]{:S(2)}, u32[]{:S(2)}) collective-permute-start(bf16[32,1280]{1,0:T(8,128)(2,1)} %shard_map.85), channel_id=1, source_target_pairs={{0,64},{16,80},{32,96},{48,112},{64,128},{80,144},{96,160},{112,17... | collective-permute-start | bytes 245768 | tf_op jit(solution)/shard_map/ppermute | solution.py:19
  31.2 0.9 copy-start.2
  31.2 13.2 %copy-start.9 = (s32[512]{0:T(512)S(1)}, s32[512]{0:T(512)}, u32[]{:S(2)}) copy-start(s32[512]{0:T(512)} %param.8) | copy-start | bytes 6148
  31.2 13.2 %copy-start.3 = (bf16[32,1152]{1,0:T(8,128)(2,1)S(1)}, bf16[32,1152]{1,0:T(8,128)(2,1)}, u32[]{:S(2)}) copy-start(bf16[32,1152]{1,0:T(8,128)(2,1)} %refs_0_.1) | copy-start | bytes 221188
  42.4 10.0 %collective-permute-start.1 = (bf16[64,1280]{1,0:T(8,128)(2,1)}, bf16[64,1280]{1,0:T(8,128)(2,1)S(1)}, u32[]{:S(2)}, u32[]{:S(2)}) collective-permute-start(bf16[64,1280]{1,0:T(8,128)(2,1)} %get-tuple-element.32), channel_id=1, source_target_pairs={{0,992},{16,1008},{32,0},{48,16},{64,32},{80,48},{96,64},{112,80},... | collective-permute-start | bytes 491528 | tf_op jit(solution)/shard_map/ppermute | solution.py:19
  44.6 11.1 %collective-permute-start.3 = (bf16[64,1280]{1,0:T(8,128)(2,1)}, bf16[64,1280]{1,0:T(8,128)(2,1)S(1)}, u32[]{:S(2)}, u32[]{:S(2)}) collective-permute-start(bf16[64,1280]{1,0:T(8,128)(2,1)} %get-tuple-element.31), channel_id=1, source_target_pairs={{0,32},{16,48},{32,64},{48,80},{64,96},{80,112},{96,128},{112,144}... | collective-permute-start | bytes 491528 | tf_op jit(solution)/shard_map/ppermute | solution.py:19
  56.8 10.7 %collective-permute-start.4 = (bf16[160,1280]{1,0:T(8,128)(2,1)S(1)}, bf16[160,1280]{1,0:T(8,128)(2,1)S(1)}, u32[]{:S(2)}, u32[]{:S(2)}) collective-permute-start(bf16[160,1280]{1,0:T(8,128)(2,1)S(1)} %get-tuple-element.26), channel_id=1, source_target_pairs={{0,16},{16,0},{32,48},{48,32},{64,80},{80,64},{96,112},{112,96},{1... | collective-permute-start | bytes 1228808 | tf_op jit(solution)/shard_map/ppermute | solution.py:99
  59.7 12.6 %collective-permute-start.5 = (bf16[160,1280]{1,0:T(8,128)(2,1)S(1)}, bf16[160,1280]{1,0:T(8,128)(2,1)S(1)}, u32[]{:S(2)}, u32[]{:S(2)}) collective-permute-start(bf16[160,1280]{1,0:T(8,128)(2,1)S(1)} %get-tuple-element.25), channel_id=1, source_target_pairs={{0,1008},{16,32},{32,16},{48,64},{64,48},{80,96},{96,80},{112,128}... | collective-permute-start | bytes 1228808 | tf_op jit(solution)/shard_map/ppermute | solution.py:99
  77.0 18.9 %collective-permute-start.7 = (f16[160,1152]{1,0:T(8,128)(2,1)}, f16[160,1152]{1,0:T(8,128)(2,1)S(1)}, u32[]{:S(2)}, u32[]{:S(2)}) collective-permute-start(f16[160,1152]{1,0:T(8,128)(2,1)} %convolution_convert_fusion), channel_id=1, source_target_pairs={{0,16},{16,0},{32,48},{48,32},{64,80},{80,64},{96,112},{112,96},{1... | collective-permute-start | bytes 1105928 | tf_op jit(solution)/shard_map/ppermute | solution.py:99
  78.9 17.0 %collective-permute-start.6 = (f16[160,1152]{1,0:T(8,128)(2,1)}, f16[160,1152]{1,0:T(8,128)(2,1)S(1)}, u32[]{:S(2)}, u32[]{:S(2)}) collective-permute-start(f16[160,1152]{1,0:T(8,128)(2,1)} %convolution_convert_fusion.1), channel_id=1, source_target_pairs={{0,1008},{16,32},{32,16},{48,64},{64,48},{80,96},{96,80},{112,128}... | collective-permute-start | bytes 1105928 | tf_op jit(solution)/shard_map/ppermute | solution.py:99
  86.0 9.9 %copy-start.1 = (f32[224,1152]{1,0:T(8,128)S(1)}, f32[224,1152]{1,0:T(8,128)}, u32[]{:S(2)}) copy-start(f32[224,1152]{1,0:T(8,128)} %fusion.35) | copy-start | bytes 3096580
  87.7 30.3 %all-to-all-start = ((f32[64,1,128]{2,1,0:T(1,128)}), f32[64,1,128]{2,1,0:T(1,128)S(1)}, u32[]{:S(2)}, u32[]{:S(2)}) async-start(f32[64,1,128]{2,1,0:T(1,128)} %bitcast.3), calls=%async_computation | async-start | bytes 65536 | tf_op jit(solution)/shard_map/all_to_all | solution.py:148
  95.9 24.8 %copy-start.5 = (f16[160,1152]{1,0:T(8,128)(2,1)}, f16[160,1152]{1,0:T(8,128)(2,1)S(1)}, u32[]{:S(2)}) copy-start(f16[160,1152]{1,0:T(8,128)(2,1)S(1)} %collective-permute-done.7) | copy-start | bytes 1105924
  95.9 24.8 %copy-start.6 = (f16[160,1152]{1,0:T(8,128)(2,1)}, f16[160,1152]{1,0:T(8,128)(2,1)S(1)}, u32[]{:S(2)}) copy-start(f16[160,1152]{1,0:T(8,128)(2,1)S(1)} %collective-permute-done.6) | copy-start | bytes 1105924
  96.1 21.9 %collective-permute-start.9 = (f16[64,1152]{1,0:T(8,128)(2,1)S(1)}, f16[64,1152]{1,0:T(8,128)(2,1)S(1)}, u32[]{:S(2)}, u32[]{:S(2)}) collective-permute-start(f16[64,1152]{1,0:T(8,128)(2,1)S(1)} %pad_maximum_fusion.5), channel_id=1, source_target_pairs={{0,992},{16,1008},{32,0},{48,16},{64,32},{80,48},{96,64},{112,80},... | collective-permute-start | bytes 442376 | tf_op jit(solution)/shard_map/ppermute | solution.py:19
  103.1 14.9 %collective-permute-start.8 = (f16[64,1152]{1,0:T(8,128)(2,1)}, f16[64,1152]{1,0:T(8,128)(2,1)S(1)}, u32[]{:S(2)}, u32[]{:S(2)}) collective-permute-start(f16[64,1152]{1,0:T(8,128)(2,1)} %pad_maximum_fusion.4), channel_id=1, source_target_pairs={{0,32},{16,48},{32,64},{48,80},{64,96},{80,112},{96,128},{112,144}... | collective-permute-start | bytes 442376 | tf_op jit(solution)/shard_map/ppermute | solution.py:19
  118.0 2.7 %copy-start.7 = (f16[64,1152]{1,0:T(8,128)(2,1)}, f16[64,1152]{1,0:T(8,128)(2,1)S(1)}, u32[]{:S(2)}) copy-start(f16[64,1152]{1,0:T(8,128)(2,1)S(1)} %collective-permute-done.9) | copy-start | bytes 442372
  118.0 2.7 %copy-start.8 = (f16[64,1152]{1,0:T(8,128)(2,1)}, f16[64,1152]{1,0:T(8,128)(2,1)S(1)}, u32[]{:S(2)}) copy-start(f16[64,1152]{1,0:T(8,128)(2,1)S(1)} %collective-permute-done.8) | copy-start | bytes 442372
  120.7 31.6 %all-to-all-start.1 = ((f16[16,32,1280]{2,1,0:T(8,128)(2,1)}), f16[16,32,1280]{2,1,0:T(8,128)(2,1)S(1)}, u32[]{:S(2)}, u32[]{:S(2)}) async-start(f16[16,32,1280]{2,1,0:T(8,128)(2,1)} %bitcast.5), calls=%async_computation.1 | async-start | bytes 2621440 | tf_op jit(solution)/shard_map/all_to_all | solution.py:171
  131.3 20.3 %copy-start.4 = (bf16[32,1152]{1,0:T(8,128)(2,1)S(1)}, bf16[32,1152]{1,0:T(8,128)(2,1)}, u32[]{:S(2)}) copy-start(bf16[32,1152]{1,0:T(8,128)(2,1)} %refs_0_.1) | copy-start | bytes 221188
  132.6 17.7 %collective-permute-start.10 = (f16[32,1152]{1,0:T(8,128)(2,1)S(1)}, f16[32,1152]{1,0:T(8,128)(2,1)S(1)}, u32[]{:S(2)}, u32[]{:S(2)}) collective-permute-start(f16[32,1152]{1,0:T(8,128)(2,1)S(1)} %get-tuple-element.19), channel_id=1, source_target_pairs={{0,80},{16,96},{32,112},{48,128},{64,144},{80,160},{96,176},{112,1... | collective-permute-start | bytes 221192 | tf_op jit(solution)/shard_map/ppermute | solution.py:19
  136.1 14.2 %collective-permute-start.11 = (f16[32,1152]{1,0:T(8,128)(2,1)S(1)}, f16[32,1152]{1,0:T(8,128)(2,1)S(1)}, u32[]{:S(2)}, u32[]{:S(2)}) collective-permute-start(f16[32,1152]{1,0:T(8,128)(2,1)S(1)} %get-tuple-element.20), channel_id=1, source_target_pairs={{0,960},{16,976},{32,992},{48,1008},{64,0},{80,16},{96,32},{112,48... | collective-permute-start | bytes 221192 | tf_op jit(solution)/shard_map/ppermute | solution.py:19

commit v4 on v3

--- a/solution.py
+++ b/solution.py
@@ -13,10 +13,19 @@
 F32 = jnp.float32
 
 
-def passed_along(value, steps):
-    count = lax.axis_size("blk")
-    pairs = [(source, (source + steps) % count) for source in range(count)]
-    return lax.ppermute(value, "blk", pairs)
+def passed_along(value, steps0, steps1):
+    nblk, ndepth = (lax.axis_size("blk"), lax.axis_size("depth"))
+    pairs = []
+    for b in range(nblk):
+        for d in range(ndepth):
+            to = (b + (steps1 if d % 2 else steps0)) % nblk
+            pairs.append((b * ndepth + d, to * ndepth + d))
+    return lax.ppermute(value, ("blk", "depth"), pairs)
+
+
+def core_swapped(value):
+    ndepth = lax.axis_size("depth")
+    return lax.ppermute(value, "depth", [(d, d ^ 1) for d in range(ndepth)])
 
 
 def unit_rows(x):
@@ -93,36 +102,35 @@
     )(text, ids[None, :])
 
 
-def exchanged(value, side):
-    count = lax.axis_size("blk")
-    pairs = [(b, (b + (1 if (b + side) % 2 == 0 else -1)) % count) for b in range(count)]
-    return lax.ppermute(value, "blk", pairs)
-
-
 def shards(video, text, video_ids, text_ids, log_scale, bias):
     rows, width = video.shape
     n = text.shape[0]
     nblk = lax.axis_size("blk")
     ndepth = lax.axis_size("depth")
     half = nblk // 8
-    even = lax.axis_index("blk") % 2 == 0
+    depth = lax.axis_index("depth")
+    core0 = depth % 2 == 0
 
     own = own_unit_slice(text, text_ids)
-    up5 = passed_along(own, -5)
-    down4 = passed_along(own, 4)
-
-    vunit, _ = unit_rows(video)
+    r1 = passed_along(own, -5, 4)
+    r2 = passed_along(own, 4, -5)
+
+    def by_core(x):
+        x = x.reshape(ndepth // 2, 2, n, *x.shape[1:])
+        mine = jnp.where(core0, x[:, 0], x[:, 1])
+        other = jnp.where(core0, x[:, 1], x[:, 0])
+        return jnp.stack([mine, other]).reshape(rows, *x.shape[3:])
+
+    vunit, _ = unit_rows(by_core(video))
     vhat = vunit.astype(BF16)
-    vids = video_ids.astype(F32)[None, :]
+    vids = by_core(video_ids).astype(F32)[None, :]
     part = jnp.float32(1.0 / (rows * nblk * 2 * half))
     params = jnp.stack([jnp.exp(log_scale[0]), bias[0], part])
 
-    up27 = passed_along(jnp.concatenate([own, up5], axis=0), -2)
-    down26 = passed_along(jnp.concatenate([own, down4], axis=0), 2)
-    for_lower = jnp.concatenate([own, up27[:n], up5, up27[n:], up5], axis=0)
-    for_upper = jnp.concatenate([own, down4, down26, up5], axis=0)
-    side0 = exchanged(jnp.where(even, for_upper, for_lower), 0)
-    side1 = exchanged(jnp.where(even, for_lower, for_upper), 1)
+    q1 = passed_along(jnp.concatenate([own, r1], axis=0), -2, 2)
+    q2 = passed_along(jnp.concatenate([own, r2], axis=0), 2, -2)
+    s1 = passed_along(jnp.concatenate([own, q1, r1, r2], axis=0), -1, 1)
+    s2 = passed_along(jnp.concatenate([own, q2, r2, r1], axis=0), 1, -1)
 
     def text_grad(coef):
         return jnp.einsum("cr,rd->cd", coef, vhat, preferred_element_type=F32)
@@ -130,60 +138,64 @@
     def video_grad(coef, texts):
         return jnp.einsum("cr,cd->rd", coef, texts, preferred_element_type=F32)
 
-    held_text = jnp.concatenate([own, up27, up5, down4, down26], axis=0)
+    held_text = jnp.concatenate([own, q1, r1, q2, r2], axis=0)
     coef0, total = pair_coefs(params, held_text, vhat, vids, jnp.zeros((nblk, LANES), F32))
     share0 = video_grad(coef0, held_text)
     held = text_grad(coef0)
-
-    fifth = jnp.where(even, side1[4 * n :], side0[4 * n :])
-    arrived = jnp.concatenate([side0[: 4 * n], side1[: 4 * n], fifth], axis=0)
+    s1, s2, share0, held = lax.optimization_barrier((s1, s2, share0, held))
+
+    fifth = jnp.where(core0, s2[4 * n :], s1[4 * n :])
+    arrived = jnp.concatenate([s1[: 4 * n], s2[: 4 * n], fifth], axis=0)
     coef1, total = pair_coefs(params, arrived, vhat, vids, total)
 
-    coef_side0 = jnp.concatenate([coef1[: 4 * n], coef1[8 * n :]], axis=0)
-    back0 = exchanged(text_grad(coef_side0).astype(F16), 0)
-    back1 = exchanged(text_grad(coef1[4 * n :]).astype(F16), 1)
-
-    share = (share0 + video_grad(coef1, arrived)).astype(F16)
-    share, total = lax.optimization_barrier((share, total))
+    total = total + core_swapped(total)
     totals = lax.all_to_all(total, "blk", 0, 0, tiled=True)
+
+    coef_s1 = jnp.concatenate([coef1[: 4 * n], coef1[8 * n :]], axis=0)
+    m1 = passed_along(text_grad(coef_s1).astype(F16), 1, -1)
+    m2 = passed_along(text_grad(coef1[4 * n :]).astype(F16), -1, 1)
+    m1, m2, _ = lax.optimization_barrier((m1, m2, total))
+
+    mid = rows // 2
+    sent = (share0[mid:] + video_grad(coef1[:, mid:], arrived)).astype(F16)
+    share = share0[:mid] + video_grad(coef1[:, :mid], arrived)
+    share = (share + core_swapped(sent).astype(F32)).astype(F16)
 
     def unit_of(value, i):
         return value[i * n : (i + 1) * n].astype(F32)
 
-    def of_sides(i, j):
-        low = jnp.where(even, unit_of(back1, i), unit_of(back0, i)) if i is not None else 0.0
-        high = jnp.where(even, unit_of(back0, j), unit_of(back1, j)) if j is not None else 0.0
-        return low + high
-
-    to_up = [unit_of(held, 1) + of_sides(1, None), unit_of(held, 2) + of_sides(3, None)]
-    to_down = [unit_of(held, 5) + of_sides(None, 2), unit_of(held, 6) + of_sides(None, 3)]
-    back_up = passed_along(jnp.concatenate(to_up, axis=0).astype(F16), 2)
-    back_down = passed_along(jnp.concatenate(to_down, axis=0).astype(F16), -2)
-    totals, _, _ = lax.optimization_barrier((totals, back_up, back_down))
+    def pair_of(i, back):
+        units = [unit_of(held, i) + unit_of(back, 1), unit_of(held, i + 1) + unit_of(back, 2)]
+        return jnp.concatenate(units, axis=0).astype(F16)
+
+    n1 = passed_along(pair_of(1, m1), 2, -2)
+    n2 = passed_along(pair_of(4, m2), -2, 2)
+
+    totals, _, _ = lax.optimization_barrier((totals, n1, n2))
     total = jnp.sum(totals[:, 0])
     first = total.astype(F16)
     rest = (total - first.astype(F32)) * 2.0**11
     second = rest.astype(F16)
     third = ((rest - second.astype(F32)) * 2.0**11).astype(F16)
-    lane = lax.broadcasted_iota(jnp.int32, (rows, LANES), 1)
+    lane = lax.broadcasted_iota(jnp.int32, (mid, LANES), 1)
     digits = jnp.where(lane == 0, first, jnp.where(lane == 1, second, third))
     share = lax.dynamic_update_slice(share, digits, (0, width))
-    shares = lax.all_to_all(share, "depth", 0, 0, tiled=True)
-    shares = shares.reshape(ndepth, n, width + LANES)
+    groups = [list(range(core, ndepth, 2)) for core in range(2)]
+    shares = lax.all_to_all(share, "depth", 0, 0, axis_index_groups=groups, tiled=True)
+    shares = shares.reshape(ndepth // 2, n, width + LANES)
     grad_vhat = jnp.sum(shares[:, :, :width].astype(F32), axis=0)
     digits = jnp.sum(shares[:, 0, width : width + 3].astype(F32), axis=0)
     loss = digits[0] + digits[1] * 2.0**-11 + digits[2] * 2.0**-22
 
-    home5 = unit_of(held, 3) + of_sides(2, 4) + unit_of(back_up, 1)
-    home4 = unit_of(held, 4) + of_sides(None, 1) + unit_of(back_down, 1)
-    home = unit_of(held, 0) + of_sides(0, 0) + unit_of(back_up, 0) + unit_of(back_down, 0)
-    home5 = passed_along(home5.astype(F16), 5)
-    home4 = passed_along(home4.astype(F16), -4)
-    grad_that = home + home5.astype(F32) + home4.astype(F32)
+    h1 = unit_of(held, 3) + unit_of(m1, 3) + jnp.where(core0, unit_of(m2, 4), 0.0) + unit_of(n1, 1)
+    h2 = unit_of(held, 6) + unit_of(m2, 3) + jnp.where(core0, 0.0, unit_of(m1, 4)) + unit_of(n2, 1)
+    home = unit_of(held, 0) + unit_of(m1, 0) + unit_of(m2, 0) + unit_of(n1, 0) + unit_of(n2, 0)
+    h1 = passed_along(h1.astype(F16), 5, -4)
+    h2 = passed_along(h2.astype(F16), -4, 5)
+    grad_that = home + h1.astype(F32) + h2.astype(F32)
 
     tunit, tnorm = unit_rows(text)
-    offset = lax.axis_index("depth") * n
-    own_unit, own_norm = unit_rows(lax.dynamic_slice_in_dim(video, offset, n, 0))
+    own_unit, own_norm = unit_rows(lax.dynamic_slice_in_dim(video, depth * n, n, 0))
     grad_video = (
         grad_vhat - own_unit * jnp.sum(own_unit * grad_vhat, axis=-1, keepdims=True)
     ) / own_norm

time: 158 us -> 161 us (1.019)
  the two profiles are of different devices: /device:TPU:1 before, /device:TPU:2 now
where the time goes in v4:
time: 161 us; the launch traced here: 160 us
  starting transfers between devices  94.2 us (59%)
  waiting for transfers between devices  25.6 us (16%)
  other arithmetic  19.1 us (12%)
  between operations  6.82 us (4%)
  matrix products  6.28 us (4%)
  Pallas kernels  4.82 us (3%)
  local copies, waits for them, and re-layouts  2.77 us (2%)
    ppermute x12, starting transfers between devices, passed_along(): return lax.ppermute(value, ('blk', 'depth'), pairs)  70.7 us
    all_to_all x1, starting transfers between devices, shards(): totals = lax.all_to_all(total, 'blk', 0, 0, tiled=True)  10.9 us
    all_to_all x1, waiting for transfers between devices, shards(): totals = lax.all_to_all(total, 'blk', 0, 0, tiled=True)  10.6 us
    ppermute x12, waiting for transfers between devices, passed_along(): return lax.ppermute(value, ('blk', 'depth'), pairs)  7.99 us
    all_to_all x1, starting transfers between devices, shards(): lax.all_to_all(share, 'depth', 0, 0, axis_index_groups=groups, tiled=True)  7.12 us
    all_to_all x1, waiting for transfers between devices, shards(): lax.all_to_all(share, 'depth', 0, 0, axis_index_groups=groups, tiled=True)  6.95 us
    ppermute x2, starting transfers between devices, core_swapped(): return lax.ppermute(value, 'depth', [(d, d ^ 1) for d in range(ndepth)])  5.54 us
    dot_general x3, matrix products, video_grad(): return jnp.einsum('cr,cd->rd', coef, texts, preferred_element_type=F32)  3.52 us
  transfers between devices with their start and end apart: 16, of which 4 were waited for; matrix products, arithmetic and copies ran while one was open for 14% of the time, Pallas kernels for 1%

profile of v4, /device:TPU:2, one launch (start us, length us, event | category | flops | bytes accessed | tf_op | source)
XLA Modules:
  0.0 159.6 jit_solution(17426457524869739242)
XLA Ops:
  2.3 9.1 %collective-permute-start.2 = (bf16[32,1280]{1,0:T(8,128)(2,1)}, bf16[32,1280]{1,0:T(8,128)(2,1)S(1)}, u32[]{:S(2)}, u32[]{:S(2)}) collective-permute-start(bf16[32,1280]{1,0:T(8,128)(2,1)} %shard_map.85), channel_id=1, source_target_pairs={{0,64},{1,945},{2,66},{3,947},{4,68},{5,949},{6,70},{7,951},{8,72}... | collective-permute-start | bytes 245768 | tf_op jit(solution)/shard_map/ppermute | solution.py:23
  11.4 17.9 %collective-permute-start = (bf16[32,1280]{1,0:T(8,128)(2,1)}, bf16[32,1280]{1,0:T(8,128)(2,1)S(1)}, u32[]{:S(2)}, u32[]{:S(2)}) collective-permute-start(bf16[32,1280]{1,0:T(8,128)(2,1)} %shard_map.85), channel_id=1, source_target_pairs={{0,944},{1,65},{2,946},{3,67},{4,948},{5,69},{6,950},{7,71},{8,952... | collective-permute-start | bytes 245768 | tf_op jit(solution)/shard_map/ppermute | solution.py:23
  35.6 1.9 %fusion.refs_2_ = bf16[512,1152]{1,0:T(8,128)(2,1)S(1)} fusion(f32[2,8,32,1152]{3,2,1,0:T(8,128)} %maximum_convert_fusion, f32[512]{0:T(512)S(1)} %sqrt.28), kind=kLoop, calls=%fused_computation.3 | loop fusion | flops 1179648 | bytes 3540992 | tf_op jit(solution)/shard_map/convert_element_type | solution.py:125
  37.7 1.9 %collective-permute-start.4 = (bf16[64,1280]{1,0:T(8,128)(2,1)S(1)}, bf16[64,1280]{1,0:T(8,128)(2,1)S(1)}, u32[]{:S(2)}, u32[]{:S(2)}) collective-permute-start(bf16[64,1280]{1,0:T(8,128)(2,1)S(1)} %get-tuple-element.39), channel_id=1, source_target_pairs={{0,32},{1,993},{2,34},{3,995},{4,36},{5,997},{6,38},{7,999},{8,40}... | collective-permute-start | bytes 491528 | tf_op jit(solution)/shard_map/ppermute | solution.py:23
  39.6 6.9 %collective-permute-start.1 = (bf16[64,1280]{1,0:T(8,128)(2,1)S(1)}, bf16[64,1280]{1,0:T(8,128)(2,1)S(1)}, u32[]{:S(2)}, u32[]{:S(2)}) collective-permute-start(bf16[64,1280]{1,0:T(8,128)(2,1)S(1)} %get-tuple-element.40), channel_id=1, source_target_pairs={{0,992},{1,33},{2,994},{3,35},{4,996},{5,37},{6,998},{7,39},{8,100... | collective-permute-start | bytes 491528 | tf_op jit(solution)/shard_map/ppermute | solution.py:23
  48.0 3.9 %collective-permute-done.4 = bf16[64,1280]{1,0:T(8,128)(2,1)S(1)} collective-permute-done((bf16[64,1280]{1,0:T(8,128)(2,1)S(1)}, bf16[64,1280]{1,0:T(8,128)(2,1)S(1)}, u32[]{:S(2)}, u32[]{:S(2)}) %collective-permute-start.4) | collective-permute-done | bytes 163872 | tf_op jit(solution)/shard_map/ppermute | solution.py:23
  52.0 1.9 %collective-permute-start.5 = (bf16[160,1280]{1,0:T(8,128)(2,1)S(1)}, bf16[160,1280]{1,0:T(8,128)(2,1)S(1)}, u32[]{:S(2)}, u32[]{:S(2)}) collective-permute-start(bf16[160,1280]{1,0:T(8,128)(2,1)S(1)} %get-tuple-element.37), channel_id=1, source_target_pairs={{0,16},{1,1009},{2,18},{3,1011},{4,20},{5,1013},{6,22},{7,1015},{8... | collective-permute-start | bytes 1228808 | tf_op jit(solution)/shard_map/ppermute | solution.py:23
  53.9 6.0 %collective-permute-start.3 = (bf16[160,1280]{1,0:T(8,128)(2,1)S(1)}, bf16[160,1280]{1,0:T(8,128)(2,1)S(1)}, u32[]{:S(2)}, u32[]{:S(2)}) collective-permute-start(bf16[160,1280]{1,0:T(8,128)(2,1)S(1)} %get-tuple-element.38), channel_id=1, source_target_pairs={{0,1008},{1,17},{2,1010},{3,19},{4,1012},{5,21},{6,1014},{7,23},{8... | collective-permute-start | bytes 1228808 | tf_op jit(solution)/shard_map/ppermute | solution.py:23
  62.6 4.1 %collective-permute-done.5 = bf16[160,1280]{1,0:T(8,128)(2,1)S(1)} collective-permute-done((bf16[160,1280]{1,0:T(8,128)(2,1)S(1)}, bf16[160,1280]{1,0:T(8,128)(2,1)S(1)}, u32[]{:S(2)}, u32[]{:S(2)}) %collective-permute-start.5) | collective-permute-done | bytes 409632 | tf_op jit(solution)/shard_map/ppermute | solution.py:23
  66.9 1.7 %shard_map.87 = (bf16[288,512]{1,0:T(8,128)(2,1)S(1)}, f32[64,128]{1,0:T(8,128)S(1)}) custom-call(f32[3]{0:T(128)S(1)} %pad_maximum_fusion.7.refs_0_, bf16[288,1280]{1,0:T(8,128)(2,1)S(1)} %pad_maximum_fusion.refs_1_, bf16[512,1152]{1,0:T(8,128)(2,1)S(1)} %fusion.refs_2_, f32[1,512]{1,0:T(1,128)S(1)} %convert_element_type.129.refs_3_, ...), custom_call_target="tpu_custom_call" | custom-call | flops 339738624 | bytes 1843200 | tf_op jit(solution)/shard_map/pallas_call | solution.py:62
  69.7 5.2 %collective-permute-start.9 = (f16[160,1152]{1,0:T(8,128)(2,1)}, f16[160,1152]{1,0:T(8,128)(2,1)}, u32[]{:S(2)}, u32[]{:S(2)}) collective-permute-start(f16[160,1152]{1,0:T(8,128)(2,1)} %convolution_convert_fusion), channel_id=1, source_target_pairs={{0,1008},{1,17},{2,1010},{3,19},{4,1012},{5,21},{6,1014},{7,23},{8... | collective-permute-start | bytes 1105928 | tf_op jit(solution)/shard_map/ppermute | solution.py:23
  76.0 1.9 %collective-permute-start.8 = (f16[160,1152]{1,0:T(8,128)(2,1)}, f16[160,1152]{1,0:T(8,128)(2,1)S(1)}, u32[]{:S(2)}, u32[]{:S(2)}) collective-permute-start(f16[160,1152]{1,0:T(8,128)(2,1)} %convolution_convert_fusion.1), channel_id=1, source_target_pairs={{0,16},{1,1009},{2,18},{3,1011},{4,20},{5,1013},{6,22},{7,1015},{8... | collective-permute-start | bytes 1105928 | tf_op jit(solution)/shard_map/ppermute | solution.py:23
  77.9 3.6 %collective-permute-start.7 = (f32[64,128]{1,0:T(8,128)S(1)}, f32[64,128]{1,0:T(8,128)S(1)}, u32[]{:S(2)}, u32[]{:S(2)}) collective-permute-start(f32[64,128]{1,0:T(8,128)S(1)} %get-tuple-element.20), channel_id=1, source_target_pairs={{0,1},{1,0},{2,3},{3,2},{4,5},{5,4},{6,7},{7,6},{8,9},{9,8},{10,11... | collective-permute-start | bytes 98312 | tf_op jit(solution)/shard_map/ppermute | solution.py:28
  82.9 1.9 %collective-permute-start.6 = (f16[256,1280]{1,0:T(8,128)(2,1)}, f16[256,1280]{1,0:T(8,128)(2,1)}, u32[]{:S(2)}, u32[]{:S(2)}) collective-permute-start(f16[256,1280]{1,0:T(8,128)(2,1)} %add_convert_fusion.1), channel_id=1, source_target_pairs={{0,1},{1,0},{2,3},{3,2},{4,5},{5,4},{6,7},{7,6},{8,9},{9,8},{10,11... | collective-permute-start | bytes 1966088 | tf_op jit(solution)/shard_map/ppermute | solution.py:28
  85.5 10.9 %all-to-all-start = ((f32[64,1,128]{2,1,0:T(1,128)}), f32[64,1,128]{2,1,0:T(1,128)S(1)}, u32[]{:S(2)}, u32[]{:S(2)}) async-start(f32[64,1,128]{2,1,0:T(1,128)} %bitcast.10), calls=%async_computation | async-start | bytes 65536 | tf_op jit(solution)/shard_map/all_to_all | solution.py:152
  98.3 4.4 %collective-permute-start.10 = (f16[64,1152]{1,0:T(8,128)(2,1)}, f16[64,1152]{1,0:T(8,128)(2,1)S(1)}, u32[]{:S(2)}, u32[]{:S(2)}) collective-permute-start(f16[64,1152]{1,0:T(8,128)(2,1)} %pad_maximum_fusion.5), channel_id=1, source_target_pairs={{0,32},{1,993},{2,34},{3,995},{4,36},{5,997},{6,38},{7,999},{8,40}... | collective-permute-start | bytes 442376 | tf_op jit(solution)/shard_map/ppermute | solution.py:23
  103.4 4.7 %collective-permute-start.11 = (f16[64,1152]{1,0:T(8,128)(2,1)}, f16[64,1152]{1,0:T(8,128)(2,1)}, u32[]{:S(2)}, u32[]{:S(2)}) collective-permute-start(f16[64,1152]{1,0:T(8,128)(2,1)} %pad_maximum_fusion.6), channel_id=1, source_target_pairs={{0,992},{1,33},{2,994},{3,35},{4,996},{5,37},{6,998},{7,39},{8,100... | collective-permute-start | bytes 442376 | tf_op jit(solution)/shard_map/ppermute | solution.py:23
  109.8 10.6 %all-to-all-done = f32[64,1,128]{2,1,0:T(1,128)S(1)} async-done(((f32[64,1,128]{2,1,0:T(1,128)}), f32[64,1,128]{2,1,0:T(1,128)S(1)}, u32[]{:S(2)}, u32[]{:S(2)}) %all-to-all-start) | async-done | bytes 32800 | tf_op jit(solution)/shard_map/all_to_all | solution.py:152
  123.6 2.9 %collective-permute-start.12 = (f16[32,1152]{1,0:T(8,128)(2,1)S(1)}, f16[32,1152]{1,0:T(8,128)(2,1)S(1)}, u32[]{:S(2)}, u32[]{:S(2)}) collective-permute-start(f16[32,1152]{1,0:T(8,128)(2,1)S(1)} %get-tuple-element.27), channel_id=1, source_target_pairs={{0,80},{1,961},{2,82},{3,963},{4,84},{5,965},{6,86},{7,967},{8,88}... | collective-permute-start | bytes 221192 | tf_op jit(solution)/shard_map/ppermute | solution.py:23
  126.5 7.9 %collective-permute-start.13 = (f16[32,1152]{1,0:T(8,128)(2,1)S(1)}, f16[32,1152]{1,0:T(8,128)(2,1)S(1)}, u32[]{:S(2)}, u32[]{:S(2)}) collective-permute-start(f16[32,1152]{1,0:T(8,128)(2,1)S(1)} %get-tuple-element.28), channel_id=1, source_target_pairs={{0,960},{1,81},{2,962},{3,83},{4,964},{5,85},{6,966},{7,87},{8,968... | collective-permute-start | bytes 221192 | tf_op jit(solution)/shard_map/ppermute | solution.py:23
  134.4 1.7 %add_convert_fusion = f16[256,1280]{1,0:T(8,128)(2,1)S(1)} fusion(f16[256,1280]{1,0:T(8,128)(2,1)} %collective-permute-done.6, f32[256,1280]{1,0:T(8,128)} %fusion.15, f32[512,1280]{1,0:T(8,128)S(1)} %copy-done.1), kind=kLoop, calls=%fused_computation.5 | loop fusion | flops 1310720 | bytes 3932160 | tf_op jit(solution)/shard_map/convert_element_type | solution.py:162
  137.0 7.1 %all-to-all-start.1 = ((f16[8,32,1280]{2,1,0:T(8,128)(2,1)}), f16[8,32,1280]{2,1,0:T(8,128)(2,1)S(1)}, u32[]{:S(2)}, u32[]{:S(2)}) async-start(f16[8,32,1280]{2,1,0:T(8,128)(2,1)} %bitcast.41), calls=%async_computation.1 | async-start | bytes 1310720 | tf_op jit(solution)/shard_map/all_to_all | solution.py:184
  146.2 6.9 %all-to-all-done.1 = f16[8,32,1280]{2,1,0:T(8,128)(2,1)S(1)} async-done(((f16[8,32,1280]{2,1,0:T(8,128)(2,1)}), f16[8,32,1280]{2,1,0:T(8,128)(2,1)S(1)}, u32[]{:S(2)}, u32[]{:S(2)}) %all-to-all-start.1) | async-done | bytes 655392 | tf_op jit(solution)/shard_map/all_to_all | solution.py:184
  154.3 1.6 %subtract_divide_fusion.1 = f32[32,1152]{1,0:T(8,128)} fusion(f32[32,1152]{1,0:T(8,128)S(1)} %convert_reduce_fusion, f32[32]{0:T(128)S(1)} %multiply_reduce_fusion.2, f32[32]{0:T(128)S(1)} %add_sqrt_fusion.2, bf16[512,1152]{1,0:T(8,128)(2,1)} %param.6, s32[]{:T(128)S(6)} %select_n.120), kind=kLoop, calls=%fused_computation.39 | loop fusion | flops 184320 | bytes 368900 | tf_op jit(solution)/shard_map/div | solution.py:199
  (84 shorter events, 26.0 us)
Async XLA Ops:
  2.3 35.3 %collective-permute-start.2 = (bf16[32,1280]{1,0:T(8,128)(2,1)}, bf16[32,1280]{1,0:T(8,128)(2,1)S(1)}, u32[]{:S(2)}, u32[]{:S(2)}) collective-permute-start(bf16[32,1280]{1,0:T(8,128)(2,1)} %shard_map.85), channel_id=1, source_target_pairs={{0,64},{1,945},{2,66},{3,947},{4,68},{5,949},{6,70},{7,951},{8,72}... | collective-permute-start | bytes 245768 | tf_op jit(solution)/shard_map/ppermute | solution.py:23
  11.4 26.3 %collective-permute-start = (bf16[32,1280]{1,0:T(8,128)(2,1)}, bf16[32,1280]{1,0:T(8,128)(2,1)S(1)}, u32[]{:S(2)}, u32[]{:S(2)}) collective-permute-start(bf16[32,1280]{1,0:T(8,128)(2,1)} %shard_map.85), channel_id=1, source_target_pairs={{0,944},{1,65},{2,946},{3,67},{4,948},{5,69},{6,950},{7,71},{8,952... | collective-permute-start | bytes 245768 | tf_op jit(solution)/shard_map/ppermute | solution.py:23
  32.8 2.6 %copy-start.9 = (s32[512]{0:T(512)S(1)}, s32[512]{0:T(512)}, u32[]{:S(2)}) copy-start(s32[512]{0:T(512)} %param.8) | copy-start | bytes 6148
  37.7 14.2 %collective-permute-start.4 = (bf16[64,1280]{1,0:T(8,128)(2,1)S(1)}, bf16[64,1280]{1,0:T(8,128)(2,1)S(1)}, u32[]{:S(2)}, u32[]{:S(2)}) collective-permute-start(bf16[64,1280]{1,0:T(8,128)(2,1)S(1)} %get-tuple-element.39), channel_id=1, source_target_pairs={{0,32},{1,993},{2,34},{3,995},{4,36},{5,997},{6,38},{7,999},{8,40}... | collective-permute-start | bytes 491528 | tf_op jit(solution)/shard_map/ppermute | solution.py:23
  39.6 12.3 %collective-permute-start.1 = (bf16[64,1280]{1,0:T(8,128)(2,1)S(1)}, bf16[64,1280]{1,0:T(8,128)(2,1)S(1)}, u32[]{:S(2)}, u32[]{:S(2)}) collective-permute-start(bf16[64,1280]{1,0:T(8,128)(2,1)S(1)} %get-tuple-element.40), channel_id=1, source_target_pairs={{0,992},{1,33},{2,994},{3,35},{4,996},{5,37},{6,998},{7,39},{8,100... | collective-permute-start | bytes 491528 | tf_op jit(solution)/shard_map/ppermute | solution.py:23
  52.0 14.7 %collective-permute-start.5 = (bf16[160,1280]{1,0:T(8,128)(2,1)S(1)}, bf16[160,1280]{1,0:T(8,128)(2,1)S(1)}, u32[]{:S(2)}, u32[]{:S(2)}) collective-permute-start(bf16[160,1280]{1,0:T(8,128)(2,1)S(1)} %get-tuple-element.37), channel_id=1, source_target_pairs={{0,16},{1,1009},{2,18},{3,1011},{4,20},{5,1013},{6,22},{7,1015},{8... | collective-permute-start | bytes 1228808 | tf_op jit(solution)/shard_map/ppermute | solution.py:23
  53.9 12.8 %collective-permute-start.3 = (bf16[160,1280]{1,0:T(8,128)(2,1)S(1)}, bf16[160,1280]{1,0:T(8,128)(2,1)S(1)}, u32[]{:S(2)}, u32[]{:S(2)}) collective-permute-start(bf16[160,1280]{1,0:T(8,128)(2,1)S(1)} %get-tuple-element.38), channel_id=1, source_target_pairs={{0,1008},{1,17},{2,1010},{3,19},{4,1012},{5,21},{6,1014},{7,23},{8... | collective-permute-start | bytes 1228808 | tf_op jit(solution)/shard_map/ppermute | solution.py:23
  62.0 34.4 %copy-start.2 = (f32[224,1152]{1,0:T(8,128)}, f32[224,1152]{1,0:T(8,128)S(1)}, u32[]{:S(2)}) copy-start(f32[224,1152]{1,0:T(8,128)S(1)} %fusion.22) | copy-start | bytes 3096580
  62.6 18.9 %copy-start = (f32[512,1280]{1,0:T(8,128)}, f32[512,1280]{1,0:T(8,128)S(1)}, u32[]{:S(2)}) copy-start(f32[512,1280]{1,0:T(8,128)S(1)} %fusion.21) | copy-start | bytes 7864324
  66.8 14.8 %copy-start.4 = (bf16[128,1280]{1,0:T(8,128)(2,1)}, bf16[128,1280]{1,0:T(8,128)(2,1)S(1)}, u32[]{:S(2)}) copy-start(bf16[128,1280]{1,0:T(8,128)(2,1)S(1)} %slice.135) | copy-start | bytes 983044
  69.7 26.7 %collective-permute-start.9 = (f16[160,1152]{1,0:T(8,128)(2,1)}, f16[160,1152]{1,0:T(8,128)(2,1)}, u32[]{:S(2)}, u32[]{:S(2)}) collective-permute-start(f16[160,1152]{1,0:T(8,128)(2,1)} %convolution_convert_fusion), channel_id=1, source_target_pairs={{0,1008},{1,17},{2,1010},{3,19},{4,1012},{5,21},{6,1014},{7,23},{8... | collective-permute-start | bytes 1105928 | tf_op jit(solution)/shard_map/ppermute | solution.py:23
  76.0 20.5 %collective-permute-start.8 = (f16[160,1152]{1,0:T(8,128)(2,1)}, f16[160,1152]{1,0:T(8,128)(2,1)S(1)}, u32[]{:S(2)}, u32[]{:S(2)}) collective-permute-start(f16[160,1152]{1,0:T(8,128)(2,1)} %convolution_convert_fusion.1), channel_id=1, source_target_pairs={{0,16},{1,1009},{2,18},{3,1011},{4,20},{5,1013},{6,22},{7,1015},{8... | collective-permute-start | bytes 1105928 | tf_op jit(solution)/shard_map/ppermute | solution.py:23
  77.9 7.0 %collective-permute-start.7 = (f32[64,128]{1,0:T(8,128)S(1)}, f32[64,128]{1,0:T(8,128)S(1)}, u32[]{:S(2)}, u32[]{:S(2)}) collective-permute-start(f32[64,128]{1,0:T(8,128)S(1)} %get-tuple-element.20), channel_id=1, source_target_pairs={{0,1},{1,0},{2,3},{3,2},{4,5},{5,4},{6,7},{7,6},{8,9},{9,8},{10,11... | collective-permute-start | bytes 98312 | tf_op jit(solution)/shard_map/ppermute | solution.py:28
  82.9 51.5 %collective-permute-start.6 = (f16[256,1280]{1,0:T(8,128)(2,1)}, f16[256,1280]{1,0:T(8,128)(2,1)}, u32[]{:S(2)}, u32[]{:S(2)}) collective-permute-start(f16[256,1280]{1,0:T(8,128)(2,1)} %add_convert_fusion.1), channel_id=1, source_target_pairs={{0,1},{1,0},{2,3},{3,2},{4,5},{5,4},{6,7},{7,6},{8,9},{9,8},{10,11... | collective-permute-start | bytes 1966088 | tf_op jit(solution)/shard_map/ppermute | solution.py:28
  85.5 34.9 %all-to-all-start = ((f32[64,1,128]{2,1,0:T(1,128)}), f32[64,1,128]{2,1,0:T(1,128)S(1)}, u32[]{:S(2)}, u32[]{:S(2)}) async-start(f32[64,1,128]{2,1,0:T(1,128)} %bitcast.10), calls=%async_computation | async-start | bytes 65536 | tf_op jit(solution)/shard_map/all_to_all | solution.py:152
  96.4 11.7 %copy-start.5 = (bf16[128,1280]{1,0:T(8,128)(2,1)S(1)}, bf16[128,1280]{1,0:T(8,128)(2,1)}, u32[]{:S(2)}) copy-start(bf16[128,1280]{1,0:T(8,128)(2,1)} %copy-done.4) | copy-start | bytes 983044
  96.5 6.2 %copy-start.8 = (f16[160,1152]{1,0:T(8,128)(2,1)}, f16[160,1152]{1,0:T(8,128)(2,1)S(1)}, u32[]{:S(2)}) copy-start(f16[160,1152]{1,0:T(8,128)(2,1)S(1)} %collective-permute-done.8) | copy-start | bytes 1105924
  98.3 22.1 %collective-permute-start.10 = (f16[64,1152]{1,0:T(8,128)(2,1)}, f16[64,1152]{1,0:T(8,128)(2,1)S(1)}, u32[]{:S(2)}, u32[]{:S(2)}) collective-permute-start(f16[64,1152]{1,0:T(8,128)(2,1)} %pad_maximum_fusion.5), channel_id=1, source_target_pairs={{0,32},{1,993},{2,34},{3,995},{4,36},{5,997},{6,38},{7,999},{8,40}... | collective-permute-start | bytes 442376 | tf_op jit(solution)/shard_map/ppermute | solution.py:23
  103.4 31.0 %copy-start.1 = (f32[512,1280]{1,0:T(8,128)S(1)}, f32[512,1280]{1,0:T(8,128)}, u32[]{:S(2)}) copy-start(f32[512,1280]{1,0:T(8,128)} %copy-done) | copy-start | bytes 7864324
  103.4 17.0 %collective-permute-start.11 = (f16[64,1152]{1,0:T(8,128)(2,1)}, f16[64,1152]{1,0:T(8,128)(2,1)}, u32[]{:S(2)}, u32[]{:S(2)}) collective-permute-start(f16[64,1152]{1,0:T(8,128)(2,1)} %pad_maximum_fusion.6), channel_id=1, source_target_pairs={{0,992},{1,33},{2,994},{3,35},{4,996},{5,37},{6,998},{7,39},{8,100... | collective-permute-start | bytes 442376 | tf_op jit(solution)/shard_map/ppermute | solution.py:23
  123.6 20.5 %collective-permute-start.12 = (f16[32,1152]{1,0:T(8,128)(2,1)S(1)}, f16[32,1152]{1,0:T(8,128)(2,1)S(1)}, u32[]{:S(2)}, u32[]{:S(2)}) collective-permute-start(f16[32,1152]{1,0:T(8,128)(2,1)S(1)} %get-tuple-element.27), channel_id=1, source_target_pairs={{0,80},{1,961},{2,82},{3,963},{4,84},{5,965},{6,86},{7,967},{8,88}... | collective-permute-start | bytes 221192 | tf_op jit(solution)/shard_map/ppermute | solution.py:23
  126.5 17.7 %collective-permute-start.13 = (f16[32,1152]{1,0:T(8,128)(2,1)S(1)}, f16[32,1152]{1,0:T(8,128)(2,1)S(1)}, u32[]{:S(2)}, u32[]{:S(2)}) collective-permute-start(f16[32,1152]{1,0:T(8,128)(2,1)S(1)} %get-tuple-element.28), channel_id=1, source_target_pairs={{0,960},{1,81},{2,962},{3,83},{4,964},{5,85},{6,966},{7,87},{8,968... | collective-permute-start | bytes 221192 | tf_op jit(solution)/shard_map/ppermute | solution.py:23
  136.2 8.0 %copy-start.7 = (bf16[32,1152]{1,0:T(8,128)(2,1)S(1)}, bf16[32,1152]{1,0:T(8,128)(2,1)}, u32[]{:S(2)}) copy-start(bf16[32,1152]{1,0:T(8,128)(2,1)} %refs_0_.1) | copy-start | bytes 221188
  137.0 16.1 %all-to-all-start.1 = ((f16[8,32,1280]{2,1,0:T(8,128)(2,1)}), f16[8,32,1280]{2,1,0:T(8,128)(2,1)S(1)}, u32[]{:S(2)}, u32[]{:S(2)}) async-start(f16[8,32,1280]{2,1,0:T(8,128)(2,1)} %bitcast.41), calls=%async_computation.1 | async-start | bytes 1310720 | tf_op jit(solution)/shard_map/all_to_all | solution.py:184
  (2 other events, 2.8 us)

commit v5 on v4

--- a/solution.py
+++ b/solution.py
@@ -115,15 +115,11 @@
     r1 = passed_along(own, -5, 4)
     r2 = passed_along(own, 4, -5)
 
-    def by_core(x):
-        x = x.reshape(ndepth // 2, 2, n, *x.shape[1:])
-        mine = jnp.where(core0, x[:, 0], x[:, 1])
-        other = jnp.where(core0, x[:, 1], x[:, 0])
-        return jnp.stack([mine, other]).reshape(rows, *x.shape[3:])
-
-    vunit, _ = unit_rows(by_core(video))
-    vhat = vunit.astype(BF16)
-    vids = by_core(video_ids).astype(F32)[None, :]
+    video32 = video.astype(F32)
+    vnorm = jnp.sqrt(jnp.sum(video32 * video32, axis=-1, keepdims=True) + EPS)
+    vnorm, r1 = lax.optimization_barrier((vnorm, r1))
+    vhat = (video32 / vnorm).astype(BF16)
+    vids = video_ids.astype(F32)[None, :]
     part = jnp.float32(1.0 / (rows * nblk * 2 * half))
     params = jnp.stack([jnp.exp(log_scale[0]), bias[0], part])
 
@@ -148,18 +144,13 @@
     arrived = jnp.concatenate([s1[: 4 * n], s2[: 4 * n], fifth], axis=0)
     coef1, total = pair_coefs(params, arrived, vhat, vids, total)
 
-    total = total + core_swapped(total)
     totals = lax.all_to_all(total, "blk", 0, 0, tiled=True)
 
     coef_s1 = jnp.concatenate([coef1[: 4 * n], coef1[8 * n :]], axis=0)
     m1 = passed_along(text_grad(coef_s1).astype(F16), 1, -1)
     m2 = passed_along(text_grad(coef1[4 * n :]).astype(F16), -1, 1)
-    m1, m2, _ = lax.optimization_barrier((m1, m2, total))
-
-    mid = rows // 2
-    sent = (share0[mid:] + video_grad(coef1[:, mid:], arrived)).astype(F16)
-    share = share0[:mid] + video_grad(coef1[:, :mid], arrived)
-    share = (share + core_swapped(sent).astype(F32)).astype(F16)
+
+    share = (share0 + video_grad(coef1, arrived)).astype(F16)
 
     def unit_of(value, i):
         return value[i * n : (i + 1) * n].astype(F32)
@@ -172,17 +163,16 @@
     n2 = passed_along(pair_of(4, m2), -2, 2)
 
     totals, _, _ = lax.optimization_barrier((totals, n1, n2))
-    total = jnp.sum(totals[:, 0])
+    total = jnp.sum(totals, axis=0, keepdims=True)
     first = total.astype(F16)
     rest = (total - first.astype(F32)) * 2.0**11
     second = rest.astype(F16)
     third = ((rest - second.astype(F32)) * 2.0**11).astype(F16)
-    lane = lax.broadcasted_iota(jnp.int32, (mid, LANES), 1)
+    lane = lax.broadcasted_iota(jnp.int32, (1, LANES), 1)
     digits = jnp.where(lane == 0, first, jnp.where(lane == 1, second, third))
+    digits = jnp.broadcast_to(digits, (rows, LANES))
     share = lax.dynamic_update_slice(share, digits, (0, width))
-    groups = [list(range(core, ndepth, 2)) for core in range(2)]
-    shares = lax.all_to_all(share, "depth", 0, 0, axis_index_groups=groups, tiled=True)
-    shares = shares.reshape(ndepth // 2, n, width + LANES)
+    shares = lax.all_to_all(share, "depth", 0, 0, tiled=True).reshape(ndepth, n, width + LANES)
     grad_vhat = jnp.sum(shares[:, :, :width].astype(F32), axis=0)
     digits = jnp.sum(shares[:, 0, width : width + 3].astype(F32), axis=0)
     loss = digits[0] + digits[1] * 2.0**-11 + digits[2] * 2.0**-22

time: 161 us -> 152 us (0.944)
  the two profiles are of different devices: /device:TPU:2 before, /device:TPU:1 now
where the time goes in v5:
time: 152 us; the launch traced here: 151 us
  starting transfers between devices  90 us (59%)
  waiting for transfers between devices  28.1 us (18%)
  other arithmetic  12.9 us (8%)
  matrix products  6.17 us (4%)
  Pallas kernels  5.53 us (4%)
  between operations  5.35 us (4%)
  local copies, waits for them, and re-layouts  3.02 us (2%)
    ppermute x12, starting transfers between devices, passed_along(): return lax.ppermute(value, ('blk', 'depth'), pairs)  70.6 us
    ppermute x12, waiting for transfers between devices, passed_along(): return lax.ppermute(value, ('blk', 'depth'), pairs)  18.8 us
    all_to_all x1, starting transfers between devices, shards(): lax.all_to_all(share, 'depth', 0, 0, tiled=True)  10.4 us
    all_to_all x1, waiting for transfers between devices, shards(): totals = lax.all_to_all(total, 'blk', 0, 0, tiled=True)  9.29 us
    all_to_all x1, starting transfers between devices, shards(): totals = lax.all_to_all(total, 'blk', 0, 0, tiled=True)  9.07 us
    pallas_call x2, Pallas kernels, pair_coefs(): pl.pallas_call(lambda *refs: coef_kernel(width, *refs), out_shape=(jax.Sh...  3.8 us
    dot_general x3, matrix products, text_grad(): return jnp.einsum('cr,rd->cd', coef, vhat, preferred_element_type=F32)  3.71 us
  transfers between devices with their start and end apart: 14, of which 7 were waited for; matrix products, arithmetic and copies ran while one was open for 10% of the time, Pallas kernels for 1%

profile of v5, /device:TPU:1, one launch (start us, length us, event | category | flops | bytes accessed | tf_op | source)
XLA Modules:
  0.0 151.1 jit_solution(3024896222348137743)
XLA Ops:
  0.7 1.7 %shard_map.85 = bf16[32,1280]{1,0:T(8,128)(2,1)} custom-call(bf16[32,1152]{1,0:T(8,128)(2,1)} %refs_0_.1, s32[1,32]{1,0:T(1,128)} %bitcast.21), custom_call_target="tpu_custom_call" | custom-call | tf_op jit(solution)/shard_map/pallas_call | solution.py:97
  2.4 9.8 %collective-permute-start = (bf16[32,1280]{1,0:T(8,128)(2,1)}, bf16[32,1280]{1,0:T(8,128)(2,1)S(1)}, u32[]{:S(2)}, u32[]{:S(2)}) collective-permute-start(bf16[32,1280]{1,0:T(8,128)(2,1)} %shard_map.85), channel_id=1, source_target_pairs={{0,944},{1,65},{2,946},{3,67},{4,948},{5,69},{6,950},{7,71},{8,952... | collective-permute-start | bytes 245768 | tf_op jit(solution)/shard_map/ppermute | solution.py:23
  12.2 17.6 %collective-permute-start.2 = (bf16[32,1280]{1,0:T(8,128)(2,1)}, bf16[32,1280]{1,0:T(8,128)(2,1)S(1)}, u32[]{:S(2)}, u32[]{:S(2)}) collective-permute-start(bf16[32,1280]{1,0:T(8,128)(2,1)} %shard_map.85), channel_id=1, source_target_pairs={{0,64},{1,945},{2,66},{3,947},{4,68},{5,949},{6,70},{7,951},{8,72}... | collective-permute-start | bytes 245768 | tf_op jit(solution)/shard_map/ppermute | solution.py:23
  31.7 1.6 %fusion = f32[512]{0:T(512)S(1)} fusion(bf16[512,1152]{1,0:T(8,128)(2,1)} %param.6), kind=kLoop, calls=%fused_computation.5 | loop fusion | flops 1768960 | bytes 1181696 | tf_op jit(solution)/shard_map/reduce_sum | solution.py:119
  36.2 1.9 %collective-permute-start.1 = (bf16[64,1280]{1,0:T(8,128)(2,1)S(1)}, bf16[64,1280]{1,0:T(8,128)(2,1)S(1)}, u32[]{:S(2)}, u32[]{:S(2)}) collective-permute-start(bf16[64,1280]{1,0:T(8,128)(2,1)S(1)} %get-tuple-element.38), channel_id=1, source_target_pairs={{0,992},{1,33},{2,994},{3,35},{4,996},{5,37},{6,998},{7,39},{8,100... | collective-permute-start | bytes 491528 | tf_op jit(solution)/shard_map/ppermute | solution.py:23
  38.1 6.4 %collective-permute-start.4 = (bf16[64,1280]{1,0:T(8,128)(2,1)S(1)}, bf16[64,1280]{1,0:T(8,128)(2,1)S(1)}, u32[]{:S(2)}, u32[]{:S(2)}) collective-permute-start(bf16[64,1280]{1,0:T(8,128)(2,1)S(1)} %get-tuple-element.37), channel_id=1, source_target_pairs={{0,32},{1,993},{2,34},{3,995},{4,36},{5,997},{6,38},{7,999},{8,40}... | collective-permute-start | bytes 491528 | tf_op jit(solution)/shard_map/ppermute | solution.py:23
  45.3 3.1 %collective-permute-done.4 = bf16[64,1280]{1,0:T(8,128)(2,1)S(1)} collective-permute-done((bf16[64,1280]{1,0:T(8,128)(2,1)S(1)}, bf16[64,1280]{1,0:T(8,128)(2,1)S(1)}, u32[]{:S(2)}, u32[]{:S(2)}) %collective-permute-start.4) | collective-permute-done | bytes 163872 | tf_op jit(solution)/shard_map/ppermute | solution.py:23
  48.4 3.5 %collective-permute-start.3 = (bf16[160,1280]{1,0:T(8,128)(2,1)S(1)}, bf16[160,1280]{1,0:T(8,128)(2,1)S(1)}, u32[]{:S(2)}, u32[]{:S(2)}) collective-permute-start(bf16[160,1280]{1,0:T(8,128)(2,1)S(1)} %get-tuple-element.36), channel_id=1, source_target_pairs={{0,1008},{1,17},{2,1010},{3,19},{4,1012},{5,21},{6,1014},{7,23},{8... | collective-permute-start | bytes 1228808 | tf_op jit(solution)/shard_map/ppermute | solution.py:23
  51.9 5.9 %collective-permute-start.5 = (bf16[160,1280]{1,0:T(8,128)(2,1)S(1)}, bf16[160,1280]{1,0:T(8,128)(2,1)S(1)}, u32[]{:S(2)}, u32[]{:S(2)}) collective-permute-start(bf16[160,1280]{1,0:T(8,128)(2,1)S(1)} %get-tuple-element.35), channel_id=1, source_target_pairs={{0,16},{1,1009},{2,18},{3,1011},{4,20},{5,1013},{6,22},{7,1015},{8... | collective-permute-start | bytes 1228808 | tf_op jit(solution)/shard_map/ppermute | solution.py:23
  61.4 5.7 %collective-permute-done.5 = bf16[160,1280]{1,0:T(8,128)(2,1)S(1)} collective-permute-done((bf16[160,1280]{1,0:T(8,128)(2,1)S(1)}, bf16[160,1280]{1,0:T(8,128)(2,1)S(1)}, u32[]{:S(2)}, u32[]{:S(2)}) %collective-permute-start.5) | collective-permute-done | bytes 409632 | tf_op jit(solution)/shard_map/ppermute | solution.py:23
  67.9 2.3 %shard_map.87 = (bf16[288,512]{1,0:T(8,128)(2,1)S(1)}, f32[64,128]{1,0:T(8,128)}) custom-call(f32[3]{0:T(128)S(1)} %pad_maximum_fusion.7.refs_0_, bf16[288,1280]{1,0:T(8,128)(2,1)S(1)} %pad_maximum_fusion.refs_1_, bf16[512,1152]{1,0:T(8,128)(2,1)S(1)} %fusion.1.refs_2_, f32[1,512]{1,0:T(1,128)S(1)} %bitcast.18, f32[64,128]{1,0:T(8,128)S(1)} %get-tuple-element.20.refs_4_), custom_call_target="tpu_custom_call" | custom-call | flops 339738624 | bytes 1843200 | tf_op jit(solution)/shard_map/pallas_call | solution.py:62
  72.4 6.2 %collective-permute-start.6 = (f16[160,1152]{1,0:T(8,128)(2,1)}, f16[160,1152]{1,0:T(8,128)(2,1)}, u32[]{:S(2)}, u32[]{:S(2)}) collective-permute-start(f16[160,1152]{1,0:T(8,128)(2,1)} %convolution_convert_fusion.1), channel_id=1, source_target_pairs={{0,16},{1,1009},{2,18},{3,1011},{4,20},{5,1013},{6,22},{7,1015},{8... | collective-permute-start | bytes 1105928 | tf_op jit(solution)/shard_map/ppermute | solution.py:23
  78.6 1.9 %collective-permute-start.8 = (f16[160,1152]{1,0:T(8,128)(2,1)}, f16[160,1152]{1,0:T(8,128)(2,1)}, u32[]{:S(2)}, u32[]{:S(2)}) collective-permute-start(f16[160,1152]{1,0:T(8,128)(2,1)} %convolution_convert_fusion), channel_id=1, source_target_pairs={{0,1008},{1,17},{2,1010},{3,19},{4,1012},{5,21},{6,1014},{7,23},{8... | collective-permute-start | bytes 1105928 | tf_op jit(solution)/shard_map/ppermute | solution.py:23
  81.6 9.1 %all-to-all-start = ((f32[64,1,128]{2,1,0:T(1,128)}), f32[64,1,128]{2,1,0:T(1,128)S(1)}, u32[]{:S(2)}, u32[]{:S(2)}) async-start(f32[64,1,128]{2,1,0:T(1,128)} %bitcast.5), calls=%async_computation | async-start | bytes 65536 | tf_op jit(solution)/shard_map/all_to_all | solution.py:147
  90.7 1.9 %fusion.14 = f32[512,1280]{1,0:T(8,128)S(1)} fusion(bf16[288,512]{1,0:T(8,128)(2,1)S(1)} %get-tuple-element.21, bf16[32,1280]{1,0:T(8,128)(2,1)S(1)} %slice_select_fusion, bf16[128,1280]{1,0:T(8,128)(2,1)S(1)} %slice.100, bf16[128,1280]{1,0:T(8,128)(2,1)} %copy-done.2), kind=kOutput, calls=%fused_computation.56 | convolution fusion | flops 379699200 | bytes 3653632 | tf_op jit(solution)/shard_map/cr,cd->rd/dot_general | solution.py:135
  93.7 3.8 %collective-permute-start.9 = (f16[64,1152]{1,0:T(8,128)(2,1)S(1)}, f16[64,1152]{1,0:T(8,128)(2,1)S(1)}, u32[]{:S(2)}, u32[]{:S(2)}) collective-permute-start(f16[64,1152]{1,0:T(8,128)(2,1)S(1)} %pad_maximum_fusion.6), channel_id=1, source_target_pairs={{0,992},{1,33},{2,994},{3,35},{4,996},{5,37},{6,998},{7,39},{8,100... | collective-permute-start | bytes 442376 | tf_op jit(solution)/shard_map/ppermute | solution.py:23
  97.6 4.5 %collective-permute-start.7 = (f16[64,1152]{1,0:T(8,128)(2,1)S(1)}, f16[64,1152]{1,0:T(8,128)(2,1)S(1)}, u32[]{:S(2)}, u32[]{:S(2)}) collective-permute-start(f16[64,1152]{1,0:T(8,128)(2,1)S(1)} %pad_maximum_fusion.5), channel_id=1, source_target_pairs={{0,32},{1,993},{2,34},{3,995},{4,36},{5,997},{6,38},{7,999},{8,40}... | collective-permute-start | bytes 442376 | tf_op jit(solution)/shard_map/ppermute | solution.py:23
  103.5 9.3 %all-to-all-done = f32[64,1,128]{2,1,0:T(1,128)S(1)} async-done(((f32[64,1,128]{2,1,0:T(1,128)}), f32[64,1,128]{2,1,0:T(1,128)S(1)}, u32[]{:S(2)}, u32[]{:S(2)}) %all-to-all-start) | async-done | bytes 32800 | tf_op jit(solution)/shard_map/all_to_all | solution.py:147
  113.5 10.4 %all-to-all-start.1 = ((f16[16,32,1280]{2,1,0:T(8,128)(2,1)}), f16[16,32,1280]{2,1,0:T(8,128)(2,1)S(1)}, u32[]{:S(2)}, u32[]{:S(2)}) async-start(f16[16,32,1280]{2,1,0:T(8,128)(2,1)} %bitcast.19), calls=%async_computation.1 | async-start | bytes 2621440 | tf_op jit(solution)/shard_map/all_to_all | solution.py:175
  125.1 3.1 %collective-permute-start.10 = (f16[32,1152]{1,0:T(8,128)(2,1)S(1)}, f16[32,1152]{1,0:T(8,128)(2,1)S(1)}, u32[]{:S(2)}, u32[]{:S(2)}) collective-permute-start(f16[32,1152]{1,0:T(8,128)(2,1)S(1)} %get-tuple-element.27), channel_id=1, source_target_pairs={{0,80},{1,961},{2,82},{3,963},{4,84},{5,965},{6,86},{7,967},{8,88}... | collective-permute-start | bytes 221192 | tf_op jit(solution)/shard_map/ppermute | solution.py:23
  128.3 6.0 %collective-permute-start.11 = (f16[32,1152]{1,0:T(8,128)(2,1)S(1)}, f16[32,1152]{1,0:T(8,128)(2,1)S(1)}, u32[]{:S(2)}, u32[]{:S(2)}) collective-permute-start(f16[32,1152]{1,0:T(8,128)(2,1)S(1)} %get-tuple-element.28), channel_id=1, source_target_pairs={{0,960},{1,81},{2,962},{3,83},{4,964},{5,85},{6,966},{7,87},{8,968... | collective-permute-start | bytes 221192 | tf_op jit(solution)/shard_map/ppermute | solution.py:23
  134.3 2.5 %collective-permute-done.10 = f16[32,1152]{1,0:T(8,128)(2,1)S(1)} collective-permute-done((f16[32,1152]{1,0:T(8,128)(2,1)S(1)}, f16[32,1152]{1,0:T(8,128)(2,1)S(1)}, u32[]{:S(2)}, u32[]{:S(2)}) %collective-permute-start.10) | collective-permute-done | bytes 73760 | tf_op jit(solution)/shard_map/ppermute | solution.py:23
  136.8 5.8 %collective-permute-done.11 = f16[32,1152]{1,0:T(8,128)(2,1)S(1)} collective-permute-done((f16[32,1152]{1,0:T(8,128)(2,1)S(1)}, f16[32,1152]{1,0:T(8,128)(2,1)S(1)}, u32[]{:S(2)}, u32[]{:S(2)}) %collective-permute-start.11) | collective-permute-done | bytes 73760 | tf_op jit(solution)/shard_map/ppermute | solution.py:23
  145.8 1.6 %subtract_divide_fusion.1 = f32[32,1152]{1,0:T(8,128)} fusion(f32[32,1152]{1,0:T(8,128)S(1)} %convert_reduce_fusion, f32[32]{0:T(128)S(1)} %multiply_reduce_fusion.1, f32[32]{0:T(128)S(1)} %add_sqrt_fusion.2, bf16[512,1152]{1,0:T(8,128)(2,1)} %param.6, s32[]{:T(128)S(6)} %select_n.54), kind=kLoop, calls=%fused_computation.34 | loop fusion | flops 184320 | bytes 368900 | tf_op jit(solution)/shard_map/div | solution.py:189
  (62 shorter events, 20.3 us)
Async XLA Ops:
  0.6 43.8 %copy-start = (bf16[512,1152]{1,0:T(8,128)(2,1)S(1)}, bf16[512,1152]{1,0:T(8,128)(2,1)}, u32[]{:S(2)}) copy-start(bf16[512,1152]{1,0:T(8,128)(2,1)} %param.6) | copy-start | bytes 3538948
  0.6 32.6 %copy-start.5 = (s32[512]{0:T(512)S(1)}, s32[512]{0:T(512)}, u32[]{:S(2)}) copy-start(s32[512]{0:T(512)} %param.8) | copy-start | bytes 6148
  2.4 33.7 %copy-start.3 = (bf16[32,1280]{1,0:T(8,128)(2,1)S(1)}, bf16[32,1280]{1,0:T(8,128)(2,1)}, u32[]{:S(2)}) copy-start(bf16[32,1280]{1,0:T(8,128)(2,1)} %shard_map.85) | copy-start | bytes 245764
  2.4 32.3 %collective-permute-start = (bf16[32,1280]{1,0:T(8,128)(2,1)}, bf16[32,1280]{1,0:T(8,128)(2,1)S(1)}, u32[]{:S(2)}, u32[]{:S(2)}) collective-permute-start(bf16[32,1280]{1,0:T(8,128)(2,1)} %shard_map.85), channel_id=1, source_target_pairs={{0,944},{1,65},{2,946},{3,67},{4,948},{5,69},{6,950},{7,71},{8,952... | collective-permute-start | bytes 245768 | tf_op jit(solution)/shard_map/ppermute | solution.py:23
  12.2 24.0 %collective-permute-start.2 = (bf16[32,1280]{1,0:T(8,128)(2,1)}, bf16[32,1280]{1,0:T(8,128)(2,1)S(1)}, u32[]{:S(2)}, u32[]{:S(2)}) collective-permute-start(bf16[32,1280]{1,0:T(8,128)(2,1)} %shard_map.85), channel_id=1, source_target_pairs={{0,64},{1,945},{2,66},{3,947},{4,68},{5,949},{6,70},{7,951},{8,72}... | collective-permute-start | bytes 245768 | tf_op jit(solution)/shard_map/ppermute | solution.py:23
  36.2 9.1 %collective-permute-start.1 = (bf16[64,1280]{1,0:T(8,128)(2,1)S(1)}, bf16[64,1280]{1,0:T(8,128)(2,1)S(1)}, u32[]{:S(2)}, u32[]{:S(2)}) collective-permute-start(bf16[64,1280]{1,0:T(8,128)(2,1)S(1)} %get-tuple-element.38), channel_id=1, source_target_pairs={{0,992},{1,33},{2,994},{3,35},{4,996},{5,37},{6,998},{7,39},{8,100... | collective-permute-start | bytes 491528 | tf_op jit(solution)/shard_map/ppermute | solution.py:23
  38.1 10.3 %collective-permute-start.4 = (bf16[64,1280]{1,0:T(8,128)(2,1)S(1)}, bf16[64,1280]{1,0:T(8,128)(2,1)S(1)}, u32[]{:S(2)}, u32[]{:S(2)}) collective-permute-start(bf16[64,1280]{1,0:T(8,128)(2,1)S(1)} %get-tuple-element.37), channel_id=1, source_target_pairs={{0,32},{1,993},{2,34},{3,995},{4,36},{5,997},{6,38},{7,999},{8,40}... | collective-permute-start | bytes 491528 | tf_op jit(solution)/shard_map/ppermute | solution.py:23
  48.4 13.0 %collective-permute-start.3 = (bf16[160,1280]{1,0:T(8,128)(2,1)S(1)}, bf16[160,1280]{1,0:T(8,128)(2,1)S(1)}, u32[]{:S(2)}, u32[]{:S(2)}) collective-permute-start(bf16[160,1280]{1,0:T(8,128)(2,1)S(1)} %get-tuple-element.36), channel_id=1, source_target_pairs={{0,1008},{1,17},{2,1010},{3,19},{4,1012},{5,21},{6,1014},{7,23},{8... | collective-permute-start | bytes 1228808 | tf_op jit(solution)/shard_map/ppermute | solution.py:23
  51.9 15.2 %collective-permute-start.5 = (bf16[160,1280]{1,0:T(8,128)(2,1)S(1)}, bf16[160,1280]{1,0:T(8,128)(2,1)S(1)}, u32[]{:S(2)}, u32[]{:S(2)}) collective-permute-start(bf16[160,1280]{1,0:T(8,128)(2,1)S(1)} %get-tuple-element.35), channel_id=1, source_target_pairs={{0,16},{1,1009},{2,18},{3,1011},{4,20},{5,1013},{6,22},{7,1015},{8... | collective-permute-start | bytes 1228808 | tf_op jit(solution)/shard_map/ppermute | solution.py:23
  67.1 0.7 copy-start.2
  72.4 20.2 %collective-permute-start.6 = (f16[160,1152]{1,0:T(8,128)(2,1)}, f16[160,1152]{1,0:T(8,128)(2,1)}, u32[]{:S(2)}, u32[]{:S(2)}) collective-permute-start(f16[160,1152]{1,0:T(8,128)(2,1)} %convolution_convert_fusion.1), channel_id=1, source_target_pairs={{0,16},{1,1009},{2,18},{3,1011},{4,20},{5,1013},{6,22},{7,1015},{8... | collective-permute-start | bytes 1105928 | tf_op jit(solution)/shard_map/ppermute | solution.py:23
  78.6 14.0 %collective-permute-start.8 = (f16[160,1152]{1,0:T(8,128)(2,1)}, f16[160,1152]{1,0:T(8,128)(2,1)}, u32[]{:S(2)}, u32[]{:S(2)}) collective-permute-start(f16[160,1152]{1,0:T(8,128)(2,1)} %convolution_convert_fusion), channel_id=1, source_target_pairs={{0,1008},{1,17},{2,1010},{3,19},{4,1012},{5,21},{6,1014},{7,23},{8... | collective-permute-start | bytes 1105928 | tf_op jit(solution)/shard_map/ppermute | solution.py:23
  81.6 31.2 %all-to-all-start = ((f32[64,1,128]{2,1,0:T(1,128)}), f32[64,1,128]{2,1,0:T(1,128)S(1)}, u32[]{:S(2)}, u32[]{:S(2)}) async-start(f32[64,1,128]{2,1,0:T(1,128)} %bitcast.5), calls=%async_computation | async-start | bytes 65536 | tf_op jit(solution)/shard_map/all_to_all | solution.py:147
  90.6 2.0 %copy-start.1 = (f32[224,1152]{1,0:T(8,128)S(1)}, f32[224,1152]{1,0:T(8,128)}, u32[]{:S(2)}) copy-start(f32[224,1152]{1,0:T(8,128)} %fusion.17) | copy-start | bytes 3096580
  93.7 19.1 %collective-permute-start.9 = (f16[64,1152]{1,0:T(8,128)(2,1)S(1)}, f16[64,1152]{1,0:T(8,128)(2,1)S(1)}, u32[]{:S(2)}, u32[]{:S(2)}) collective-permute-start(f16[64,1152]{1,0:T(8,128)(2,1)S(1)} %pad_maximum_fusion.6), channel_id=1, source_target_pairs={{0,992},{1,33},{2,994},{3,35},{4,996},{5,37},{6,998},{7,39},{8,100... | collective-permute-start | bytes 442376 | tf_op jit(solution)/shard_map/ppermute | solution.py:23
  97.6 15.2 %collective-permute-start.7 = (f16[64,1152]{1,0:T(8,128)(2,1)S(1)}, f16[64,1152]{1,0:T(8,128)(2,1)S(1)}, u32[]{:S(2)}, u32[]{:S(2)}) collective-permute-start(f16[64,1152]{1,0:T(8,128)(2,1)S(1)} %pad_maximum_fusion.5), channel_id=1, source_target_pairs={{0,32},{1,993},{2,34},{3,995},{4,36},{5,997},{6,38},{7,999},{8,40}... | collective-permute-start | bytes 442376 | tf_op jit(solution)/shard_map/ppermute | solution.py:23
  113.5 29.0 %copy-start.4 = (bf16[32,1152]{1,0:T(8,128)(2,1)S(1)}, bf16[32,1152]{1,0:T(8,128)(2,1)}, u32[]{:S(2)}) copy-start(bf16[32,1152]{1,0:T(8,128)(2,1)} %refs_0_.1) | copy-start | bytes 221188
  113.5 31.0 %all-to-all-start.1 = ((f16[16,32,1280]{2,1,0:T(8,128)(2,1)}), f16[16,32,1280]{2,1,0:T(8,128)(2,1)S(1)}, u32[]{:S(2)}, u32[]{:S(2)}) async-start(f16[16,32,1280]{2,1,0:T(8,128)(2,1)} %bitcast.19), calls=%async_computation.1 | async-start | bytes 2621440 | tf_op jit(solution)/shard_map/all_to_all | solution.py:175
  125.1 11.6 %collective-permute-start.10 = (f16[32,1152]{1,0:T(8,128)(2,1)S(1)}, f16[32,1152]{1,0:T(8,128)(2,1)S(1)}, u32[]{:S(2)}, u32[]{:S(2)}) collective-permute-start(f16[32,1152]{1,0:T(8,128)(2,1)S(1)} %get-tuple-element.27), channel_id=1, source_target_pairs={{0,80},{1,961},{2,82},{3,963},{4,84},{5,965},{6,86},{7,967},{8,88}... | collective-permute-start | bytes 221192 | tf_op jit(solution)/shard_map/ppermute | solution.py:23
  128.3 14.3 %collective-permute-start.11 = (f16[32,1152]{1,0:T(8,128)(2,1)S(1)}, f16[32,1152]{1,0:T(8,128)(2,1)S(1)}, u32[]{:S(2)}, u32[]{:S(2)}) collective-permute-start(f16[32,1152]{1,0:T(8,128)(2,1)S(1)} %get-tuple-element.28), channel_id=1, source_target_pairs={{0,960},{1,81},{2,962},{3,83},{4,964},{5,85},{6,966},{7,87},{8,968... | collective-permute-start | bytes 221192 | tf_op jit(solution)/shard_map/ppermute | solution.py:23

commit v6 on v5

--- a/solution.py
+++ b/solution.py
@@ -13,19 +13,19 @@
 F32 = jnp.float32
 
 
-def passed_along(value, steps0, steps1):
+def moved(value, rule):
     nblk, ndepth = (lax.axis_size("blk"), lax.axis_size("depth"))
     pairs = []
     for b in range(nblk):
         for d in range(ndepth):
-            to = (b + (steps1 if d % 2 else steps0)) % nblk
-            pairs.append((b * ndepth + d, to * ndepth + d))
+            to = rule(b, d)
+            if to is not None:
+                pairs.append((b * ndepth + d, to[0] % nblk * ndepth + to[1]))
     return lax.ppermute(value, ("blk", "depth"), pairs)
 
 
-def core_swapped(value):
-    ndepth = lax.axis_size("depth")
-    return lax.ppermute(value, "depth", [(d, d ^ 1) for d in range(ndepth)])
+def passed_along(value, steps0, steps1):
+    return moved(value, lambda b, d: (b + (steps1 if d % 2 else steps0), d))
 
 
 def unit_rows(x):
@@ -112,21 +112,22 @@
     core0 = depth % 2 == 0
 
     own = own_unit_slice(text, text_ids)
-    r1 = passed_along(own, -5, 4)
-    r2 = passed_along(own, 4, -5)
+    near = moved(own, lambda b, d: (b - 1, d - 1) if d % 2 else (b, d + 1))
+    above = moved(own, lambda b, d: None if d % 2 else (b - 1, d))
+    base = jnp.concatenate([jnp.where(core0, above, near), jnp.where(core0, near, own)], axis=0)
 
     video32 = video.astype(F32)
     vnorm = jnp.sqrt(jnp.sum(video32 * video32, axis=-1, keepdims=True) + EPS)
-    vnorm, r1 = lax.optimization_barrier((vnorm, r1))
+    vnorm, base = lax.optimization_barrier((vnorm, base))
     vhat = (video32 / vnorm).astype(BF16)
     vids = video_ids.astype(F32)[None, :]
     part = jnp.float32(1.0 / (rows * nblk * 2 * half))
     params = jnp.stack([jnp.exp(log_scale[0]), bias[0], part])
 
-    q1 = passed_along(jnp.concatenate([own, r1], axis=0), -2, 2)
-    q2 = passed_along(jnp.concatenate([own, r2], axis=0), 2, -2)
-    s1 = passed_along(jnp.concatenate([own, q1, r1, r2], axis=0), -1, 1)
-    s2 = passed_along(jnp.concatenate([own, q2, r2, r1], axis=0), 1, -1)
+    by4 = passed_along(base, -4, 4)
+    by2 = passed_along(jnp.concatenate([base, by4], axis=0), -2, 2)
+    held_text = jnp.concatenate([base, by4, by2], axis=0)
+    arrived = passed_along(held_text, -1, 1)
 
     def text_grad(coef):
         return jnp.einsum("cr,rd->cd", coef, vhat, preferred_element_type=F32)
@@ -134,58 +135,51 @@
     def video_grad(coef, texts):
         return jnp.einsum("cr,cd->rd", coef, texts, preferred_element_type=F32)
 
-    held_text = jnp.concatenate([own, q1, r1, q2, r2], axis=0)
     coef0, total = pair_coefs(params, held_text, vhat, vids, jnp.zeros((nblk, LANES), F32))
     share0 = video_grad(coef0, held_text)
     held = text_grad(coef0)
-    s1, s2, share0, held = lax.optimization_barrier((s1, s2, share0, held))
-
-    fifth = jnp.where(core0, s2[4 * n :], s1[4 * n :])
-    arrived = jnp.concatenate([s1[: 4 * n], s2[: 4 * n], fifth], axis=0)
+    arrived, share0, held = lax.optimization_barrier((arrived, share0, held))
     coef1, total = pair_coefs(params, arrived, vhat, vids, total)
 
+    back1 = passed_along(text_grad(coef1).astype(F16), 1, -1)
+
     totals = lax.all_to_all(total, "blk", 0, 0, tiled=True)
 
-    coef_s1 = jnp.concatenate([coef1[: 4 * n], coef1[8 * n :]], axis=0)
-    m1 = passed_along(text_grad(coef_s1).astype(F16), 1, -1)
-    m2 = passed_along(text_grad(coef1[4 * n :]).astype(F16), -1, 1)
-
     share = (share0 + video_grad(coef1, arrived)).astype(F16)
 
-    def unit_of(value, i):
-        return value[i * n : (i + 1) * n].astype(F32)
-
-    def pair_of(i, back):
-        units = [unit_of(held, i) + unit_of(back, 1), unit_of(held, i + 1) + unit_of(back, 2)]
-        return jnp.concatenate(units, axis=0).astype(F16)
-
-    n1 = passed_along(pair_of(1, m1), 2, -2)
-    n2 = passed_along(pair_of(4, m2), -2, 2)
-
-    totals, _, _ = lax.optimization_barrier((totals, n1, n2))
+    def rows_of(value, i, j):
+        return value[i * n : j * n].astype(F32)
+
+    back2 = passed_along((rows_of(held, 4, 8) + rows_of(back1, 4, 8)).astype(F16), 2, -2)
+    home4 = rows_of(held, 2, 4) + rows_of(back1, 2, 4) + rows_of(back2, 2, 4)
+    home = rows_of(held, 0, 2) + rows_of(back1, 0, 2) + rows_of(back2, 0, 2)
+    home = home + passed_along(home4.astype(F16), 4, -4).astype(F32)
+
+    to_near = jnp.where(core0, home[n:], home[:n]).astype(F16)
+    near = moved(to_near, lambda b, d: (b, d - 1) if d % 2 else (b + 1, d + 1))
+    below = moved(home[:n].astype(F16), lambda b, d: None if d % 2 else (b + 1, d))
+    grad_that = near.astype(F32) + jnp.where(core0, below.astype(F32), home[n:])
+
+    totals, back2 = lax.optimization_barrier((totals, back2))
     total = jnp.sum(totals, axis=0, keepdims=True)
     first = total.astype(F16)
     rest = (total - first.astype(F32)) * 2.0**11
     second = rest.astype(F16)
     third = ((rest - second.astype(F32)) * 2.0**11).astype(F16)
     lane = lax.broadcasted_iota(jnp.int32, (1, LANES), 1)
-    digits = jnp.where(lane == 0, first, jnp.where(lane == 1, second, third))
+    digits = jnp.where(lane == 2, third, jnp.zeros_like(third))
+    digits = jnp.where(lane == 0, first, jnp.where(lane == 1, second, digits))
     digits = jnp.broadcast_to(digits, (rows, LANES))
     share = lax.dynamic_update_slice(share, digits, (0, width))
     shares = lax.all_to_all(share, "depth", 0, 0, tiled=True).reshape(ndepth, n, width + LANES)
     grad_vhat = jnp.sum(shares[:, :, :width].astype(F32), axis=0)
-    digits = jnp.sum(shares[:, 0, width : width + 3].astype(F32), axis=0)
-    loss = digits[0] + digits[1] * 2.0**-11 + digits[2] * 2.0**-22
-
-    h1 = unit_of(held, 3) + unit_of(m1, 3) + jnp.where(core0, unit_of(m2, 4), 0.0) + unit_of(n1, 1)
-    h2 = unit_of(held, 6) + unit_of(m2, 3) + jnp.where(core0, 0.0, unit_of(m1, 4)) + unit_of(n2, 1)
-    home = unit_of(held, 0) + unit_of(m1, 0) + unit_of(m2, 0) + unit_of(n1, 0) + unit_of(n2, 0)
-    h1 = passed_along(h1.astype(F16), 5, -4)
-    h2 = passed_along(h2.astype(F16), -4, 5)
-    grad_that = home + h1.astype(F32) + h2.astype(F32)
+    weight = jnp.where(lane == 0, 1.0, jnp.where(lane == 1, 2.0**-11, 2.0**-22))
+    weight = jnp.where(lane < 3, weight, 0.0)
+    loss = jnp.sum(shares[:, 0, width:].astype(F32) * weight)
 
     tunit, tnorm = unit_rows(text)
-    own_unit, own_norm = unit_rows(lax.dynamic_slice_in_dim(video, depth * n, n, 0))
+    own_norm = lax.dynamic_slice_in_dim(vnorm, depth * n, n, 0)
+    own_unit = lax.dynamic_slice_in_dim(video, depth * n, n, 0).astype(F32) / own_norm
     grad_video = (
         grad_vhat - own_unit * jnp.sum(own_unit * grad_vhat, axis=-1, keepdims=True)
     ) / own_norm

time: 152 us -> 151 us (level)
  waiting for transfers between devices: 28.1 us -> 52 us
  starting transfers between devices: 90 us -> 71.5 us
  between operations: 5.35 us -> 2.26 us
  matrix products: 6.17 us -> 3.94 us
    ppermute x12 -> x10, starting transfers between devices: 70.6 us -> 46.3 us  [moved(): return lax.ppermute(value, ('blk', 'depth'), pairs)]
    ppermute x12 -> x10, waiting for transfers between devices: 18.8 us -> 30.6 us  [moved(): return lax.ppermute(value, ('blk', 'depth'), pairs)]
    all_to_all x1, waiting for transfers between devices: 0.01 us -> 9.49 us  [shards(): lax.all_to_all(share, 'depth', 0, 0, tiled=True)]
    all_to_all x1, starting transfers between devices: 9.07 us -> 13.2 us  [shards(): totals = lax.all_to_all(total, 'blk', 0, 0, tiled=True)]
    all_to_all x1, waiting for transfers between devices: 9.29 us -> 11.9 us  [shards(): totals = lax.all_to_all(total, 'blk', 0, 0, tiled=True)]
    reduce_sum x2 -> x1, other arithmetic: 2.01 us -> 0.13 us  [unit_rows(): norms = jnp.sqrt(jnp.sum(x32 * x32, axis=-1, keepdims=True) + EPS)]
    all_to_all x1, starting transfers between devices: 10.4 us -> 12 us  [shards(): lax.all_to_all(share, 'depth', 0, 0, tiled=True)]
    dot_general x3 -> x2, matrix products: 3.71 us -> 2.86 us  [text_grad(): return jnp.einsum('cr,rd->cd', coef, vhat, preferred_element_type=F32)]
  transfers between devices with their start and end apart: 14 -> 12, of which waited for: 7 -> 6; matrix products, arithmetic and copies ran while one was open for 10% -> 7% of each run, Pallas kernels for 1% -> 1%
where the time goes in v6:
time: 151 us; the launch traced here: 150 us
  starting transfers between devices  71.5 us (47%)
  waiting for transfers between devices  52 us (34%)
  other arithmetic  13.2 us (9%)
  Pallas kernels  5.44 us (4%)
  matrix products  3.94 us (3%)
  between operations  2.26 us (1%)
  local copies, waits for them, and re-layouts  1.58 us (1%)
    ppermute x10, starting transfers between devices, moved(): return lax.ppermute(value, ('blk', 'depth'), pairs)  46.3 us
    ppermute x10, waiting for transfers between devices, moved(): return lax.ppermute(value, ('blk', 'depth'), pairs)  30.6 us
    all_to_all x1, starting transfers between devices, shards(): totals = lax.all_to_all(total, 'blk', 0, 0, tiled=True)  13.2 us
    all_to_all x1, starting transfers between devices, shards(): lax.all_to_all(share, 'depth', 0, 0, tiled=True)  12 us
    all_to_all x1, waiting for transfers between devices, shards(): totals = lax.all_to_all(total, 'blk', 0, 0, tiled=True)  11.9 us
    all_to_all x1, waiting for transfers between devices, shards(): lax.all_to_all(share, 'depth', 0, 0, tiled=True)  9.49 us
    pallas_call x2, Pallas kernels, pair_coefs(): pl.pallas_call(lambda *refs: coef_kernel(width, *refs), out_shape=(jax.Sh...  3.75 us
  transfers between devices with their start and end apart: 12, of which 6 were waited for; matrix products, arithmetic and copies ran while one was open for 7% of the time, Pallas kernels for 1%

profile of v6, /device:TPU:1, one launch (start us, length us, event | category | flops | bytes accessed | tf_op | source)
XLA Modules:
  0.0 149.9 jit_solution(14171740415544089377)
XLA Ops:
  0.7 1.7 %shard_map.85 = bf16[32,1280]{1,0:T(8,128)(2,1)} custom-call(bf16[32,1152]{1,0:T(8,128)(2,1)} %refs_0_.1, s32[1,32]{1,0:T(1,128)} %bitcast.25), custom_call_target="tpu_custom_call" | custom-call | tf_op jit(solution)/shard_map/pallas_call | solution.py:97
  2.3 20.8 %collective-permute-start.1 = (bf16[32,1280]{1,0:T(8,128)(2,1)}, bf16[32,1280]{1,0:T(8,128)(2,1)S(1)}, u32[]{:S(2)}, u32[]{:S(2)}) collective-permute-start(bf16[32,1280]{1,0:T(8,128)(2,1)} %shard_map.85), channel_id=1, source_target_pairs={{0,1},{1,1008},{2,3},{3,1010},{4,5},{5,1012},{6,7},{7,1014},{8,9},... | collective-permute-start | bytes 245768 | tf_op jit(solution)/shard_map/ppermute | solution.py:24
  23.8 1.6 %fusion = f32[512]{0:T(512)S(1)} fusion(bf16[512,1152]{1,0:T(8,128)(2,1)} %param.6), kind=kLoop, calls=%fused_computation.4 | loop fusion | flops 1768960 | bytes 1181696 | tf_op jit(solution)/shard_map/reduce_sum | solution.py:120
  27.8 1.9 %collective-permute-start.2 = (bf16[64,1280]{1,0:T(8,128)(2,1)S(1)}, bf16[64,1280]{1,0:T(8,128)(2,1)S(1)}, u32[]{:S(2)}, u32[]{:S(2)}) collective-permute-start(bf16[64,1280]{1,0:T(8,128)(2,1)S(1)} %pad_maximum_fusion.1), channel_id=1, source_target_pairs={{0,960},{1,65},{2,962},{3,67},{4,964},{5,69},{6,966},{7,71},{8,968... | collective-permute-start | bytes 491528 | tf_op jit(solution)/shard_map/ppermute | solution.py:24
  29.9 13.5 %collective-permute-done.2 = bf16[64,1280]{1,0:T(8,128)(2,1)S(1)} collective-permute-done((bf16[64,1280]{1,0:T(8,128)(2,1)S(1)}, bf16[64,1280]{1,0:T(8,128)(2,1)S(1)}, u32[]{:S(2)}, u32[]{:S(2)}) %collective-permute-start.2) | collective-permute-done | bytes 163872 | tf_op jit(solution)/shard_map/ppermute | solution.py:24
  43.5 1.9 %collective-permute-start.3 = (bf16[128,1280]{1,0:T(8,128)(2,1)S(1)}, bf16[128,1280]{1,0:T(8,128)(2,1)S(1)}, u32[]{:S(2)}, u32[]{:S(2)}) collective-permute-start(bf16[128,1280]{1,0:T(8,128)(2,1)S(1)} %pad_maximum_fusion), channel_id=1, source_target_pairs={{0,992},{1,33},{2,994},{3,35},{4,996},{5,37},{6,998},{7,39},{8,100... | collective-permute-start | bytes 983048 | tf_op jit(solution)/shard_map/ppermute | solution.py:24
  45.5 9.5 %collective-permute-done.3 = bf16[128,1280]{1,0:T(8,128)(2,1)S(1)} collective-permute-done((bf16[128,1280]{1,0:T(8,128)(2,1)S(1)}, bf16[128,1280]{1,0:T(8,128)(2,1)S(1)}, u32[]{:S(2)}, u32[]{:S(2)}) %collective-permute-start.3) | collective-permute-done | bytes 327712 | tf_op jit(solution)/shard_map/ppermute | solution.py:24
  55.0 1.9 %collective-permute-start.4 = (bf16[256,1280]{1,0:T(8,128)(2,1)S(1)}, bf16[256,1280]{1,0:T(8,128)(2,1)S(1)}, u32[]{:S(2)}, u32[]{:S(2)}) collective-permute-start(bf16[256,1280]{1,0:T(8,128)(2,1)S(1)} %constant_dynamic-update-slice_fusion.refs_1_), channel_id=1, source_target_pairs={{0,1008},{1,17},{2,1010},{3,19},{4,1012},{5,21},{6,1014},{7,23},{8... | collective-permute-start | bytes 1966088 | tf_op jit(solution)/shard_map/ppermute | solution.py:24
  57.3 1.6 %shard_map.86 = (bf16[256,512]{1,0:T(8,128)(2,1)S(1)}, f32[64,128]{1,0:T(8,128)S(1)}) custom-call(f32[3]{0:T(128)S(1)} %pad_maximum_fusion.2.refs_0_, bf16[256,1280]{1,0:T(8,128)(2,1)S(1)} %constant_dynamic-update-slice_fusion.refs_1_, bf16[512,1152]{1,0:T(8,128)(2,1)S(1)} %fusion.1.refs_2_, f32[1,512]{1,0:T(1,128)S(1)} %bitcast.20, ...), custom_call_target="tpu_custom_call" | custom-call | flops 301989888 | bytes 1769472 | tf_op jit(solution)/shard_map/pallas_call | solution.py:62
  58.9 1.5 %fusion.5 = f32[256,1152]{1,0:T(8,128)} fusion(bf16[256,512]{1,0:T(8,128)(2,1)S(1)} %get-tuple-element.15, bf16[512,1152]{1,0:T(8,128)(2,1)S(1)} %fusion.1.refs_2_), kind=kOutput, calls=%fused_computation.43 | convolution fusion | flops 301989888 | bytes 2621440 | tf_op jit(solution)/shard_map/cr,rd->cd/dot_general | solution.py:133
  61.0 7.5 %collective-permute-done.4.refs_1_ = bf16[256,1280]{1,0:T(8,128)(2,1)S(1)} collective-permute-done((bf16[256,1280]{1,0:T(8,128)(2,1)S(1)}, bf16[256,1280]{1,0:T(8,128)(2,1)S(1)}, u32[]{:S(2)}, u32[]{:S(2)}) %collective-permute-start.4) | collective-permute-done | bytes 655392 | tf_op jit(solution)/shard_map/ppermute | solution.py:24
  68.4 2.2 %shard_map.87 = (bf16[256,512]{1,0:T(8,128)(2,1)S(1)}, f32[64,128]{1,0:T(8,128)}) custom-call(f32[3]{0:T(128)S(1)} %pad_maximum_fusion.2.refs_0_, bf16[256,1280]{1,0:T(8,128)(2,1)S(1)} %collective-permute-done.4.refs_1_, bf16[512,1152]{1,0:T(8,128)(2,1)S(1)} %fusion.1.refs_2_, f32[1,512]{1,0:T(1,128)S(1)} %bitcast.21, f32[64,128]{1,0:T(8,128)S(1)} %get-tuple-element.18.refs_4_), custom_call_target="tpu_custom_call" | custom-call | flops 301989888 | bytes 1769472 | tf_op jit(solution)/shard_map/pallas_call | solution.py:62
  70.6 1.3 convolution_convert_fusion
  71.9 1.9 %collective-permute-start.5 = (f16[256,1152]{1,0:T(8,128)(2,1)}, f16[256,1152]{1,0:T(8,128)(2,1)}, u32[]{:S(2)}, u32[]{:S(2)}) collective-permute-start(f16[256,1152]{1,0:T(8,128)(2,1)} %convolution_convert_fusion), channel_id=1, source_target_pairs={{0,16},{1,1009},{2,18},{3,1011},{4,20},{5,1013},{6,22},{7,1015},{8... | collective-permute-start | bytes 1769480 | tf_op jit(solution)/shard_map/ppermute | solution.py:24
  73.9 13.2 %all-to-all-start = ((f32[64,1,128]{2,1,0:T(1,128)}), f32[64,1,128]{2,1,0:T(1,128)}, u32[]{:S(2)}, u32[]{:S(2)}) async-start(f32[64,1,128]{2,1,0:T(1,128)} %bitcast.5), calls=%async_computation | async-start | bytes 65536 | tf_op jit(solution)/shard_map/all_to_all | solution.py:146
  89.4 6.2 %collective-permute-start.6 = (f16[128,1152]{1,0:T(8,128)(2,1)S(1)}, f16[128,1152]{1,0:T(8,128)(2,1)S(1)}, u32[]{:S(2)}, u32[]{:S(2)}) collective-permute-start(f16[128,1152]{1,0:T(8,128)(2,1)S(1)} %add_convert_fusion.1), channel_id=1, source_target_pairs={{0,32},{1,993},{2,34},{3,995},{4,36},{5,997},{6,38},{7,999},{8,40}... | collective-permute-start | bytes 884744 | tf_op jit(solution)/shard_map/ppermute | solution.py:24
  95.6 1.4 add_convert_fusion
  97.0 11.9 %all-to-all-done = f32[64,1,128]{2,1,0:T(1,128)} async-done(((f32[64,1,128]{2,1,0:T(1,128)}), f32[64,1,128]{2,1,0:T(1,128)}, u32[]{:S(2)}, u32[]{:S(2)}) %all-to-all-start) | async-done | bytes 32800 | tf_op jit(solution)/shard_map/all_to_all | solution.py:146
  110.8 2.5 %collective-permute-start.7 = (f16[64,1152]{1,0:T(8,128)(2,1)S(1)}, f16[64,1152]{1,0:T(8,128)(2,1)S(1)}, u32[]{:S(2)}, u32[]{:S(2)}) collective-permute-start(f16[64,1152]{1,0:T(8,128)(2,1)S(1)} %add_convert_fusion.2), channel_id=1, source_target_pairs={{0,64},{1,961},{2,66},{3,963},{4,68},{5,965},{6,70},{7,967},{8,72}... | collective-permute-start | bytes 442376 | tf_op jit(solution)/shard_map/ppermute | solution.py:24
  114.0 12.0 %all-to-all-start.1 = ((f16[16,32,1280]{2,1,0:T(8,128)(2,1)}), f16[16,32,1280]{2,1,0:T(8,128)(2,1)S(1)}, u32[]{:S(2)}, u32[]{:S(2)}) async-start(f16[16,32,1280]{2,1,0:T(8,128)(2,1)} %bitcast.22), calls=%async_computation.1 | async-start | bytes 2621440 | tf_op jit(solution)/shard_map/all_to_all | solution.py:174
  126.0 1.2 convert_add_fusion
  127.2 7.8 %collective-permute-start.8 = (f16[32,1152]{1,0:T(8,128)(2,1)S(1)}, f16[32,1152]{1,0:T(8,128)(2,1)S(1)}, u32[]{:S(2)}, u32[]{:S(2)}) collective-permute-start(f16[32,1152]{1,0:T(8,128)(2,1)S(1)} %get-tuple-element.23), channel_id=1, source_target_pairs={{0,17},{1,0},{2,19},{3,2},{4,21},{5,4},{6,23},{7,6},{8,25},{9,8},{... | collective-permute-start | bytes 221192 | tf_op jit(solution)/shard_map/ppermute | solution.py:24
  136.9 9.5 %all-to-all-done.1 = f16[16,32,1280]{2,1,0:T(8,128)(2,1)S(1)} async-done(((f16[16,32,1280]{2,1,0:T(8,128)(2,1)}), f16[16,32,1280]{2,1,0:T(8,128)(2,1)S(1)}, u32[]{:S(2)}, u32[]{:S(2)}) %all-to-all-start.1) | async-done | bytes 1310752 | tf_op jit(solution)/shard_map/all_to_all | solution.py:174
  147.6 1.6 %subtract_divide_fusion.1 = f32[32,1152]{1,0:T(8,128)} fusion(f32[32,1152]{1,0:T(8,128)S(1)} %convert_reduce_fusion, f32[32]{0:T(128)S(1)} %multiply_reduce_fusion.1, f32[32]{0:T(128)S(1)} %fusion.3, bf16[512,1152]{1,0:T(8,128)(2,1)} %param.6, s32[]{:T(128)S(6)} %select_n.97), kind=kLoop, calls=%fused_computation.19 | loop fusion | flops 184320 | bytes 368900 | tf_op jit(solution)/shard_map/div | solution.py:183
  (50 shorter events, 11.5 us)
Async XLA Ops:
  0.6 29.2 %copy-start.2 = (bf16[32,1152]{1,0:T(8,128)(2,1)S(1)}, bf16[32,1152]{1,0:T(8,128)(2,1)}, u32[]{:S(2)}) copy-start(bf16[32,1152]{1,0:T(8,128)(2,1)} %refs_0_.1) | copy-start | bytes 221188
  0.6 29.2 %copy-start.5 = (s32[512]{0:T(512)S(1)}, s32[512]{0:T(512)}, u32[]{:S(2)}) copy-start(s32[512]{0:T(512)} %param.8) | copy-start | bytes 6148
  2.3 24.4 %collective-permute-start.1 = (bf16[32,1280]{1,0:T(8,128)(2,1)}, bf16[32,1280]{1,0:T(8,128)(2,1)S(1)}, u32[]{:S(2)}, u32[]{:S(2)}) collective-permute-start(bf16[32,1280]{1,0:T(8,128)(2,1)} %shard_map.85), channel_id=1, source_target_pairs={{0,1},{1,1008},{2,3},{3,1010},{4,5},{5,1012},{6,7},{7,1014},{8,9},... | collective-permute-start | bytes 245768 | tf_op jit(solution)/shard_map/ppermute | solution.py:24
  23.1 3.6 %collective-permute-start = (bf16[32,1280]{1,0:T(8,128)(2,1)}, bf16[32,1280]{1,0:T(8,128)(2,1)S(1)}, u32[]{:S(2)}, u32[]{:S(2)}) collective-permute-start(bf16[32,1280]{1,0:T(8,128)(2,1)} %shard_map.85), channel_id=1, source_target_pairs={{0,1008},{2,1010},{4,1012},{6,1014},{8,1016},{10,1018},{12,1020},{... | collective-permute-start | bytes 245768 | tf_op jit(solution)/shard_map/ppermute | solution.py:24
  26.7 30.2 %copy-start = (bf16[512,1152]{1,0:T(8,128)(2,1)S(1)}, bf16[512,1152]{1,0:T(8,128)(2,1)}, u32[]{:S(2)}) copy-start(bf16[512,1152]{1,0:T(8,128)(2,1)} %param.6) | copy-start | bytes 3538948
  27.8 15.7 %collective-permute-start.2 = (bf16[64,1280]{1,0:T(8,128)(2,1)S(1)}, bf16[64,1280]{1,0:T(8,128)(2,1)S(1)}, u32[]{:S(2)}, u32[]{:S(2)}) collective-permute-start(bf16[64,1280]{1,0:T(8,128)(2,1)S(1)} %pad_maximum_fusion.1), channel_id=1, source_target_pairs={{0,960},{1,65},{2,962},{3,67},{4,964},{5,69},{6,966},{7,71},{8,968... | collective-permute-start | bytes 491528 | tf_op jit(solution)/shard_map/ppermute | solution.py:24
  43.5 11.5 %collective-permute-start.3 = (bf16[128,1280]{1,0:T(8,128)(2,1)S(1)}, bf16[128,1280]{1,0:T(8,128)(2,1)S(1)}, u32[]{:S(2)}, u32[]{:S(2)}) collective-permute-start(bf16[128,1280]{1,0:T(8,128)(2,1)S(1)} %pad_maximum_fusion), channel_id=1, source_target_pairs={{0,992},{1,33},{2,994},{3,35},{4,996},{5,37},{6,998},{7,39},{8,100... | collective-permute-start | bytes 983048 | tf_op jit(solution)/shard_map/ppermute | solution.py:24
  55.0 13.4 %collective-permute-start.4 = (bf16[256,1280]{1,0:T(8,128)(2,1)S(1)}, bf16[256,1280]{1,0:T(8,128)(2,1)S(1)}, u32[]{:S(2)}, u32[]{:S(2)}) collective-permute-start(bf16[256,1280]{1,0:T(8,128)(2,1)S(1)} %constant_dynamic-update-slice_fusion.refs_1_), channel_id=1, source_target_pairs={{0,1008},{1,17},{2,1010},{3,19},{4,1012},{5,21},{6,1014},{7,23},{8... | collective-permute-start | bytes 1966088 | tf_op jit(solution)/shard_map/ppermute | solution.py:24
  71.9 15.7 %collective-permute-start.5 = (f16[256,1152]{1,0:T(8,128)(2,1)}, f16[256,1152]{1,0:T(8,128)(2,1)}, u32[]{:S(2)}, u32[]{:S(2)}) collective-permute-start(f16[256,1152]{1,0:T(8,128)(2,1)} %convolution_convert_fusion), channel_id=1, source_target_pairs={{0,16},{1,1009},{2,18},{3,1011},{4,20},{5,1013},{6,22},{7,1015},{8... | collective-permute-start | bytes 1769480 | tf_op jit(solution)/shard_map/ppermute | solution.py:24
  73.9 35.0 %all-to-all-start = ((f32[64,1,128]{2,1,0:T(1,128)}), f32[64,1,128]{2,1,0:T(1,128)}, u32[]{:S(2)}, u32[]{:S(2)}) async-start(f32[64,1,128]{2,1,0:T(1,128)} %bitcast.5), calls=%async_computation | async-start | bytes 65536 | tf_op jit(solution)/shard_map/all_to_all | solution.py:146
  87.1 1.3 copy-start.1
  89.4 19.5 %collective-permute-start.6 = (f16[128,1152]{1,0:T(8,128)(2,1)S(1)}, f16[128,1152]{1,0:T(8,128)(2,1)S(1)}, u32[]{:S(2)}, u32[]{:S(2)}) collective-permute-start(f16[128,1152]{1,0:T(8,128)(2,1)S(1)} %add_convert_fusion.1), channel_id=1, source_target_pairs={{0,32},{1,993},{2,34},{3,995},{4,36},{5,997},{6,38},{7,999},{8,40}... | collective-permute-start | bytes 884744 | tf_op jit(solution)/shard_map/ppermute | solution.py:24
  108.9 5.1 %copy-start.4 = (f16[128,1152]{1,0:T(8,128)(2,1)}, f16[128,1152]{1,0:T(8,128)(2,1)S(1)}, u32[]{:S(2)}) copy-start(f16[128,1152]{1,0:T(8,128)(2,1)S(1)} %collective-permute-done.6) | copy-start | bytes 884740
  110.8 15.3 %collective-permute-start.7 = (f16[64,1152]{1,0:T(8,128)(2,1)S(1)}, f16[64,1152]{1,0:T(8,128)(2,1)S(1)}, u32[]{:S(2)}, u32[]{:S(2)}) collective-permute-start(f16[64,1152]{1,0:T(8,128)(2,1)S(1)} %add_convert_fusion.2), channel_id=1, source_target_pairs={{0,64},{1,961},{2,66},{3,963},{4,68},{5,965},{6,70},{7,967},{8,72}... | collective-permute-start | bytes 442376 | tf_op jit(solution)/shard_map/ppermute | solution.py:24
  114.0 32.4 %all-to-all-start.1 = ((f16[16,32,1280]{2,1,0:T(8,128)(2,1)}), f16[16,32,1280]{2,1,0:T(8,128)(2,1)S(1)}, u32[]{:S(2)}, u32[]{:S(2)}) async-start(f16[16,32,1280]{2,1,0:T(8,128)(2,1)} %bitcast.22), calls=%async_computation.1 | async-start | bytes 2621440 | tf_op jit(solution)/shard_map/all_to_all | solution.py:174
  126.0 9.9 %copy-start.3 = (bf16[32,1152]{1,0:T(8,128)(2,1)S(1)}, bf16[32,1152]{1,0:T(8,128)(2,1)}, u32[]{:S(2)}) copy-start(bf16[32,1152]{1,0:T(8,128)(2,1)} %refs_0_.1) | copy-start | bytes 221188
  127.2 8.7 %collective-permute-start.8 = (f16[32,1152]{1,0:T(8,128)(2,1)S(1)}, f16[32,1152]{1,0:T(8,128)(2,1)S(1)}, u32[]{:S(2)}, u32[]{:S(2)}) collective-permute-start(f16[32,1152]{1,0:T(8,128)(2,1)S(1)} %get-tuple-element.23), channel_id=1, source_target_pairs={{0,17},{1,0},{2,19},{3,2},{4,21},{5,4},{6,23},{7,6},{8,25},{9,8},{... | collective-permute-start | bytes 221192 | tf_op jit(solution)/shard_map/ppermute | solution.py:24
  135.0 0.9 collective-permute-start.9

commit v7 on v6

--- a/solution.py
+++ b/solution.py
@@ -125,6 +125,10 @@
     params = jnp.stack([jnp.exp(log_scale[0]), bias[0], part])
 
     by4 = passed_along(base, -4, 4)
+    own_video = lax.dynamic_slice_in_dim(video, depth * n, n, 0)
+    own_video, text, by4 = lax.optimization_barrier((own_video, text, by4))
+    own_unit, own_norm = unit_rows(own_video)
+    tunit, tnorm = unit_rows(text)
     by2 = passed_along(jnp.concatenate([base, by4], axis=0), -2, 2)
     held_text = jnp.concatenate([base, by4, by2], axis=0)
     arrived = passed_along(held_text, -1, 1)
@@ -138,7 +142,9 @@
     coef0, total = pair_coefs(params, held_text, vhat, vids, jnp.zeros((nblk, LANES), F32))
     share0 = video_grad(coef0, held_text)
     held = text_grad(coef0)
-    arrived, share0, held = lax.optimization_barrier((arrived, share0, held))
+    arrived, share0, held, own_unit, own_norm, tunit, tnorm = lax.optimization_barrier(
+        (arrived, share0, held, own_unit, own_norm, tunit, tnorm)
+    )
     coef1, total = pair_coefs(params, arrived, vhat, vids, total)
 
     back1 = passed_along(text_grad(coef1).astype(F16), 1, -1)
@@ -177,9 +183,6 @@
     weight = jnp.where(lane < 3, weight, 0.0)
     loss = jnp.sum(shares[:, 0, width:].astype(F32) * weight)
 
-    tunit, tnorm = unit_rows(text)
-    own_norm = lax.dynamic_slice_in_dim(vnorm, depth * n, n, 0)
-    own_unit = lax.dynamic_slice_in_dim(video, depth * n, n, 0).astype(F32) / own_norm
     grad_video = (
         grad_vhat - own_unit * jnp.sum(own_unit * grad_vhat, axis=-1, keepdims=True)
     ) / own_norm

time: 151 us -> 147 us (0.974)
  starting transfers between devices: 71.5 us -> 68.6 us
  other arithmetic: 13.2 us -> 11.2 us
    ppermute x10, waiting for transfers between devices: 30.6 us -> 44.1 us  [moved(): return lax.ppermute(value, ('blk', 'depth'), pairs)]
    all_to_all x1, waiting for transfers between devices: 11.9 us -> 0.01 us  [shards(): totals = lax.all_to_all(total, 'blk', 0, 0, tiled=True)]
    all_to_all x1, starting transfers between devices: 13.2 us -> 10 us  [shards(): totals = lax.all_to_all(total, 'blk', 0, 0, tiled=True)]
  transfers between devices with their start and end apart: 12 -> 12, of which waited for: 6 -> 6; matrix products, arithmetic and copies ran while one was open for 7% -> 9% of each run, Pallas kernels for 1% -> 1%
where the time goes in v7:
time: 147 us; the launch traced here: 146 us
  starting transfers between devices  68.6 us (47%)
  waiting for transfers between devices  53.5 us (36%)
  other arithmetic  11.2 us (8%)
  Pallas kernels  5.48 us (4%)
  matrix products  3.94 us (3%)
  between operations  2.31 us (2%)
  local copies, waits for them, and re-layouts  1.5 us (1%)
    ppermute x10, starting transfers between devices, moved(): return lax.ppermute(value, ('blk', 'depth'), pairs)  47.2 us
    ppermute x10, waiting for transfers between devices, moved(): return lax.ppermute(value, ('blk', 'depth'), pairs)  44.1 us
    all_to_all x1, starting transfers between devices, shards(): lax.all_to_all(share, 'depth', 0, 0, tiled=True)  11.3 us
    all_to_all x1, starting transfers between devices, shards(): totals = lax.all_to_all(total, 'blk', 0, 0, tiled=True)  10 us
    all_to_all x1, waiting for transfers between devices, shards(): lax.all_to_all(share, 'depth', 0, 0, tiled=True)  9.37 us
    pallas_call x2, Pallas kernels, pair_coefs(): pl.pallas_call(lambda *refs: coef_kernel(width, *refs), out_shape=(jax.Sh...  3.75 us
  transfers between devices with their start and end apart: 12, of which 6 were waited for; matrix products, arithmetic and copies ran while one was open for 9% of the time, Pallas kernels for 1%

profile of v7, /device:TPU:1, one launch (start us, length us, event | category | flops | bytes accessed | tf_op | source)
XLA Modules:
  0.0 146.5 jit_solution(17072352712380445371)
XLA Ops:
  0.7 1.7 %shard_map.85 = bf16[32,1280]{1,0:T(8,128)(2,1)} custom-call(bf16[32,1152]{1,0:T(8,128)(2,1)} %refs_0_.1, s32[1,32]{1,0:T(1,128)} %bitcast.28), custom_call_target="tpu_custom_call" | custom-call | tf_op jit(solution)/shard_map/pallas_call | solution.py:97
  3.2 23.1 %collective-permute-start.1 = (bf16[32,1280]{1,0:T(8,128)(2,1)}, bf16[32,1280]{1,0:T(8,128)(2,1)S(1)}, u32[]{:S(2)}, u32[]{:S(2)}) collective-permute-start(bf16[32,1280]{1,0:T(8,128)(2,1)} %shard_map.85), channel_id=1, source_target_pairs={{0,1},{1,1008},{2,3},{3,1010},{4,5},{5,1012},{6,7},{7,1014},{8,9},... | collective-permute-start | bytes 245768 | tf_op jit(solution)/shard_map/ppermute | solution.py:24
  26.2 1.6 %fusion = f32[512]{0:T(512)S(1)} fusion(bf16[512,1152]{1,0:T(8,128)(2,1)} %param.6), kind=kLoop, calls=%fused_computation.4 | loop fusion | flops 1768960 | bytes 1181696 | tf_op jit(solution)/shard_map/reduce_sum | solution.py:120
  29.4 1.9 %collective-permute-start.2 = (bf16[64,1280]{1,0:T(8,128)(2,1)S(1)}, bf16[64,1280]{1,0:T(8,128)(2,1)S(1)}, u32[]{:S(2)}, u32[]{:S(2)}) collective-permute-start(bf16[64,1280]{1,0:T(8,128)(2,1)S(1)} %pad_maximum_fusion.1), channel_id=1, source_target_pairs={{0,960},{1,65},{2,962},{3,67},{4,964},{5,69},{6,966},{7,71},{8,968... | collective-permute-start | bytes 491528 | tf_op jit(solution)/shard_map/ppermute | solution.py:24
  31.7 12.9 %collective-permute-done.2 = bf16[64,1280]{1,0:T(8,128)(2,1)S(1)} collective-permute-done((bf16[64,1280]{1,0:T(8,128)(2,1)S(1)}, bf16[64,1280]{1,0:T(8,128)(2,1)S(1)}, u32[]{:S(2)}, u32[]{:S(2)}) %collective-permute-start.2) | collective-permute-done | bytes 163872 | tf_op jit(solution)/shard_map/ppermute | solution.py:24
  44.6 1.9 %collective-permute-start.3 = (bf16[128,1280]{1,0:T(8,128)(2,1)S(1)}, bf16[128,1280]{1,0:T(8,128)(2,1)S(1)}, u32[]{:S(2)}, u32[]{:S(2)}) collective-permute-start(bf16[128,1280]{1,0:T(8,128)(2,1)S(1)} %pad_maximum_fusion), channel_id=1, source_target_pairs={{0,992},{1,33},{2,994},{3,35},{4,996},{5,37},{6,998},{7,39},{8,100... | collective-permute-start | bytes 983048 | tf_op jit(solution)/shard_map/ppermute | solution.py:24
  46.9 12.1 %collective-permute-done.3 = bf16[128,1280]{1,0:T(8,128)(2,1)S(1)} collective-permute-done((bf16[128,1280]{1,0:T(8,128)(2,1)S(1)}, bf16[128,1280]{1,0:T(8,128)(2,1)S(1)}, u32[]{:S(2)}, u32[]{:S(2)}) %collective-permute-start.3) | collective-permute-done | bytes 327712 | tf_op jit(solution)/shard_map/ppermute | solution.py:24
  59.0 1.9 %collective-permute-start.4 = (bf16[256,1280]{1,0:T(8,128)(2,1)S(1)}, bf16[256,1280]{1,0:T(8,128)(2,1)S(1)}, u32[]{:S(2)}, u32[]{:S(2)}) collective-permute-start(bf16[256,1280]{1,0:T(8,128)(2,1)S(1)} %constant_dynamic-update-slice_fusion.refs_1_), channel_id=1, source_target_pairs={{0,1008},{1,17},{2,1010},{3,19},{4,1012},{5,21},{6,1014},{7,23},{8... | collective-permute-start | bytes 1966088 | tf_op jit(solution)/shard_map/ppermute | solution.py:24
  61.7 1.6 %shard_map.86 = (bf16[256,512]{1,0:T(8,128)(2,1)S(1)}, f32[64,128]{1,0:T(8,128)S(1)}) custom-call(f32[3]{0:T(128)S(1)} %pad_maximum_fusion.2.refs_0_, bf16[256,1280]{1,0:T(8,128)(2,1)S(1)} %constant_dynamic-update-slice_fusion.refs_1_, bf16[512,1152]{1,0:T(8,128)(2,1)S(1)} %fusion.1.refs_2_, f32[1,512]{1,0:T(1,128)S(1)} %bitcast.24, ...), custom_call_target="tpu_custom_call" | custom-call | flops 301989888 | bytes 1769472 | tf_op jit(solution)/shard_map/pallas_call | solution.py:62
  63.3 1.5 %fusion.7 = f32[256,1152]{1,0:T(8,128)} fusion(bf16[256,512]{1,0:T(8,128)(2,1)S(1)} %get-tuple-element.23, bf16[512,1152]{1,0:T(8,128)(2,1)S(1)} %fusion.1.refs_2_), kind=kOutput, calls=%fused_computation.47 | convolution fusion | flops 301989888 | bytes 2621440 | tf_op jit(solution)/shard_map/cr,rd->cd/dot_general | solution.py:137
  65.4 7.1 %collective-permute-done.4.refs_1_ = bf16[256,1280]{1,0:T(8,128)(2,1)S(1)} collective-permute-done((bf16[256,1280]{1,0:T(8,128)(2,1)S(1)}, bf16[256,1280]{1,0:T(8,128)(2,1)S(1)}, u32[]{:S(2)}, u32[]{:S(2)}) %collective-permute-start.4) | collective-permute-done | bytes 655392 | tf_op jit(solution)/shard_map/ppermute | solution.py:24
  72.4 2.2 %shard_map.87 = (bf16[256,512]{1,0:T(8,128)(2,1)S(1)}, f32[64,128]{1,0:T(8,128)}) custom-call(f32[3]{0:T(128)S(1)} %pad_maximum_fusion.2.refs_0_, bf16[256,1280]{1,0:T(8,128)(2,1)S(1)} %collective-permute-done.4.refs_1_, bf16[512,1152]{1,0:T(8,128)(2,1)S(1)} %fusion.1.refs_2_, f32[1,512]{1,0:T(1,128)S(1)} %bitcast.25, f32[64,128]{1,0:T(8,128)S(1)} %get-tuple-element.28.refs_4_), custom_call_target="tpu_custom_call" | custom-call | flops 301989888 | bytes 1769472 | tf_op jit(solution)/shard_map/pallas_call | solution.py:62
  74.6 1.3 convolution_convert_fusion
  76.0 1.9 %collective-permute-start.5 = (f16[256,1152]{1,0:T(8,128)(2,1)}, f16[256,1152]{1,0:T(8,128)(2,1)}, u32[]{:S(2)}, u32[]{:S(2)}) collective-permute-start(f16[256,1152]{1,0:T(8,128)(2,1)} %convolution_convert_fusion), channel_id=1, source_target_pairs={{0,16},{1,1009},{2,18},{3,1011},{4,20},{5,1013},{6,22},{7,1015},{8... | collective-permute-start | bytes 1769480 | tf_op jit(solution)/shard_map/ppermute | solution.py:24
  77.9 10.0 %all-to-all-start = ((f32[64,1,128]{2,1,0:T(1,128)}), f32[64,1,128]{2,1,0:T(1,128)}, u32[]{:S(2)}, u32[]{:S(2)}) async-start(f32[64,1,128]{2,1,0:T(1,128)} %bitcast.7), calls=%async_computation | async-start | bytes 65536 | tf_op jit(solution)/shard_map/all_to_all | solution.py:152
  90.2 6.2 %collective-permute-start.6 = (f16[128,1152]{1,0:T(8,128)(2,1)S(1)}, f16[128,1152]{1,0:T(8,128)(2,1)S(1)}, u32[]{:S(2)}, u32[]{:S(2)}) collective-permute-start(f16[128,1152]{1,0:T(8,128)(2,1)S(1)} %add_convert_fusion.1), channel_id=1, source_target_pairs={{0,32},{1,993},{2,34},{3,995},{4,36},{5,997},{6,38},{7,999},{8,40}... | collective-permute-start | bytes 884744 | tf_op jit(solution)/shard_map/ppermute | solution.py:24
  96.4 1.4 add_convert_fusion
  97.8 6.3 %collective-permute-done.6 = f16[128,1152]{1,0:T(8,128)(2,1)S(1)} collective-permute-done((f16[128,1152]{1,0:T(8,128)(2,1)S(1)}, f16[128,1152]{1,0:T(8,128)(2,1)S(1)}, u32[]{:S(2)}, u32[]{:S(2)}) %collective-permute-start.6) | collective-permute-done | bytes 294944 | tf_op jit(solution)/shard_map/ppermute | solution.py:24
  105.2 6.7 %collective-permute-start.7 = (f16[64,1152]{1,0:T(8,128)(2,1)S(1)}, f16[64,1152]{1,0:T(8,128)(2,1)S(1)}, u32[]{:S(2)}, u32[]{:S(2)}) collective-permute-start(f16[64,1152]{1,0:T(8,128)(2,1)S(1)} %add_convert_fusion.2), channel_id=1, source_target_pairs={{0,64},{1,961},{2,66},{3,963},{4,68},{5,965},{6,70},{7,967},{8,72}... | collective-permute-start | bytes 442376 | tf_op jit(solution)/shard_map/ppermute | solution.py:24
  113.4 11.3 %all-to-all-start.1 = ((f16[16,32,1280]{2,1,0:T(8,128)(2,1)}), f16[16,32,1280]{2,1,0:T(8,128)(2,1)S(1)}, u32[]{:S(2)}, u32[]{:S(2)}) async-start(f16[16,32,1280]{2,1,0:T(8,128)(2,1)} %bitcast.26), calls=%async_computation.1 | async-start | bytes 2621440 | tf_op jit(solution)/shard_map/all_to_all | solution.py:180
  124.8 1.1 convert_add_fusion
  126.0 2.1 %collective-permute-start.8 = (f16[32,1152]{1,0:T(8,128)(2,1)S(1)}, f16[32,1152]{1,0:T(8,128)(2,1)S(1)}, u32[]{:S(2)}, u32[]{:S(2)}) collective-permute-start(f16[32,1152]{1,0:T(8,128)(2,1)S(1)} %get-tuple-element.37), channel_id=1, source_target_pairs={{0,17},{1,0},{2,19},{3,2},{4,21},{5,4},{6,23},{7,6},{8,25},{9,8},{... | collective-permute-start | bytes 221192 | tf_op jit(solution)/shard_map/ppermute | solution.py:24
  128.8 5.7 %collective-permute-done.8 = f16[32,1152]{1,0:T(8,128)(2,1)S(1)} collective-permute-done((f16[32,1152]{1,0:T(8,128)(2,1)S(1)}, f16[32,1152]{1,0:T(8,128)(2,1)S(1)}, u32[]{:S(2)}, u32[]{:S(2)}) %collective-permute-start.8) | collective-permute-done | bytes 73760 | tf_op jit(solution)/shard_map/ppermute | solution.py:24
  135.4 9.4 %all-to-all-done.1 = f16[16,32,1280]{2,1,0:T(8,128)(2,1)S(1)} async-done(((f16[16,32,1280]{2,1,0:T(8,128)(2,1)}), f16[16,32,1280]{2,1,0:T(8,128)(2,1)S(1)}, u32[]{:S(2)}, u32[]{:S(2)}) %all-to-all-start.1) | async-done | bytes 1310752 | tf_op jit(solution)/shard_map/all_to_all | solution.py:180
  (59 shorter events, 11.1 us)
Async XLA Ops:
  0.6 27.2 %copy-start = (bf16[512,1152]{1,0:T(8,128)(2,1)S(1)}, bf16[512,1152]{1,0:T(8,128)(2,1)}, u32[]{:S(2)}) copy-start(bf16[512,1152]{1,0:T(8,128)(2,1)} %param.6) | copy-start | bytes 3538948
  0.6 27.2 %copy-start.8 = (s32[512]{0:T(512)S(1)}, s32[512]{0:T(512)}, u32[]{:S(2)}) copy-start(s32[512]{0:T(512)} %param.8) | copy-start | bytes 6148
  2.4 26.9 %copy-start.5 = (bf16[32,1280]{1,0:T(8,128)(2,1)S(1)}, bf16[32,1280]{1,0:T(8,128)(2,1)}, u32[]{:S(2)}) copy-start(bf16[32,1280]{1,0:T(8,128)(2,1)} %shard_map.85) | copy-start | bytes 245764
  2.4 26.9 %collective-permute-start = (bf16[32,1280]{1,0:T(8,128)(2,1)}, bf16[32,1280]{1,0:T(8,128)(2,1)S(1)}, u32[]{:S(2)}, u32[]{:S(2)}) collective-permute-start(bf16[32,1280]{1,0:T(8,128)(2,1)} %shard_map.85), channel_id=1, source_target_pairs={{0,1008},{2,1010},{4,1012},{6,1014},{8,1016},{10,1018},{12,1020},{... | collective-permute-start | bytes 245768 | tf_op jit(solution)/shard_map/ppermute | solution.py:24
  3.2 26.1 %collective-permute-start.1 = (bf16[32,1280]{1,0:T(8,128)(2,1)}, bf16[32,1280]{1,0:T(8,128)(2,1)S(1)}, u32[]{:S(2)}, u32[]{:S(2)}) collective-permute-start(bf16[32,1280]{1,0:T(8,128)(2,1)} %shard_map.85), channel_id=1, source_target_pairs={{0,1},{1,1008},{2,3},{3,1010},{4,5},{5,1012},{6,7},{7,1014},{8,9},... | collective-permute-start | bytes 245768 | tf_op jit(solution)/shard_map/ppermute | solution.py:24
  29.4 15.2 %collective-permute-start.2 = (bf16[64,1280]{1,0:T(8,128)(2,1)S(1)}, bf16[64,1280]{1,0:T(8,128)(2,1)S(1)}, u32[]{:S(2)}, u32[]{:S(2)}) collective-permute-start(bf16[64,1280]{1,0:T(8,128)(2,1)S(1)} %pad_maximum_fusion.1), channel_id=1, source_target_pairs={{0,960},{1,65},{2,962},{3,67},{4,964},{5,69},{6,966},{7,71},{8,968... | collective-permute-start | bytes 491528 | tf_op jit(solution)/shard_map/ppermute | solution.py:24
  31.3 15.3 %copy-start.4 = (bf16[32,1152]{1,0:T(8,128)(2,1)S(1)}, bf16[32,1152]{1,0:T(8,128)(2,1)}, u32[]{:S(2)}) copy-start(bf16[32,1152]{1,0:T(8,128)(2,1)} %refs_0_.1) | copy-start | bytes 221188
  44.6 14.3 %collective-permute-start.3 = (bf16[128,1280]{1,0:T(8,128)(2,1)S(1)}, bf16[128,1280]{1,0:T(8,128)(2,1)S(1)}, u32[]{:S(2)}, u32[]{:S(2)}) collective-permute-start(bf16[128,1280]{1,0:T(8,128)(2,1)S(1)} %pad_maximum_fusion), channel_id=1, source_target_pairs={{0,992},{1,33},{2,994},{3,35},{4,996},{5,37},{6,998},{7,39},{8,100... | collective-permute-start | bytes 983048 | tf_op jit(solution)/shard_map/ppermute | solution.py:24
  59.0 13.4 %collective-permute-start.4 = (bf16[256,1280]{1,0:T(8,128)(2,1)S(1)}, bf16[256,1280]{1,0:T(8,128)(2,1)S(1)}, u32[]{:S(2)}, u32[]{:S(2)}) collective-permute-start(bf16[256,1280]{1,0:T(8,128)(2,1)S(1)} %constant_dynamic-update-slice_fusion.refs_1_), channel_id=1, source_target_pairs={{0,1008},{1,17},{2,1010},{3,19},{4,1012},{5,21},{6,1014},{7,23},{8... | collective-permute-start | bytes 1966088 | tf_op jit(solution)/shard_map/ppermute | solution.py:24
  76.0 12.5 %collective-permute-start.5 = (f16[256,1152]{1,0:T(8,128)(2,1)}, f16[256,1152]{1,0:T(8,128)(2,1)}, u32[]{:S(2)}, u32[]{:S(2)}) collective-permute-start(f16[256,1152]{1,0:T(8,128)(2,1)} %convolution_convert_fusion), channel_id=1, source_target_pairs={{0,16},{1,1009},{2,18},{3,1011},{4,20},{5,1013},{6,22},{7,1015},{8... | collective-permute-start | bytes 1769480 | tf_op jit(solution)/shard_map/ppermute | solution.py:24
  77.9 34.1 %all-to-all-start = ((f32[64,1,128]{2,1,0:T(1,128)}), f32[64,1,128]{2,1,0:T(1,128)}, u32[]{:S(2)}, u32[]{:S(2)}) async-start(f32[64,1,128]{2,1,0:T(1,128)} %bitcast.7), calls=%async_computation | async-start | bytes 65536 | tf_op jit(solution)/shard_map/all_to_all | solution.py:152
  87.9 1.3 copy-start.1
  90.2 13.9 %collective-permute-start.6 = (f16[128,1152]{1,0:T(8,128)(2,1)S(1)}, f16[128,1152]{1,0:T(8,128)(2,1)S(1)}, u32[]{:S(2)}, u32[]{:S(2)}) collective-permute-start(f16[128,1152]{1,0:T(8,128)(2,1)S(1)} %add_convert_fusion.1), channel_id=1, source_target_pairs={{0,32},{1,993},{2,34},{3,995},{4,36},{5,997},{6,38},{7,999},{8,40}... | collective-permute-start | bytes 884744 | tf_op jit(solution)/shard_map/ppermute | solution.py:24
  104.1 1.1 copy-start.6
  105.2 19.6 %collective-permute-start.7 = (f16[64,1152]{1,0:T(8,128)(2,1)S(1)}, f16[64,1152]{1,0:T(8,128)(2,1)S(1)}, u32[]{:S(2)}, u32[]{:S(2)}) collective-permute-start(f16[64,1152]{1,0:T(8,128)(2,1)S(1)} %add_convert_fusion.2), channel_id=1, source_target_pairs={{0,64},{1,961},{2,66},{3,963},{4,68},{5,965},{6,70},{7,967},{8,72}... | collective-permute-start | bytes 442376 | tf_op jit(solution)/shard_map/ppermute | solution.py:24
  113.4 11.4 %copy-start.7 = (f16[128,1152]{1,0:T(8,128)(2,1)S(1)}, f16[128,1152]{1,0:T(8,128)(2,1)}, u32[]{:S(2)}) copy-start(f16[128,1152]{1,0:T(8,128)(2,1)} %copy-done.6) | copy-start | bytes 884740
  113.4 31.4 %all-to-all-start.1 = ((f16[16,32,1280]{2,1,0:T(8,128)(2,1)}), f16[16,32,1280]{2,1,0:T(8,128)(2,1)S(1)}, u32[]{:S(2)}, u32[]{:S(2)}) async-start(f16[16,32,1280]{2,1,0:T(8,128)(2,1)} %bitcast.26), calls=%async_computation.1 | async-start | bytes 2621440 | tf_op jit(solution)/shard_map/all_to_all | solution.py:180
  124.8 9.7 %copy-start.3 = (f32[32,1152]{1,0:T(8,128)S(1)}, f32[32,1152]{1,0:T(8,128)}, u32[]{:S(2)}) copy-start(f32[32,1152]{1,0:T(8,128)} %get-tuple-element.35) | copy-start | bytes 442372
  125.9 19.0 %copy-start.2 = (f32[32,1152]{1,0:T(8,128)S(1)}, f32[32,1152]{1,0:T(8,128)}, u32[]{:S(2)}) copy-start(f32[32,1152]{1,0:T(8,128)} %get-tuple-element.33) | copy-start | bytes 442372
  126.0 8.6 %collective-permute-start.8 = (f16[32,1152]{1,0:T(8,128)(2,1)S(1)}, f16[32,1152]{1,0:T(8,128)(2,1)S(1)}, u32[]{:S(2)}, u32[]{:S(2)}) collective-permute-start(f16[32,1152]{1,0:T(8,128)(2,1)S(1)} %get-tuple-element.37), channel_id=1, source_target_pairs={{0,17},{1,0},{2,19},{3,2},{4,21},{5,4},{6,23},{7,6},{8,25},{9,8},{... | collective-permute-start | bytes 221192 | tf_op jit(solution)/shard_map/ppermute | solution.py:24
  128.1 6.4 %collective-permute-start.9 = (f16[32,1152]{1,0:T(8,128)(2,1)S(1)}, f16[32,1152]{1,0:T(8,128)(2,1)S(1)}, u32[]{:S(2)}, u32[]{:S(2)}) collective-permute-start(f16[32,1152]{1,0:T(8,128)(2,1)S(1)} %get-tuple-element.38), channel_id=1, source_target_pairs={{0,16},{2,18},{4,20},{6,22},{8,24},{10,26},{12,28},{14,30},{16,32}... | collective-permute-start | bytes 221192 | tf_op jit(solution)/shard_map/ppermute | solution.py:24
